TPU v7x, 128 devices: a whole 4x4x4 slice. The times are simulated.
128 devices in a mesh: grp: 16 (over x, z_hi, core), tp: 8 (over z_lo, y).
Axes of the slice: x: 4, y: 4, z: 4 (z_hi: 2, z_lo: 2; z = z_hi * 2 + z_lo), core: 2. Of those that a mesh axis runs over, the one named last changes fastest.
Arguments:
- residual: bfloat16 [4096, 5120], P('grp', 'tp'), may hold values from -5 to 5
- queries: bfloat16 [128, 32, 8192], P('grp', None, 'tp'), may hold values from -125 to 125
- cache_kv: bfloat16 [128, 2, 2048, 1024], P('grp', None, None, 'tp'), may hold values from -5 to 5
- fresh_kv: bfloat16 [128, 2, 32, 1024], P('grp', None, None, 'tp'), may hold values from -5 to 5
- lengths: int32 [128], replicated, may hold values from 1 to 2048, 87381 in all
- destination_place: int32 [128], replicated, may hold values from 0 to 127, each once
- out_weight: bfloat16 [8192, 5120], P('tp'), may hold values from -0.59765625 to 0.59765625
- norm_gain: bfloat16 [5120], replicated, may hold values from 0.5 to 1.5
- gate_up: bfloat16 [5120, 2, 13312], P('grp', None, 'tp'), may hold values from -0.078125 to 0.078125
- block_of: int32 [16], replicated, may hold values from 0 to 15, each once
Outputs:
- evened_activations: bfloat16 [4096, 5120], P('grp', 'tp')
- gated_activations: bfloat16 [4096, 13312], P('grp', 'tp')
Inputs may be any that keep to these rules, and one draw needn't show every extreme that they name: `lengths`: the longest sequence uses exactly 2048 stored positions. `destination_place`: every target slot is named by exactly one sequence. `block_of`: every block is held by exactly one index of grp.
All inputs are finite; a program needn't handle non-finite values.
Results may differ from a plain program's by a relative error of at most 0.0081.
Values may be sent and summed in bfloat16 or wider, within the bound.
No kernel may reach another device: no remote copies, remote signals or barrier semaphores. Data moves between devices by JAX's collectives and lax.ppermute only.
A program may use at most 256 MiB of HBM per device.

v0:
```python
import jax
import jax.numpy as jnp
from jax import lax
from jax.sharding import PartitionSpec as P

HQ = 64
KVH = 8
HD = 128


masked_score = -1e30
epsilon = 1e-06


def attend_sequence(queries, stored, fresh_rows, seq_length, heads_kv, share, head_size, key_block):
    count_rows = queries.shape[0]
    factor = head_size ** (-0.5)
    grouped = queries.reshape(count_rows, heads_kv, share, head_size)
    fresh_keys = fresh_rows[0].reshape(count_rows, heads_kv, head_size)
    fresh_values = fresh_rows[1].reshape(count_rows, heads_kv, head_size)
    fresh_scores = (
        jnp.einsum("rkgd,nkd->kgrn", grouped, fresh_keys, preferred_element_type=jnp.float32)
        * factor
    )
    causal = lax.broadcasted_iota(jnp.int32, (count_rows, count_rows), 1) <= lax.broadcasted_iota(
        jnp.int32, (count_rows, count_rows), 0
    )
    fresh_scores = jnp.where(causal, fresh_scores, masked_score)
    highest = jnp.max(fresh_scores, axis=-1)
    denominator = jnp.sum(jnp.exp(fresh_scores - highest[..., None]), axis=-1)
    block_count = (seq_length + key_block - 1) // key_block
    offsets = lax.iota(jnp.int32, key_block)

    def block_scores(index):
        first_pos = index * key_block
        key_rows = lax.dynamic_slice_in_dim(stored[0], first_pos, key_block, 0).reshape(
            key_block, heads_kv, head_size
        )
        scores = (
            jnp.einsum("rkgd,nkd->kgrn", grouped, key_rows, preferred_element_type=jnp.float32)
            * factor
        )
        in_use = first_pos + offsets < seq_length
        return (jnp.where(in_use, scores, masked_score), first_pos)

    def gather_stats(index, carried):
        old_high, old_sum = carried
        scores, first_pos = block_scores(index)
        new_high = jnp.maximum(old_high, jnp.max(scores, axis=-1))
        new_sum = old_sum * jnp.exp(old_high - new_high) + jnp.sum(
            jnp.exp(scores - new_high[..., None]), axis=-1
        )
        return (new_high, new_sum)

    highest, denominator = lax.fori_loop(0, block_count, gather_stats, (highest, denominator))
    fresh_probs = (jnp.exp(fresh_scores - highest[..., None]) / denominator[..., None]).astype(
        jnp.bfloat16
    )
    context = jnp.einsum(
        "kgrn,nkd->rkgd", fresh_probs, fresh_values, preferred_element_type=jnp.float32
    )

    def add_block(index, context):
        scores, first_pos = block_scores(index)
        probability = (jnp.exp(scores - highest[..., None]) / denominator[..., None]).astype(
            jnp.bfloat16
        )
        values = lax.dynamic_slice_in_dim(stored[1], first_pos, key_block, 0).reshape(
            key_block, heads_kv, head_size
        )
        return context + jnp.einsum(
            "kgrn,nkd->rkgd", probability, values, preferred_element_type=jnp.float32
        )

    context = lax.fori_loop(0, block_count, add_block, context)
    return context.reshape(count_rows, heads_kv * share * head_size).astype(jnp.bfloat16)


def per_device(
    residual,
    queries,
    cache_kv,
    fresh_kv,
    lengths,
    destination_place,
    out_weight,
    norm_gain,
    gate_up,
    block_of,
):
    seq_local = queries.shape[0]
    seq_rows = queries.shape[1]
    heads_kv = cache_kv.shape[3] // HD
    share = HQ // KVH
    key_block = min(cache_kv.shape[2], 512)
    group_index = lax.axis_index("grp")
    own_lengths = lax.dynamic_slice_in_dim(lengths, group_index * seq_local, seq_local, 0)

    def attend_one(packed):
        return attend_sequence(
            packed[0], packed[1], packed[2], packed[3], heads_kv, share, HD, key_block
        )

    context = lax.map(attend_one, (queries, cache_kv, fresh_kv, own_lengths))
    token_rows = seq_local * seq_rows
    context = context.reshape(token_rows, context.shape[2])
    head_terms = jnp.dot(context, out_weight, preferred_element_type=jnp.float32)
    attended = lax.psum_scatter(head_terms, "tp", scatter_dimension=1, tiled=True)
    combined_partials = (residual.astype(jnp.float32) + attended).astype(jnp.bfloat16)
    total_seqs = lengths.shape[0]
    own_slots = group_index * seq_local + lax.iota(jnp.int32, seq_local)
    matches = destination_place[None, :] == own_slots[:, None]
    source_seq = jnp.sum(jnp.where(matches, lax.iota(jnp.int32, total_seqs)[None, :], 0), axis=1)
    source_row = (source_seq[:, None] * seq_rows + lax.iota(jnp.int32, seq_rows)[None, :]).reshape(
        token_rows
    )
    piece = lax.all_gather(combined_partials, "grp", axis=0, tiled=True)
    selector = (source_row[:, None] == lax.iota(jnp.int32, piece.shape[0])[None, :]).astype(
        jnp.bfloat16
    )
    arrived_entries = jnp.dot(selector, piece, preferred_element_type=jnp.float32)
    evened_activations = arrived_entries.astype(jnp.bfloat16)
    model_width = norm_gain.shape[0]
    widened_entries = evened_activations.astype(jnp.float32)
    squares = lax.psum(jnp.sum(widened_entries * widened_entries, axis=1), "tp")
    inverse = lax.rsqrt(squares / model_width + epsilon)
    own_gain = lax.dynamic_slice_in_dim(
        norm_gain, lax.axis_index("tp") * widened_entries.shape[1], widened_entries.shape[1], 0
    ).astype(jnp.float32)
    local_normed = (widened_entries * inverse[:, None] * own_gain[None, :]).astype(jnp.bfloat16)
    normed = lax.all_gather(local_normed, "tp", axis=1, tiled=True)
    block_total = block_of.shape[0]
    block_rows = model_width // block_total
    ordered = jnp.take(normed.reshape(token_rows, block_total, block_rows), block_of, axis=1)
    flattened = ordered.reshape(token_rows, model_width)
    projected = jnp.einsum(
        "td,dgf->tgf",
        flattened,
        lax.all_gather(gate_up, "grp", axis=0, tiled=True),
        preferred_element_type=jnp.float32,
    )
    gated_activations = (jax.nn.silu(projected[:, 0, :]) * projected[:, 1, :]).astype(jnp.bfloat16)
    return (evened_activations, gated_activations)


def solution(mesh):
    return jax.shard_map(
        per_device,
        mesh=mesh,
        in_specs=(
            P("grp", "tp"),
            P("grp", None, "tp"),
            P("grp", None, None, "tp"),
            P("grp", None, None, "tp"),
            P(),
            P(),
            P("tp", None),
            P(),
            P("grp", None, "tp"),
            P(),
        ),
        out_specs=(P("grp", "tp"), P("grp", "tp")),
        check_vma=False,
    )
```

profile of v0, /device:TPU:1, one launch (start us, length us, event | category | flops | bytes accessed | tf_op | source)
XLA Modules:
  0.0 517.0 jit_solution(4050709815220521642)
XLA Ops:
  8.0 84.9 %while.90 = (s32[]{:T(128)}, bf16[8,32,1024]{2,1,0:T(8,128)(2,1)S(1)}, bf16[8,2,32,128]{3,2,1,0:T(8,128)(2,1)}, bf16[8,32,1024]{2,1,0:T(8,128)(2,1)}, s32[8]{0:T...) while((s32[]{:T(128)}, ...), condition=%wide.region_10.11_spmd, body=%wide.region_1.10_spmd.sunk | while | flops 106302496 | bytes 8404905 | solution.py:104
  9.1 0.9 dynamic-slice_bitcast_fusion.10
  10.0 0.9 fusion.75
  11.0 1.3 dynamic-slice_bitcast_fusion.11
  12.3 1.2 while.91
  13.5 0.9 convolution_bitcast_fusion.3
  14.5 1.1 while.92
  16.9 0.9 dynamic-slice_bitcast_fusion.10
  17.8 0.9 fusion.75
  18.7 1.3 dynamic-slice_bitcast_fusion.11
  20.0 2.4 while.91
  22.5 0.9 convolution_bitcast_fusion.3
  23.4 2.2 while.92
  26.9 0.9 dynamic-slice_bitcast_fusion.10
  27.8 0.9 fusion.75
  28.8 1.3 dynamic-slice_bitcast_fusion.11
  30.1 4.9 while.91
  35.0 0.9 convolution_bitcast_fusion.3
  35.9 4.4 while.92
  41.6 0.9 dynamic-slice_bitcast_fusion.10
  42.4 0.9 fusion.75
  43.4 1.3 dynamic-slice_bitcast_fusion.11
  44.7 1.2 while.91
  46.0 0.9 convolution_bitcast_fusion.3
  46.9 1.1 while.92
  49.3 0.9 dynamic-slice_bitcast_fusion.10
  50.2 0.9 fusion.75
  51.2 1.3 dynamic-slice_bitcast_fusion.11
  52.5 1.2 while.91
  53.7 0.9 convolution_bitcast_fusion.3
  54.6 1.1 while.92
  57.0 0.9 dynamic-slice_bitcast_fusion.10
  57.9 0.9 fusion.75
  58.9 1.3 dynamic-slice_bitcast_fusion.11
  60.2 1.2 while.91
  61.4 0.9 convolution_bitcast_fusion.3
  62.4 1.1 while.92
  64.8 0.9 dynamic-slice_bitcast_fusion.10
  65.7 0.9 fusion.75
  66.6 1.3 dynamic-slice_bitcast_fusion.11
  67.9 4.9 while.91
  72.8 0.9 convolution_bitcast_fusion.3
  73.7 4.4 while.92
  79.4 0.9 dynamic-slice_bitcast_fusion.10
  80.3 0.9 fusion.75
  81.3 1.3 dynamic-slice_bitcast_fusion.11
  82.6 4.9 while.91
  87.5 0.9 convolution_bitcast_fusion.3
  88.4 4.4 while.92
  92.9 8.6 %fusion.59 = f32[256,5120]{1,0:T(8,128)} fusion(bf16[256,1024]{1,0:T(8,128)(2,1)S(1)} %bitcast.213, bf16[1024,5120]{1,0:T(8,128)(2,1)} %param.22), kind=kOutput, calls=%fused_computation.88 | convolution fusion | flops 2684354560 | bytes 16252928 | tf_op jit(solution)/shard_map/dot_general | solution.py:107
  101.6 73.6 %reduce-scatter.2.cloned.1.call-done = f32[256,640]{1,0:T(8,128)} async-done(((f32[256,5120]{1,0:T(8,128)}), f32[256,640]{1,0:T(8,128)}) %reduce-scatter.2.cloned.1.call-update) | async-done | bytes 655376 | tf_op jit(solution)/shard_map/reduce_scatter | solution.py:108
  175.2 1.9 add_convert_fusion
  178.2 58.9 %all-gather.4.cloned.1.call-done = bf16[4096,640]{1,0:T(8,128)(2,1)} async-done(((bf16[256,640]{1,0:T(8,128)(2,1)}), bf16[4096,640]{1,0:T(8,128)(2,1)}) %all-gather.4.cloned.1.call-update) | async-done | bytes 5242896 | tf_op jit(solution)/shard_map/all_gather | solution.py:117
  237.2 4.5 fusion.53
  241.7 15.0 %psum.7 = f32[256]{0:T(256)S(1)} all-reduce(f32[256]{0:T(256)S(1)} %get-tuple-element.352), channel_id=1, replica_groups=mesh['grp'=16,'tp'=8] {'tp'}, use_global_device_ids=true, to_apply=%region_13.14 | all-reduce | flops 256 | bytes 2048 | tf_op jit(solution)/shard_map/psum | solution.py:125
  256.7 0.9 fusion.55
  257.7 1.6 copy.29
  259.6 38.0 %all-gather.6.cloned.1.call-done = bf16[256,5120]{1,0:T(8,128)(2,1)} async-done(((bf16[256,640]{1,0:T(8,128)(2,1)}), bf16[256,5120]{1,0:T(8,128)(2,1)}) %all-gather.6.cloned.1.call-update) | async-done | bytes 2621456 | tf_op jit(solution)/shard_map/all_gather | solution.py:131
  297.5 3.0 copy.28
  300.5 2.2 gather_fusion
  302.7 4.1 bitcast_select_fusion
  306.7 186.5 %all-gather.8.cloned.1.call-done = bf16[5120,2,1664]{2,0,1:T(8,128)(2,1)} async-done(((bf16[320,2,1664]{2,0,1:T(8,128)(2,1)}), bf16[5120,2,1664]{2,0,1:T(8,128)(2,1)}) %all-gather.8.cloned.1.call-update) | async-done | bytes 34078736 | tf_op jit(solution)/shard_map/all_gather | solution.py:139
  493.2 15.8 %fusion.47 = f32[256,2,1664]{2,0,1:T(8,128)S(1)} fusion(bf16[5120,2,1664]{2,0,1:T(8,128)(2,1)} %all-gather.8.cloned.1.call-done, bf16[256,5120]{0,1:T(8,128)(2,1)S(1)} %bitcast_select_fusion), kind=kOutput, calls=%fused_computation.62 | convolution fusion | flops 8724152320 | bytes 40108032 | tf_op jit(solution)/shard_map/td,dgf->tgf/dot_general | solution.py:136
  509.0 1.4 fusion.51
  (284 shorter events, 47.8 us)
Async XLA Ops:
  7.2 168.0 %reduce-scatter.2.cloned.1.call-start = ((), (), s32[]{:S(2)}) async-start(), calls=%async_computation.1 | async-start | bytes 5898240 | tf_op jit(solution)/shard_map/reduce_scatter | solution.py:108
  101.5 73.7 %copy-start.1 = (bf16[256,640]{1,0:T(8,128)(2,1)S(1)}, bf16[256,640]{1,0:T(8,128)(2,1)}, u32[]{:S(2)}) copy-start(bf16[256,640]{1,0:T(8,128)(2,1)} %param.16) | copy-start | bytes 983044
  101.5 75.6 %copy-start.3 = (s32[128]{0:T(128)S(1)}, s32[128]{0:T(128)}, u32[]{:S(2)}) copy-start(s32[128]{0:T(128)} %param.21) | copy-start | bytes 1540
  101.5 135.7 %all-gather.4.cloned.1.call-start = ((), (), s32[]{:S(2)}) async-start(), calls=%async_computation.2 | async-start | bytes 5570560 | tf_op jit(solution)/shard_map/all_gather | solution.py:117
  177.1 120.5 %all-gather.6.cloned.1.call-start = ((), (), s32[]{:S(2)}) async-start(), calls=%async_computation.3 | async-start | bytes 2949120 | tf_op jit(solution)/shard_map/all_gather | solution.py:131
  178.2 79.5 %copy-start = (bf16[320,2,1664]{2,1,0:T(2,128)(2,1)S(1)}, bf16[320,2,1664]{2,1,0:T(2,128)(2,1)}, u32[]{:S(2)}) copy-start(bf16[320,2,1664]{2,1,0:T(2,128)(2,1)} %param.24) | copy-start | bytes 6389764
  241.7 17.6 %copy-start.2 = (bf16[256,640]{1,0:T(8,128)(2,1)}, bf16[256,640]{1,0:T(8,128)(2,1)S(1)}, u32[]{:S(2)}) copy-start(bf16[256,640]{1,0:T(8,128)(2,1)S(1)} %get-tuple-element.353) | copy-start | bytes 983044
  257.6 1.7 copy-start.4
  257.7 235.5 %all-gather.8.cloned.1.call-start = ((), (), s32[]{:S(2)}) async-start(), calls=%async_computation.4 | async-start | bytes 36208640 | tf_op jit(solution)/shard_map/all_gather | solution.py:139
Sparse Core Ops, SparseCore 0:
  101.6 73.4 reduce-scatter.1
  178.1 58.9 all-gather.3
  257.8 39.7 all-gather.5
  299.8 193.3 all-gather.7
where the time goes:
time: 519 us; the launch traced here: 517 us
  waiting for transfers between devices  357 us (69%)
  matrix products  56.8 us (11%)
  other arithmetic  34.4 us (7%)
  local copies, waits for them, and re-layouts  32.3 us (6%)
  blocking collectives  15 us (3%)
  between operations  13.9 us (3%)
  loops' own time  7.46 us (1%)
    all_gather x1, waiting for transfers between devices, per_device(): lax.all_gather(gate_up, 'grp', axis=0, tiled=True)  186 us
    reduce_scatter x1, waiting for transfers between devices, per_device(): lax.psum_scatter(head_terms, 'tp', scatter_dimension=1, tiled=True)  73.6 us
    all_gather x1, waiting for transfers between devices, per_device(): piece = lax.all_gather(combined_partials, 'grp', axis=0, tiled=True)  58.9 us
    all_gather x1, waiting for transfers between devices, per_device(): normed = lax.all_gather(local_normed, 'tp', axis=1, tiled=True)  38 us
    lt x36, other arithmetic, block_scores(): in_use = first_pos + offsets < seq_length  20.3 us
    dot_general x1, matrix products, per_device(): jnp.einsum('td,dgf->tgf', flattened, lax.all_gather(gate_up, 'grp', axis=...  15.8 us
    psum x1, blocking collectives, per_device(): squares = lax.psum(jnp.sum(widened_entries * widened_entries, axis=1), 'tp')  15 us
    squeeze x8, local copies, waits for them, and re-layouts, per_device(): context = lax.map(attend_one, (queries, cache_kv, fresh_kv, own_lengths))  10.4 us
  transfers between devices with their start and end apart: 4, of which 4 were waited for; matrix products, arithmetic and copies ran while one was open for 2% of the time, Pallas kernels for 0%

commit v1 on v0

v1 whole, which is shorter than its diff:
```python
import functools

import jax
import jax.numpy as jnp
from jax import lax
from jax.experimental import pallas as pl
from jax.experimental.pallas import tpu as pltpu
from jax.sharding import Mesh, PartitionSpec as P

AX = ("x", "zh", "c", "zl", "y")
SIZES = dict(x=4, zh=2, c=2, zl=2, y=4)
BF = jnp.bfloat16
F32 = jnp.float32
HD = 128
HEADS = 8
SEQS = 8
ROWS = 32
LMAX = 2048
KB = 512
NB = LMAX // KB
D = 5120
DT = 640
BLK = 320
FT = 1664
NEG = -1e30
EPS = 1e-6
VM = pl.BlockSpec(memory_space=pltpu.VMEM)
SM = pl.BlockSpec(memory_space=pltpu.SMEM)
ANY = pl.BlockSpec(memory_space=pl.ANY)


def permute(value, axes, move):
    sizes = [SIZES[a] for a in axes]
    total = 1
    for n in sizes:
        total *= n
    pairs = []
    for i in range(total):
        coords, rest = [], i
        for n in reversed(sizes):
            coords.append(rest % n)
            rest //= n
        target = move(*reversed(coords))
        j = 0
        for n, q in zip(sizes, target):
            j = j * n + q
        pairs.append((i, j))
    return lax.ppermute(value, axes, pairs)


def along_x(value, k):
    return permute(value, ("x",), lambda x: ((x + k) % 4,))


def along_y(value, k):
    return permute(value, ("y",), lambda y: ((y + k) % 4,))


def along_z(value, k):
    def move(zh, zl):
        z = (zh * 2 + zl + k) % 4
        return (z // 2, z % 2)

    return permute(value, ("zh", "zl"), move)


def swap(value, axis):
    return permute(value, (axis,), lambda q: (1 - q,))


def shuffle(row, inner):
    return (row // 4 % 8) * 32 + (row // 32) * 4 + row % 4


def one_hot(n):
    out = lax.broadcasted_iota(jnp.int32, (n, n), 0)
    src = lax.broadcasted_iota(jnp.int32, (n, n), 1)
    return (shuffle(out, None) == src).astype(BF)


def front_kernel(len_ref, q_ref, fresh_ref, cache_ref, ow_ref, out_ref, kv, ow, ctx, kv_sem, ow_sem):
    def kv_copy(s, b):
        part = pl.ds(b * KB, KB)
        return pltpu.make_async_copy(
            cache_ref.at[s, :, part, :], kv.at[s, :, part, :], kv_sem.at[s, b]
        )

    for s in range(SEQS):
        for b in range(NB):

            @pl.when(b * KB < len_ref[s])
            def _(s=s, b=b):
                kv_copy(s, b).start()

    ow_copy = pltpu.make_async_copy(ow_ref, ow, ow_sem)
    ow_copy.start()
    factor = HD ** -0.5 * 1.4426950408889634
    nt = (((1,), (1,)), ((), ()))
    nn = (((1,), (0,)), ((), ()))

    def sequence(s, _):
        length = len_ref[s]
        rows = q_ref[s]
        q = jnp.concatenate([rows[:, h * HD : (h + 1) * HD] for h in range(HEADS)], axis=0)
        scores = lax.dot_general(q, fresh_ref[s, 0], nt, preferred_element_type=F32) * factor
        i = lax.broadcasted_iota(jnp.int32, scores.shape, 0) % ROWS
        j = lax.broadcasted_iota(jnp.int32, scores.shape, 1)
        scores = jnp.where(j <= i, scores, NEG)
        high = jnp.max(scores, axis=1, keepdims=True)
        p = jnp.exp2(scores - high)
        total = jnp.sum(p, axis=1, keepdims=True)
        acc = lax.dot_general(p.astype(BF), fresh_ref[s, 1], nn, preferred_element_type=F32)

        def block(b, carry):
            high, total, acc = carry
            kv_copy(s, b).wait()
            start = pl.multiple_of(b * KB, KB)
            k = kv[s, 0, pl.ds(start, KB), :]
            v = kv[s, 1, pl.ds(start, KB), :]
            scores = lax.dot_general(q, k, nt, preferred_element_type=F32) * factor
            pos = lax.broadcasted_iota(jnp.int32, scores.shape, 1)
            scores = jnp.where(pos < length - start, scores, NEG)
            new = jnp.maximum(high, jnp.max(scores, axis=1, keepdims=True))
            old = jnp.exp2(high - new)
            p = jnp.exp2(scores - new)
            total = total * old + jnp.sum(p, axis=1, keepdims=True)
            acc = acc * old + lax.dot_general(p.astype(BF), v, nn, preferred_element_type=F32)
            return new, total, acc

        high, total, acc = lax.fori_loop(0, (length + KB - 1) // KB, block, (high, total, acc))
        done = (acc / total).astype(BF)
        at = pl.ds(pl.multiple_of(s * ROWS, ROWS), ROWS)
        for h in range(HEADS):
            ctx[at, h * HD : (h + 1) * HD] = done[h * ROWS : (h + 1) * ROWS, :]
        return 0

    lax.fori_loop(0, SEQS, sequence, 0)
    mixed = jnp.dot(one_hot(256), ctx[...], preferred_element_type=F32).astype(BF)
    ow_copy.wait()
    for t in range(8):
        out_ref[t] = jnp.dot(
            mixed, ow[:, t * DT : (t + 1) * DT], preferred_element_type=F32
        ).astype(BF)


def front(lengths, queries, fresh, cache, out_weight):
    return pl.pallas_call(
        front_kernel,
        out_shape=jax.ShapeDtypeStruct((8, 256, DT), BF),
        in_specs=[SM, VM, VM, ANY, ANY],
        out_specs=VM,
        scratch_shapes=[
            pltpu.VMEM((SEQS, 2, LMAX, HD), BF),
            pltpu.VMEM((1024, D), BF),
            pltpu.VMEM((256, 1024), BF),
            pltpu.SemaphoreType.DMA((SEQS, NB)),
            pltpu.SemaphoreType.DMA,
        ],
        compiler_params=pltpu.CompilerParams(vmem_limit_bytes=48 * 2**20),
        name="attend_project",
    )(lengths, queries, fresh, cache, out_weight)


def feed_kernel(pos_ref, block_ref, src_ref, gain_ref, *refs):
    first, second, weights = refs[0:4], refs[4:8], refs[8:12]
    out_ref, act, normed, w, act_sem, w_sem = refs[12:]
    x, zh, c, zl, y = (pos_ref[i] for i in range(5))
    z = zh * 2 + zl
    copies = []
    for dz in range(2):
        for dc in range(2):
            for j, dx in enumerate((0, 3, 1, 2)):
                g = (x + dx) % 4 * 4 + (zh + dz) % 2 * 2 + (c + dc) % 2
                at = pl.multiple_of(block_ref[g] * BLK, BLK)
                copies.append(
                    pltpu.make_async_copy(
                        weights[dz * 2 + dc].at[pl.ds(j * BLK, BLK), :],
                        w.at[pl.ds(at, BLK), :],
                        w_sem.at[dz * 8 + dc * 4 + j],
                    )
                )
    pieces = []
    for half, group in enumerate((first, second)):
        for a, da in enumerate((0, 3, 1, 2)):
            for b, db in enumerate((0, 3, 1, 2)):
                dz, dy = (da, db) if half == 0 else (db, da)
                zz = (z + dz) % 4
                t = zz % 2 * 4 + (y + dy) % 4
                row = pl.multiple_of(zz // 2 * 256 + half * 128, 128)
                col = pl.multiple_of(t * DT, 128)
                pieces.append(
                    pltpu.make_async_copy(
                        group[a].at[b],
                        act.at[pl.ds(row, 128), pl.ds(col, DT)],
                        act_sem.at[half * 16 + a * 4 + b],
                    )
                )
    for copy in pieces + copies:
        copy.start()
    for copy in pieces:
        copy.wait()
    gain = gain_ref[...].astype(F32)
    for r in range(0, 512, 64):
        rows = act[r : r + 64, :].astype(F32)
        inverse = lax.rsqrt(jnp.sum(rows * rows, axis=1, keepdims=True) / D + EPS)
        normed[r : r + 64, :] = (rows * inverse * gain).astype(BF)
    for copy in copies:
        copy.wait()
    own = pl.multiple_of((zl * 4 + y) * DT, 128)
    flag = zh == 0
    for r in range(0, 512, 256):
        proj = jnp.dot(normed[r : r + 256, :], w[...], preferred_element_type=F32)
        g, u, m = proj[:, :768], proj[:, 768:1536], proj[:, 1536:]
        out_ref[r : r + 256, 0:768] = (g / (1 + jnp.exp(-g)) * u).astype(BF)
        tail = (m / (1 + jnp.exp(-m)) * pltpu.roll(m, 64, 1)).astype(BF).astype(F32)
        low = act[r : r + 256, pl.ds(own, 256)]
        mid = act[r : r + 256, pl.ds(pl.multiple_of(own + 256, 128), 128)].astype(F32)
        high = act[r : r + 256, pl.ds(pl.multiple_of(own + 384, 128), 256)]
        lane = lax.broadcasted_iota(jnp.int32, mid.shape, 1)
        mid = jnp.where(flag, pltpu.roll(mid, 64, 1), mid)
        out_ref[r : r + 256, 768:896] = jnp.where(lane < 64, tail, mid).astype(BF)
        out_ref[r : r + 256, 896:1152] = jnp.where(flag, low.astype(F32), high.astype(F32)).astype(BF)
    hot = (src_ref[...] == lax.broadcasted_iota(jnp.int32, (512, 512), 1)).astype(BF)
    out_ref[...] = jnp.dot(hot, out_ref[...], preferred_element_type=F32).astype(BF)


def feed(pos, block_of, src, gain, first, second, weights):
    return pl.pallas_call(
        feed_kernel,
        out_shape=jax.ShapeDtypeStruct((512, 1152), BF),
        in_specs=[SM, SM, VM, VM] + [ANY] * 12,
        out_specs=VM,
        scratch_shapes=[
            pltpu.VMEM((512, D), BF),
            pltpu.VMEM((512, D), BF),
            pltpu.VMEM((D, FT), BF),
            pltpu.SemaphoreType.DMA((32,)),
            pltpu.SemaphoreType.DMA((16,)),
        ],
        compiler_params=pltpu.CompilerParams(vmem_limit_bytes=56 * 2**20),
        name="feed_forward",
    )(pos, block_of, src, gain, *first, *second, *weights)


def finish_kernel(in_ref, even_ref, gated_ref):
    hot = one_hot(256)
    halves = []
    for zh in range(2):
        rows = jnp.concatenate([in_ref[x * 4 + zh * 2 + c] for x in range(4) for c in range(2)], axis=0)
        halves.append(jnp.dot(hot, rows, preferred_element_type=F32))
    a, b = halves
    lane = lax.broadcasted_iota(jnp.int32, (256, 128), 1)
    gated_ref[:, 0:768] = a[:, 0:768].astype(BF)
    gated_ref[:, 896:1664] = b[:, 0:768].astype(BF)
    am, bm = a[:, 768:896], b[:, 768:896]
    gated_ref[:, 768:896] = jnp.where(lane < 64, am, pltpu.roll(bm, 64, 1)).astype(BF)
    even_ref[:, 0:256] = a[:, 896:1152].astype(BF)
    even_ref[:, 256:384] = jnp.where(lane < 64, pltpu.roll(am, 64, 1), bm).astype(BF)
    even_ref[:, 384:640] = b[:, 896:1152].astype(BF)


def finish(parts):
    return pl.pallas_call(
        finish_kernel,
        out_shape=(jax.ShapeDtypeStruct((256, DT), BF), jax.ShapeDtypeStruct((256, FT), BF)),
        in_specs=[VM],
        out_specs=(VM, VM),
        compiler_params=pltpu.CompilerParams(vmem_limit_bytes=32 * 2**20),
        name="finish",
    )(parts)


def portion(gate_up, h):
    wide = [lax.dynamic_slice_in_dim(gate_up[:, j, :], h * 896, 768, 1) for j in range(2)]
    thin = [lax.dynamic_slice_in_dim(gate_up[:, j, :], 768 + h * 64, 64, 1) for j in range(2)]
    return jnp.concatenate(wide + thin, axis=1)


def per_device(
    residual, queries, cache_kv, fresh_kv, lengths, destination_place, out_weight, norm_gain, gate_up, block_of
):
    x, zh, c, zl, y = (lax.axis_index(a) for a in AX)
    pos = jnp.stack([x, zh, c, zl, y]).astype(jnp.int32)
    group = x * 4 + zh * 2 + c

    own = portion(gate_up, zh)
    other = portion(gate_up, 1 - zh)
    w0 = own
    w0p, w0m = along_x(w0, 1), along_x(w0, -1)
    w1 = swap(other, "zh")

    own_lengths = lax.dynamic_slice_in_dim(lengths, group * SEQS, SEQS, 0)
    terms = front(own_lengths, queries, fresh_kv, cache_kv, out_weight)

    terms, w0p, w0m, w1 = lax.optimization_barrier((terms, w0p, w0m, w1))
    w1p, w1m = along_x(w1, 1), along_x(w1, -1)
    w0a, w0b = along_x(w0p[:160], 1), along_x(w0m[160:], -1)

    terms = lax.all_to_all(terms, ("zl", "y"), 0, 0, tiled=True)
    mixed_residual = residual.reshape(8, 8, 4, DT).transpose(1, 0, 2, 3).reshape(256, DT)
    even = (mixed_residual.astype(F32) + jnp.sum(terms.astype(F32), axis=0)).astype(BF)

    even, w1p, w1m, w0a, w0b = lax.optimization_barrier((even, w1p, w1m, w0a, w0b))
    w1a, w1b = along_x(w1p[:160], 1), along_x(w1m[160:], -1)
    w0 = jnp.concatenate([w0, w0p, w0m, w0a, w0b], axis=0)
    w0s = swap(w0, "c")

    even = lax.all_to_all(even, ("x", "c"), 0, 0, tiled=True)

    h1, h2 = even[:128], even[128:]
    g1 = jnp.stack([h1, along_y(h1, 1), along_y(h1, -1), along_y(h1, 2)])
    g2 = jnp.stack([h2, along_z(h2, 1), along_z(h2, -1), along_z(h2, 2)])
    g1, g2, w1a, w1b = lax.optimization_barrier((g1, g2, w1a, w1b))
    w1 = jnp.concatenate([w1, w1p, w1m, w1a, w1b], axis=0)
    w1s = swap(w1, "c")
    first = [g1, along_z(g1, 1), along_z(g1, -1), along_z(g1, 2)]
    second = [g2, along_y(g2, 1), along_y(g2, -1), along_y(g2, 2)]

    slots = lax.iota(jnp.int32, 128)
    seq = jnp.sum(
        jnp.where(destination_place[None, :] == slots[:, None], slots[None, :], 0), axis=1
    )
    g = seq // 8
    base = (g // 2 % 2) * 256 + (g // 4 * 2 + g % 2) * 32 + seq % 8 * 4
    src = (base[:, None] + lax.iota(jnp.int32, 4)[None, :]).reshape(512, 1)
    both = feed(pos, block_of, src, norm_gain.reshape(1, D), first, second, [w0, w0s, w1, w1s])
    both = lax.all_to_all(both.reshape(16, 32, 1152), ("x", "zh", "c"), 0, 0, tiled=True)
    return finish(both)


def solution(mesh):
    inner = Mesh(mesh.devices.reshape(tuple(SIZES[a] for a in AX)), AX)
    grp, tp = ("x", "zh", "c"), ("zl", "y")
    return jax.shard_map(
        per_device,
        mesh=inner,
        in_specs=(
            P(grp, tp),
            P(grp, None, tp),
            P(grp, None, None, tp),
            P(grp, None, None, tp),
            P(),
            P(),
            P(tp, None),
            P(),
            P(grp, None, tp),
            P(),
        ),
        out_specs=(P(grp, tp), P(grp, tp)),
        check_vma=False,
    )
```

time: 519 us -> 245 us (0.47)
  waiting for transfers between devices: 357 us -> 74.6 us
  matrix products: 56.8 us -> 0 us
  starting transfers between devices: 0.16 us -> 45.9 us
  Pallas kernels: 0 us -> 40.1 us
  other arithmetic: 34.4 us -> 1.58 us
  local copies, waits for them, and re-layouts: 32.3 us -> 53.1 us
  between operations: 13.9 us -> 0.92 us
  blocking collectives: 15 us -> 27.9 us
  loops' own time: 7.46 us -> 0 us
    all_gather x3 -> x0, waiting for transfers between devices: 283 us -> none  [the longest x1 186 us: per_device(): lax.all_gather(gate_up, 'grp', axis=0, tiled=True)]
    reduce_scatter x1 -> x0, waiting for transfers between devices: 73.6 us -> none  [per_device(): lax.psum_scatter(head_terms, 'tp', scatter_dimension=1, tiled=True)]
    ppermute x0 -> x23, waiting for transfers between devices: none -> 60 us  [permute(): return lax.ppermute(value, axes, pairs)]
    dot_general x55 -> x0, matrix products: 56.8 us -> none  [the longest x1 15.8 us: per_device(): jnp.einsum('td,dgf->tgf', flattened, lax.all_gather(gate_up, 'grp', axis=...]
    pallas_call x0 -> x3, Pallas kernels: none -> 40.1 us  [the longest x1 22.5 us: feed(): pl.pallas_call(feed_kernel, out_shape=jax.ShapeDtypeStruct((512, 1152), B...]
    ppermute x0 -> x23, starting transfers between devices: none -> 34.5 us  [permute(): return lax.ppermute(value, axes, pairs)]
    all_to_all x0 -> x1, blocking collectives: none -> 27.9 us  [per_device(): lax.all_to_all(both.reshape(16, 32, 1152), ('x', 'zh', 'c'), 0, 0, tiled=...]
    lt x36 -> x0, other arithmetic: 20.3 us -> none  [block_scores(): in_use = first_pos + offsets < seq_length]
  transfers between devices with their start and end apart: 4 -> 25, of which waited for: 4 -> 13; matrix products, arithmetic and copies ran while one was open for 2% -> 14% of each run, Pallas kernels for 0% -> 7%
where the time goes in v1:
time: 245 us; the launch traced here: 244 us
  waiting for transfers between devices  74.6 us (30%)
  local copies, waits for them, and re-layouts  53.1 us (22%)
  starting transfers between devices  45.9 us (19%)
  Pallas kernels  40.1 us (16%)
  blocking collectives  27.9 us (11%)
    ppermute x23, waiting for transfers between devices, permute(): return lax.ppermute(value, axes, pairs)  60 us
    ppermute x23, starting transfers between devices, permute(): return lax.ppermute(value, axes, pairs)  34.5 us
    all_to_all x1, blocking collectives, per_device(): lax.all_to_all(both.reshape(16, 32, 1152), ('x', 'zh', 'c'), 0, 0, tiled=...  27.9 us
    pallas_call x1, Pallas kernels, feed(): pl.pallas_call(feed_kernel, out_shape=jax.ShapeDtypeStruct((512, 1152), B...  22.5 us
    unnamed x44, local copies, waits for them, and re-layouts  19.9 us
    pallas_call x1, Pallas kernels, front(): pl.pallas_call(front_kernel, out_shape=jax.ShapeDtypeStruct((8, 256, DT),...  15.9 us
    all_to_all x1, waiting for transfers between devices, per_device(): terms = lax.all_to_all(terms, ('zl', 'y'), 0, 0, tiled=True)  14.6 us
    all_to_all x1, starting transfers between devices, per_device(): even = lax.all_to_all(even, ('x', 'c'), 0, 0, tiled=True)  6.68 us
  transfers between devices with their start and end apart: 25, of which 13 were waited for; matrix products, arithmetic and copies ran while one was open for 14% of the time, Pallas kernels for 7%

profile of v1, /device:TPU:1, one launch (start us, length us, event | category | flops | bytes accessed | tf_op | source)
XLA Modules:
  0.0 244.0 jit_solution(6602592093837842116)
XLA Ops:
  0.6 6.7 %fusion.6 = (bf16[320,1,1664]{2,1,0:T(2,128)(2,1)S(1)}, bf16[320,1,1664]{2,1,0:T(2,128)(2,1)}) fusion(bf16[320,2,1664]{2,1,0:T(2,128)(2,1)} %param.18), kind=kLoop, calls=%fused_computation.56 | loop fusion | bytes 4259840 | tf_op jit(solution)/shard_map/slice | solution.py:274
  7.3 6.2 %constant_dynamic-slice_fusion.1 = (bf16[320,1,768]{2,1,0:T(2,128)(2,1)S(1)}, bf16[320,1,768]{2,1,0:T(2,128)(2,1)}, bf16[320,1,768]{2,1,0:T(2,128)(2,1)S(1)}, bf16[320,1,768]{2,1,0:T(2,128)(2,1)}) fusion(bf16[320,1,1664]{2,1,0:T(2,128)(2,1)S(1)} %get-tuple-element.36, s32[]{:T(128)S(6)} %select_n.83, s32[]{:T(128)S(6)} %select_n.81, ...), kind=kLoop, calls=%fused_computation.29 | loop fusion | bytes 3932168 | tf_op jit(solution)/shard_map/dynamic_slice | solution.py:274
  13.5 0.8 copy.60
  14.4 1.8 constant_dynamic-slice_fusion
  16.2 0.6 copy.64
  16.8 1.3 copy.61
  18.1 3.0 %concatenate.13 = bf16[320,1664]{1,0:T(8,128)(2,1)} concatenate(bf16[320,768]{1,0:T(8,128)(2,1)S(1)} %bitcast.48, bf16[320,768]{1,0:T(8,128)(2,1)} %bitcast.46, bf16[320,64]{1,0:T(8,128)(2,1)S(1)} %bitcast.60, bf16[320,64]{1,0:T(8,128)(2,1)} %bitcast.61), dimensions={1} | concatenate | bytes 2129920 | tf_op jit(solution)/shard_map/concatenate | solution.py:276
  21.1 4.4 %collective-permute-start.2 = (bf16[320,1664]{1,0:T(8,128)(2,1)}, bf16[320,1664]{1,0:T(8,128)(2,1)}, u32[]{:S(2)}, u32[]{:S(2)}) collective-permute-start(bf16[320,1664]{1,0:T(8,128)(2,1)} %concatenate.13), channel_id=1, source_target_pairs={{0,16},{16,0},{1,17},{17,1},{2,18},{18,2},{3,19},{19,3},{4,20},{20... | collective-permute-start | bytes 3194888 | tf_op jit(solution)/shard_map/ppermute | solution.py:48
  25.5 0.8 copy.62
  26.4 0.8 copy.63
  27.2 2.4 concatenate.12
  29.6 2.5 %collective-permute-start.1 = (bf16[320,1664]{1,0:T(8,128)(2,1)S(1)}, bf16[320,1664]{1,0:T(8,128)(2,1)S(1)}, u32[]{:S(2)}, u32[]{:S(2)}) collective-permute-start(bf16[320,1664]{1,0:T(8,128)(2,1)S(1)} %concatenate.12), channel_id=1, source_target_pairs={{0,96},{32,0},{64,32},{96,64},{1,97},{33,1},{65,33},{97,65},{2,98}... | collective-permute-start | bytes 3194888 | tf_op jit(solution)/shard_map/ppermute | solution.py:48
  32.2 15.9 %attend_project.1 = bf16[8,256,640]{2,1,0:T(8,128)(2,1)} custom-call(s32[8]{0:T(128)S(1)} %dynamic_slice.43.len_ref, bf16[8,32,1024]{2,1,0:T(8,128)(2,1)S(1)} %copy-done, bf16[8,2,32,128]{3,2,1,0:T(8,128)(2,1)S(1)} %copy-done.1, bf16[8,2,2048,128]{3,2,1,0:T(8,128)(2,1)} %cache_ref.1, bf16[1024,5120]{1,0:T(8,128)(2,1)} %ow_ref.1), custom_call_target="tpu_custom_call" | custom-call | tf_op jit(solution)/shard_map/attend_project/pallas_call | solution.py:147
  48.2 0.9 collective-permute-done.2
  49.0 5.0 %collective-permute-done.1 = bf16[320,1664]{1,0:T(8,128)(2,1)S(1)} collective-permute-done((bf16[320,1664]{1,0:T(8,128)(2,1)S(1)}, bf16[320,1664]{1,0:T(8,128)(2,1)S(1)}, u32[]{:S(2)}, u32[]{:S(2)}) %collective-permute-start.1) | collective-permute-done | bytes 1064992 | tf_op jit(solution)/shard_map/ppermute | solution.py:48
  54.0 3.2 %collective-permute-done = bf16[320,1664]{1,0:T(8,128)(2,1)} collective-permute-done((bf16[320,1664]{1,0:T(8,128)(2,1)S(1)}, bf16[320,1664]{1,0:T(8,128)(2,1)}, u32[]{:S(2)}, u32[]{:S(2)}) %collective-permute-start) | collective-permute-done | bytes 1064992 | tf_op jit(solution)/shard_map/ppermute | solution.py:48
  57.2 4.6 %all-to-all-start = ((bf16[8,256,640]{2,1,0:T(8,128)(2,1)}), bf16[8,256,640]{2,1,0:T(8,128)(2,1)S(1)}, u32[]{:S(2)}, u32[]{:S(2)}) async-start(bf16[8,256,640]{2,1,0:T(8,128)(2,1)} %attend_project.1), calls=%async_computation | async-start | bytes 5242880 | tf_op jit(solution)/shard_map/all_to_all | solution.py:299
  61.9 1.1 reshape.139
  63.0 0.9 copy.59
  63.9 1.3 reshape.138
  65.3 2.4 constant_dynamic-update-slice_fusion.4
  67.6 1.2 collective-permute-start.4
  69.1 2.3 constant_dynamic-update-slice_fusion.9
  71.4 1.9 slice.38
  73.3 0.9 slice.39
  74.2 2.4 collective-permute-start.6
  76.6 2.3 constant_dynamic-update-slice_fusion.3
  78.9 1.1 constant_dynamic-update-slice_fusion.2
  79.9 14.6 %all-to-all-done = bf16[8,256,640]{2,1,0:T(8,128)(2,1)S(1)} async-done(((bf16[8,256,640]{2,1,0:T(8,128)(2,1)}), bf16[8,256,640]{2,1,0:T(8,128)(2,1)S(1)}, u32[]{:S(2)}, u32[]{:S(2)}) %all-to-all-start) | async-done | bytes 2621472 | tf_op jit(solution)/shard_map/all_to_all | solution.py:299
  94.9 0.8 add_convert_fusion
  95.7 6.2 %collective-permute-done.6 = bf16[160,1664]{1,0:T(8,128)(2,1)} collective-permute-done((bf16[160,1664]{1,0:T(8,128)(2,1)}, bf16[160,1664]{1,0:T(8,128)(2,1)}, u32[]{:S(2)}, u32[]{:S(2)}) %collective-permute-start.6) | collective-permute-done | bytes 532512 | tf_op jit(solution)/shard_map/ppermute | solution.py:48
  101.9 2.4 collective-permute-done.5
  104.4 6.7 %all-to-all-start.1 = ((bf16[8,32,640]{2,1,0:T(8,128)(2,1)}), bf16[8,32,640]{2,1,0:T(8,128)(2,1)S(1)}, u32[]{:S(2)}, u32[]{:S(2)}) async-start(bf16[8,32,640]{2,1,0:T(8,128)(2,1)} %bitcast.14), calls=%async_computation.1 | async-start | bytes 655360 | tf_op jit(solution)/shard_map/all_to_all | solution.py:308
  111.0 1.1 slice.44
  112.1 1.1 slice.45
  113.2 2.7 %collective-permute-start.14 = (bf16[160,1664]{1,0:T(8,128)(2,1)S(1)}, bf16[160,1664]{1,0:T(8,128)(2,1)S(1)}, u32[]{:S(2)}, u32[]{:S(2)}) collective-permute-start(bf16[160,1664]{1,0:T(8,128)(2,1)S(1)} %slice.45), channel_id=1, source_target_pairs={{0,96},{32,0},{64,32},{96,64},{1,97},{33,1},{65,33},{97,65},{2,98}... | collective-permute-start | bytes 1597448 | tf_op jit(solution)/shard_map/ppermute | solution.py:48
  115.9 2.3 constant_dynamic-update-slice_fusion.8
  118.2 2.3 constant_dynamic-update-slice_fusion.7
  120.5 3.0 %collective-permute-start.9 = (bf16[128,640]{1,0:T(8,128)(2,1)S(1)}, bf16[128,640]{1,0:T(8,128)(2,1)S(1)}, u32[]{:S(2)}, u32[]{:S(2)}) collective-permute-start(bf16[128,640]{1,0:T(8,128)(2,1)S(1)} %bitcast.54), channel_id=1, source_target_pairs={{0,2},{1,3},{2,0},{3,1},{4,6},{5,7},{6,4},{7,5},{8,10},{9,11},{10,... | collective-permute-start | bytes 491528 | tf_op jit(solution)/shard_map/ppermute | solution.py:48
  123.6 0.9 collective-permute-start.8
  124.5 0.6 collective-permute-start.7
  125.0 1.9 constant_dynamic-update-slice_fusion.1
  127.2 0.9 collective-permute-start.12
  128.1 2.9 %collective-permute-done.8 = bf16[128,640]{1,0:T(8,128)(2,1)S(1)} collective-permute-done((bf16[128,640]{1,0:T(8,128)(2,1)S(1)}, bf16[128,640]{1,0:T(8,128)(2,1)S(1)}, u32[]{:S(2)}, u32[]{:S(2)}) %collective-permute-start.8) | collective-permute-done | bytes 163872 | tf_op jit(solution)/shard_map/ppermute | solution.py:48
  131.0 0.9 collective-permute-start.11
  131.9 0.8 collective-permute-start.10
  132.7 1.9 constant_dynamic-update-slice_fusion.refs_8_
  134.7 3.0 %collective-permute-start.21 = (bf16[1280,1664]{1,0:T(8,128)(2,1)}, bf16[1280,1664]{1,0:T(8,128)(2,1)}, u32[]{:S(2)}, u32[]{:S(2)}) collective-permute-start(bf16[1280,1664]{1,0:T(8,128)(2,1)} %constant_dynamic-update-slice_fusion.refs_8_), channel_id=1, source_target_pairs={{0,8},{8,0},{1,9},{9,1},{2,10},{10,2},{3,11},{11,3},{4,12},{12,4},... | collective-permute-start | bytes 12779528 | tf_op jit(solution)/shard_map/ppermute | solution.py:48
  138.2 0.9 constant_dynamic-update-slice_fusion.6
  139.1 0.9 constant_dynamic-update-slice_fusion.5.refs_10_
  140.0 2.7 %collective-permute-start.22 = (bf16[1280,1664]{1,0:T(8,128)(2,1)}, bf16[1280,1664]{1,0:T(8,128)(2,1)}, u32[]{:S(2)}, u32[]{:S(2)}) collective-permute-start(bf16[1280,1664]{1,0:T(8,128)(2,1)} %constant_dynamic-update-slice_fusion.5.refs_10_), channel_id=1, source_target_pairs={{0,8},{8,0},{1,9},{9,1},{2,10},{10,2},{3,11},{11,3},{4,12},{12,4},... | collective-permute-start | bytes 12779528 | tf_op jit(solution)/shard_map/ppermute | solution.py:48
  143.0 1.9 collective-permute-start.16
  144.9 15.7 %collective-permute-done.17.refs_3_ = bf16[4,128,640]{2,1,0:T(8,128)(2,1)S(1)} collective-permute-done((bf16[4,128,640]{2,1,0:T(8,128)(2,1)S(1)}, bf16[4,128,640]{2,1,0:T(8,128)(2,1)S(1)}, u32[]{:S(2)}, u32[]{:S(2)}) %collective-permute-start.17) | collective-permute-done | bytes 655392 | tf_op jit(solution)/shard_map/ppermute | solution.py:48
  160.6 2.7 %collective-permute-start.20 = (bf16[4,128,640]{2,1,0:T(8,128)(2,1)S(1)}, bf16[4,128,640]{2,1,0:T(8,128)(2,1)}, u32[]{:S(2)}, u32[]{:S(2)}) collective-permute-start(bf16[4,128,640]{2,1,0:T(8,128)(2,1)S(1)} %pad_maximum_fusion.1.refs_4_), channel_id=1, source_target_pairs={{0,2},{1,3},{2,0},{3,1},{4,6},{5,7},{6,4},{7,5},{8,10},{9,11},{10,... | collective-permute-start | bytes 1966088 | tf_op jit(solution)/shard_map/ppermute | solution.py:48
  163.3 9.6 %collective-permute-done.16.refs_2_ = bf16[4,128,640]{2,1,0:T(8,128)(2,1)S(1)} collective-permute-done((bf16[4,128,640]{2,1,0:T(8,128)(2,1)S(1)}, bf16[4,128,640]{2,1,0:T(8,128)(2,1)S(1)}, u32[]{:S(2)}, u32[]{:S(2)}) %collective-permute-start.16) | collective-permute-done | bytes 655392 | tf_op jit(solution)/shard_map/ppermute | solution.py:48
  172.9 2.4 collective-permute-start.19
  175.3 0.8 collective-permute-start.18
  176.1 0.6 reshape.136.gain_ref
  177.0 0.8 add.145.src_ref
  177.8 0.7 stack.53.pos_ref
  178.5 13.0 %collective-permute-done.19.refs_6_ = bf16[4,128,640]{2,1,0:T(8,128)(2,1)} collective-permute-done((bf16[4,128,640]{2,1,0:T(8,128)(2,1)S(1)}, bf16[4,128,640]{2,1,0:T(8,128)(2,1)}, u32[]{:S(2)}, u32[]{:S(2)}) %collective-permute-start.19) | collective-permute-done | bytes 655392 | tf_op jit(solution)/shard_map/ppermute | solution.py:48
  192.0 22.5 %feed_forward.1 = bf16[512,1152]{1,0:T(8,128)(2,1)} custom-call(s32[5]{0:T(128)} %stack.53.pos_ref, s32[16]{0:T(128)} %block_ref.1, s32[512,1]{1,0:T(8,128)} %add.145.src_ref, bf16[1,5120]{1,0:T(2,128)(2,1)} %reshape.136.gain_ref, bf16[4,128,640]{2,1,0:T(8,128)(2,1)} %copy-done.4, bf16[4,128,640]{2,1,0:T(8,128)(2,1)} %copy-done.10, ...), custom_call_target="tpu_custom_call" | custom-call | tf_op jit(solution)/shard_map/feed_forward/pallas_call | solution.py:228
  214.5 27.9 %all_to_all.19.in_ref = bf16[16,32,1152]{2,1,0:T(8,128)(2,1)S(1)} all-to-all(bf16[16,32,1152]{2,1,0:T(8,128)(2,1)} %bitcast.44), channel_id=1, replica_groups=mesh['x'=4,'zh'=2,'c'=2,'zl'=2,'y'=4] {'x','zh','c'}, dimensions={0} | all-to-all | bytes 2359296 | tf_op jit(solution)/shard_map/all_to_all | solution.py:327
  242.4 1.6 finish.1
  (60 shorter events, 2.6 us)
Async XLA Ops:
  16.1 9.4 %copy-start.3 = (bf16[320,1,768]{2,1,0:T(2,128)(2,1)S(1)}, bf16[320,1,768]{2,1,0:T(2,128)(2,1)}, u32[]{:S(2)}) copy-start(bf16[320,1,768]{2,1,0:T(2,128)(2,1)} %get-tuple-element.33) | copy-start | bytes 1474564
  18.1 14.1 %copy-start.12 = (s32[128]{0:T(128)S(1)}, s32[128]{0:T(128)}, u32[]{:S(2)}) copy-start(s32[128]{0:T(128)} %param.14) | copy-start | bytes 1540
  18.1 14.2 %copy-start = (bf16[8,32,1024]{2,1,0:T(8,128)(2,1)S(1)}, bf16[8,32,1024]{2,1,0:T(8,128)(2,1)}, u32[]{:S(2)}) copy-start(bf16[8,32,1024]{2,1,0:T(8,128)(2,1)} %q_ref.1) | copy-start | bytes 1572868
  18.1 14.1 %copy-start.1 = (bf16[8,2,32,128]{3,2,1,0:T(8,128)(2,1)S(1)}, bf16[8,2,32,128]{3,2,1,0:T(8,128)(2,1)}, u32[]{:S(2)}) copy-start(bf16[8,2,32,128]{3,2,1,0:T(8,128)(2,1)} %fresh_ref.1) | copy-start | bytes 393220
  21.1 28.0 %collective-permute-start.2 = (bf16[320,1664]{1,0:T(8,128)(2,1)}, bf16[320,1664]{1,0:T(8,128)(2,1)}, u32[]{:S(2)}, u32[]{:S(2)}) collective-permute-start(bf16[320,1664]{1,0:T(8,128)(2,1)} %concatenate.13), channel_id=1, source_target_pairs={{0,16},{16,0},{1,17},{17,1},{2,18},{18,2},{3,19},{19,3},{4,20},{20... | collective-permute-start | bytes 3194888 | tf_op jit(solution)/shard_map/ppermute | solution.py:48
  29.6 18.6 %copy-start.2 = (bf16[320,1664]{1,0:T(8,128)(2,1)}, bf16[320,1664]{1,0:T(8,128)(2,1)S(1)}, u32[]{:S(2)}) copy-start(bf16[320,1664]{1,0:T(8,128)(2,1)S(1)} %concatenate.12) | copy-start | bytes 3194884
  29.6 24.4 %collective-permute-start.1 = (bf16[320,1664]{1,0:T(8,128)(2,1)S(1)}, bf16[320,1664]{1,0:T(8,128)(2,1)S(1)}, u32[]{:S(2)}, u32[]{:S(2)}) collective-permute-start(bf16[320,1664]{1,0:T(8,128)(2,1)S(1)} %concatenate.12), channel_id=1, source_target_pairs={{0,96},{32,0},{64,32},{96,64},{1,97},{33,1},{65,33},{97,65},{2,98}... | collective-permute-start | bytes 3194888 | tf_op jit(solution)/shard_map/ppermute | solution.py:48
  32.2 25.1 %collective-permute-start = (bf16[320,1664]{1,0:T(8,128)(2,1)S(1)}, bf16[320,1664]{1,0:T(8,128)(2,1)}, u32[]{:S(2)}, u32[]{:S(2)}) collective-permute-start(bf16[320,1664]{1,0:T(8,128)(2,1)S(1)} %concatenate.12), channel_id=1, source_target_pairs={{0,32},{32,64},{64,96},{96,0},{1,33},{33,65},{65,97},{97,1},{2,34}... | collective-permute-start | bytes 3194888 | tf_op jit(solution)/shard_map/ppermute | solution.py:48
  54.0 3.2 %copy-start.6 = (bf16[320,1664]{1,0:T(8,128)(2,1)}, bf16[320,1664]{1,0:T(8,128)(2,1)S(1)}, u32[]{:S(2)}) copy-start(bf16[320,1664]{1,0:T(8,128)(2,1)S(1)} %collective-permute-done.1) | copy-start | bytes 3194884
  57.2 37.3 %all-to-all-start = ((bf16[8,256,640]{2,1,0:T(8,128)(2,1)}), bf16[8,256,640]{2,1,0:T(8,128)(2,1)S(1)}, u32[]{:S(2)}, u32[]{:S(2)}) async-start(bf16[8,256,640]{2,1,0:T(8,128)(2,1)} %attend_project.1), calls=%async_computation | async-start | bytes 5242880 | tf_op jit(solution)/shard_map/all_to_all | solution.py:299
  65.2 8.1 %copy-start.7 = (bf16[320,1664]{1,0:T(8,128)(2,1)S(1)}, bf16[320,1664]{1,0:T(8,128)(2,1)}, u32[]{:S(2)}) copy-start(bf16[320,1664]{1,0:T(8,128)(2,1)} %copy-done.6) | copy-start | bytes 3194884
  67.6 36.7 %collective-permute-start.4 = (bf16[320,1664]{1,0:T(8,128)(2,1)}, bf16[320,1664]{1,0:T(8,128)(2,1)}, u32[]{:S(2)}, u32[]{:S(2)}) collective-permute-start(bf16[320,1664]{1,0:T(8,128)(2,1)} %collective-permute-done.2), channel_id=1, source_target_pairs={{0,96},{32,0},{64,32},{96,64},{1,97},{33,1},{65,33},{97,65},{2,98}... | collective-permute-start | bytes 3194888 | tf_op jit(solution)/shard_map/ppermute | solution.py:48
  68.8 35.5 %collective-permute-start.3 = (bf16[320,1664]{1,0:T(8,128)(2,1)}, bf16[320,1664]{1,0:T(8,128)(2,1)}, u32[]{:S(2)}, u32[]{:S(2)}) collective-permute-start(bf16[320,1664]{1,0:T(8,128)(2,1)} %collective-permute-done.2), channel_id=1, source_target_pairs={{0,32},{32,64},{64,96},{96,0},{1,33},{33,65},{65,97},{97,1},{2,34}... | collective-permute-start | bytes 3194888 | tf_op jit(solution)/shard_map/ppermute | solution.py:48
  74.2 27.7 %collective-permute-start.6 = (bf16[160,1664]{1,0:T(8,128)(2,1)}, bf16[160,1664]{1,0:T(8,128)(2,1)}, u32[]{:S(2)}, u32[]{:S(2)}) collective-permute-start(bf16[160,1664]{1,0:T(8,128)(2,1)} %slice.39), channel_id=1, source_target_pairs={{0,96},{32,0},{64,32},{96,64},{1,97},{33,1},{65,33},{97,65},{2,98}... | collective-permute-start | bytes 1597448 | tf_op jit(solution)/shard_map/ppermute | solution.py:48
  76.6 27.8 %collective-permute-start.5 = (bf16[160,1664]{1,0:T(8,128)(2,1)}, bf16[160,1664]{1,0:T(8,128)(2,1)}, u32[]{:S(2)}, u32[]{:S(2)}) collective-permute-start(bf16[160,1664]{1,0:T(8,128)(2,1)} %slice.38), channel_id=1, source_target_pairs={{0,32},{32,64},{64,96},{96,0},{1,33},{33,65},{65,97},{97,1},{2,34}... | collective-permute-start | bytes 1597448 | tf_op jit(solution)/shard_map/ppermute | solution.py:48
  104.4 16.1 %all-to-all-start.1 = ((bf16[8,32,640]{2,1,0:T(8,128)(2,1)}), bf16[8,32,640]{2,1,0:T(8,128)(2,1)S(1)}, u32[]{:S(2)}, u32[]{:S(2)}) async-start(bf16[8,32,640]{2,1,0:T(8,128)(2,1)} %bitcast.14), calls=%async_computation.1 | async-start | bytes 655360 | tf_op jit(solution)/shard_map/all_to_all | solution.py:308
  113.2 24.9 %collective-permute-start.14 = (bf16[160,1664]{1,0:T(8,128)(2,1)S(1)}, bf16[160,1664]{1,0:T(8,128)(2,1)S(1)}, u32[]{:S(2)}, u32[]{:S(2)}) collective-permute-start(bf16[160,1664]{1,0:T(8,128)(2,1)S(1)} %slice.45), channel_id=1, source_target_pairs={{0,96},{32,0},{64,32},{96,64},{1,97},{33,1},{65,33},{97,65},{2,98}... | collective-permute-start | bytes 1597448 | tf_op jit(solution)/shard_map/ppermute | solution.py:48
  115.9 22.2 %collective-permute-start.13 = (bf16[160,1664]{1,0:T(8,128)(2,1)S(1)}, bf16[160,1664]{1,0:T(8,128)(2,1)S(1)}, u32[]{:S(2)}, u32[]{:S(2)}) collective-permute-start(bf16[160,1664]{1,0:T(8,128)(2,1)S(1)} %slice.44), channel_id=1, source_target_pairs={{0,32},{32,64},{64,96},{96,0},{1,33},{33,65},{65,97},{97,1},{2,34}... | collective-permute-start | bytes 1597448 | tf_op jit(solution)/shard_map/ppermute | solution.py:48
  120.5 55.7 %copy-start.11 = (bf16[5120]{0:T(1024)(128)(2,1)S(1)}, bf16[5120]{0:T(1024)(128)(2,1)}, u32[]{:S(2)}) copy-start(bf16[5120]{0:T(1024)(128)(2,1)} %param.17) | copy-start | bytes 30724
  120.5 56.3 %copy-start.13 = (s32[128]{0:T(128)S(1)}, s32[128]{0:T(128)}, u32[]{:S(2)}) copy-start(s32[128]{0:T(128)} %param.15) | copy-start | bytes 1540
  120.5 6.7 %collective-permute-start.9 = (bf16[128,640]{1,0:T(8,128)(2,1)S(1)}, bf16[128,640]{1,0:T(8,128)(2,1)S(1)}, u32[]{:S(2)}, u32[]{:S(2)}) collective-permute-start(bf16[128,640]{1,0:T(8,128)(2,1)S(1)} %bitcast.54), channel_id=1, source_target_pairs={{0,2},{1,3},{2,0},{3,1},{4,6},{5,7},{6,4},{7,5},{8,10},{9,11},{10,... | collective-permute-start | bytes 491528 | tf_op jit(solution)/shard_map/ppermute | solution.py:48
  123.6 7.4 %collective-permute-start.8 = (bf16[128,640]{1,0:T(8,128)(2,1)S(1)}, bf16[128,640]{1,0:T(8,128)(2,1)S(1)}, u32[]{:S(2)}, u32[]{:S(2)}) collective-permute-start(bf16[128,640]{1,0:T(8,128)(2,1)S(1)} %bitcast.55), channel_id=1, source_target_pairs={{0,3},{1,0},{2,1},{3,2},{4,7},{5,4},{6,5},{7,6},{8,11},{9,8},{10,9... | collective-permute-start | bytes 491528 | tf_op jit(solution)/shard_map/ppermute | solution.py:48
  124.5 7.4 %collective-permute-start.7 = (bf16[128,640]{1,0:T(8,128)(2,1)S(1)}, bf16[128,640]{1,0:T(8,128)(2,1)S(1)}, u32[]{:S(2)}, u32[]{:S(2)}) collective-permute-start(bf16[128,640]{1,0:T(8,128)(2,1)S(1)} %bitcast.56), channel_id=1, source_target_pairs={{0,1},{1,2},{2,3},{3,0},{4,5},{5,6},{6,7},{7,4},{8,9},{9,10},{10,1... | collective-permute-start | bytes 491528 | tf_op jit(solution)/shard_map/ppermute | solution.py:48
  127.2 7.5 %collective-permute-start.12 = (bf16[128,640]{1,0:T(8,128)(2,1)S(1)}, bf16[128,640]{1,0:T(8,128)(2,1)S(1)}, u32[]{:S(2)}, u32[]{:S(2)}) collective-permute-start(bf16[128,640]{1,0:T(8,128)(2,1)S(1)} %bitcast.50), channel_id=1, source_target_pairs={{0,16},{4,20},{16,0},{20,4},{1,17},{5,21},{17,1},{21,5},{2,18},{6,... | collective-permute-start | bytes 491528 | tf_op jit(solution)/shard_map/ppermute | solution.py:48
  131.0 6.7 %collective-permute-start.11 = (bf16[128,640]{1,0:T(8,128)(2,1)S(1)}, bf16[128,640]{1,0:T(8,128)(2,1)S(1)}, u32[]{:S(2)}, u32[]{:S(2)}) collective-permute-start(bf16[128,640]{1,0:T(8,128)(2,1)S(1)} %bitcast.51), channel_id=1, source_target_pairs={{0,20},{4,0},{16,4},{20,16},{1,21},{5,1},{17,5},{21,17},{2,22},{6,... | collective-permute-start | bytes 491528 | tf_op jit(solution)/shard_map/ppermute | solution.py:48
  131.9 6.1 %collective-permute-start.10 = (bf16[128,640]{1,0:T(8,128)(2,1)S(1)}, bf16[128,640]{1,0:T(8,128)(2,1)S(1)}, u32[]{:S(2)}, u32[]{:S(2)}) collective-permute-start(bf16[128,640]{1,0:T(8,128)(2,1)S(1)} %bitcast.52), channel_id=1, source_target_pairs={{0,4},{4,16},{16,20},{20,0},{1,5},{5,17},{17,21},{21,1},{2,6},{6,1... | collective-permute-start | bytes 491528 | tf_op jit(solution)/shard_map/ppermute | solution.py:48
  134.7 57.3 %copy-start.4 = (bf16[4,128,640]{2,1,0:T(8,128)(2,1)}, bf16[4,128,640]{2,1,0:T(8,128)(2,1)S(1)}, u32[]{:S(2)}) copy-start(bf16[4,128,640]{2,1,0:T(8,128)(2,1)S(1)} %pad_maximum_fusion.refs_0_) | copy-start | bytes 1966084
  134.7 57.2 %collective-permute-start.21 = (bf16[1280,1664]{1,0:T(8,128)(2,1)}, bf16[1280,1664]{1,0:T(8,128)(2,1)}, u32[]{:S(2)}, u32[]{:S(2)}) collective-permute-start(bf16[1280,1664]{1,0:T(8,128)(2,1)} %constant_dynamic-update-slice_fusion.refs_8_), channel_id=1, source_target_pairs={{0,8},{8,0},{1,9},{9,1},{2,10},{10,2},{3,11},{11,3},{4,12},{12,4},... | collective-permute-start | bytes 12779528 | tf_op jit(solution)/shard_map/ppermute | solution.py:48
  138.1 53.8 %copy-start.5 = (bf16[4,128,640]{2,1,0:T(8,128)(2,1)}, bf16[4,128,640]{2,1,0:T(8,128)(2,1)S(1)}, u32[]{:S(2)}) copy-start(bf16[4,128,640]{2,1,0:T(8,128)(2,1)S(1)} %pad_maximum_fusion.1.refs_4_) | copy-start | bytes 1966084
  140.0 52.0 %collective-permute-start.22 = (bf16[1280,1664]{1,0:T(8,128)(2,1)}, bf16[1280,1664]{1,0:T(8,128)(2,1)}, u32[]{:S(2)}, u32[]{:S(2)}) collective-permute-start(bf16[1280,1664]{1,0:T(8,128)(2,1)} %constant_dynamic-update-slice_fusion.5.refs_10_), channel_id=1, source_target_pairs={{0,8},{8,0},{1,9},{9,1},{2,10},{10,2},{3,11},{11,3},{4,12},{12,4},... | collective-permute-start | bytes 12779528 | tf_op jit(solution)/shard_map/ppermute | solution.py:48
  142.7 17.9 %collective-permute-start.17 = (bf16[4,128,640]{2,1,0:T(8,128)(2,1)S(1)}, bf16[4,128,640]{2,1,0:T(8,128)(2,1)S(1)}, u32[]{:S(2)}, u32[]{:S(2)}) collective-permute-start(bf16[4,128,640]{2,1,0:T(8,128)(2,1)S(1)} %pad_maximum_fusion.refs_0_), channel_id=1, source_target_pairs={{0,16},{4,20},{16,0},{20,4},{1,17},{5,21},{17,1},{21,5},{2,18},{6,... | collective-permute-start | bytes 1966088 | tf_op jit(solution)/shard_map/ppermute | solution.py:48
  143.0 29.9 %collective-permute-start.16 = (bf16[4,128,640]{2,1,0:T(8,128)(2,1)S(1)}, bf16[4,128,640]{2,1,0:T(8,128)(2,1)S(1)}, u32[]{:S(2)}, u32[]{:S(2)}) collective-permute-start(bf16[4,128,640]{2,1,0:T(8,128)(2,1)S(1)} %pad_maximum_fusion.refs_0_), channel_id=1, source_target_pairs={{0,20},{4,0},{16,4},{20,16},{1,21},{5,1},{17,5},{21,17},{2,22},{6,... | collective-permute-start | bytes 1966088 | tf_op jit(solution)/shard_map/ppermute | solution.py:48
  144.9 30.4 %collective-permute-start.15 = (bf16[4,128,640]{2,1,0:T(8,128)(2,1)S(1)}, bf16[4,128,640]{2,1,0:T(8,128)(2,1)S(1)}, u32[]{:S(2)}, u32[]{:S(2)}) collective-permute-start(bf16[4,128,640]{2,1,0:T(8,128)(2,1)S(1)} %pad_maximum_fusion.refs_0_), channel_id=1, source_target_pairs={{0,4},{4,16},{16,20},{20,0},{1,5},{5,17},{17,21},{21,1},{2,6},{6,1... | collective-permute-start | bytes 1966088 | tf_op jit(solution)/shard_map/ppermute | solution.py:48
  160.6 31.3 %copy-start.8 = (bf16[4,128,640]{2,1,0:T(8,128)(2,1)}, bf16[4,128,640]{2,1,0:T(8,128)(2,1)S(1)}, u32[]{:S(2)}) copy-start(bf16[4,128,640]{2,1,0:T(8,128)(2,1)S(1)} %collective-permute-done.17.refs_3_) | copy-start | bytes 1966084
  160.6 17.9 %collective-permute-start.20 = (bf16[4,128,640]{2,1,0:T(8,128)(2,1)S(1)}, bf16[4,128,640]{2,1,0:T(8,128)(2,1)}, u32[]{:S(2)}, u32[]{:S(2)}) collective-permute-start(bf16[4,128,640]{2,1,0:T(8,128)(2,1)S(1)} %pad_maximum_fusion.1.refs_4_), channel_id=1, source_target_pairs={{0,2},{1,3},{2,0},{3,1},{4,6},{5,7},{6,4},{7,5},{8,10},{9,11},{10,... | collective-permute-start | bytes 1966088 | tf_op jit(solution)/shard_map/ppermute | solution.py:48
  172.9 19.0 %copy-start.9 = (bf16[4,128,640]{2,1,0:T(8,128)(2,1)}, bf16[4,128,640]{2,1,0:T(8,128)(2,1)S(1)}, u32[]{:S(2)}) copy-start(bf16[4,128,640]{2,1,0:T(8,128)(2,1)S(1)} %collective-permute-done.16.refs_2_) | copy-start | bytes 1966084
  172.9 18.6 %collective-permute-start.19 = (bf16[4,128,640]{2,1,0:T(8,128)(2,1)S(1)}, bf16[4,128,640]{2,1,0:T(8,128)(2,1)}, u32[]{:S(2)}, u32[]{:S(2)}) collective-permute-start(bf16[4,128,640]{2,1,0:T(8,128)(2,1)S(1)} %pad_maximum_fusion.1.refs_4_), channel_id=1, source_target_pairs={{0,3},{1,0},{2,1},{3,2},{4,7},{5,4},{6,5},{7,6},{8,11},{9,8},{10,9... | collective-permute-start | bytes 1966088 | tf_op jit(solution)/shard_map/ppermute | solution.py:48
  175.3 16.6 %copy-start.10 = (bf16[4,128,640]{2,1,0:T(8,128)(2,1)}, bf16[4,128,640]{2,1,0:T(8,128)(2,1)S(1)}, u32[]{:S(2)}) copy-start(bf16[4,128,640]{2,1,0:T(8,128)(2,1)S(1)} %collective-permute-done.15.refs_1_) | copy-start | bytes 1966084
  175.3 16.6 %collective-permute-start.18 = (bf16[4,128,640]{2,1,0:T(8,128)(2,1)S(1)}, bf16[4,128,640]{2,1,0:T(8,128)(2,1)}, u32[]{:S(2)}, u32[]{:S(2)}) collective-permute-start(bf16[4,128,640]{2,1,0:T(8,128)(2,1)S(1)} %pad_maximum_fusion.1.refs_4_), channel_id=1, source_target_pairs={{0,1},{1,2},{2,3},{3,0},{4,5},{5,6},{6,7},{7,4},{8,9},{9,10},{10,1... | collective-permute-start | bytes 1966088 | tf_op jit(solution)/shard_map/ppermute | solution.py:48

commit v2 on v1

v2 whole, which is shorter than its diff:
```python
import functools

import jax
import jax.numpy as jnp
from jax import lax
from jax.experimental import pallas as pl
from jax.experimental.pallas import tpu as pltpu
from jax.sharding import Mesh, PartitionSpec as P

AX = ("x", "zh", "c", "zl", "y")
SIZES = dict(x=4, zh=2, c=2, zl=2, y=4)
BF = jnp.bfloat16
F32 = jnp.float32
HD = 128
HEADS = 8
SEQS = 8
ROWS = 32
LMAX = 2048
KB = 512
NB = LMAX // KB
D = 5120
DT = 640
BLK = 320
FT = 1664
NEG = -1e30
EPS = 1e-6
NC = 1
RR = 4 // NC
CR = 64 * RR
NH = 896
VM = pl.BlockSpec(memory_space=pltpu.VMEM)
SM = pl.BlockSpec(memory_space=pltpu.SMEM)
ANY = pl.BlockSpec(memory_space=pl.ANY)


def permute(value, axes, move):
    sizes = [SIZES[a] for a in axes]
    total = 1
    for n in sizes:
        total *= n
    pairs = []
    for i in range(total):
        coords, rest = [], i
        for n in reversed(sizes):
            coords.append(rest % n)
            rest //= n
        target = move(*reversed(coords))
        j = 0
        for n, q in zip(sizes, target):
            j = j * n + q
        pairs.append((i, j))
    return lax.ppermute(value, axes, pairs)


def along_x(value, k):
    return permute(value, ("x",), lambda x: ((x + k) % 4,))


def along_y(value, k):
    return permute(value, ("y",), lambda y: ((y + k) % 4,))


def along_z(value, k):
    def move(zh, zl):
        z = (zh * 2 + zl + k) % 4
        return (z // 2, z % 2)

    return permute(value, ("zh", "zl"), move)


def swap(value, axis):
    return permute(value, (axis,), lambda q: (1 - q,))


def one_hot(n, source):
    out = lax.broadcasted_iota(jnp.int32, (n, n), 0)
    src = lax.broadcasted_iota(jnp.int32, (n, n), 1)
    return (source(out) == src).astype(BF)


def spread(row):
    return row // RR % 8 * ROWS + row // (8 * RR) % 8 * 4 + row // CR * RR + row % RR


def gather(row):
    return row // RR % NC * CR + row // 4 % 8 * (8 * RR) + row // ROWS * RR + row % RR


def front_kernel(len_ref, q_ref, fresh_ref, res_ref, cache_ref, ow_ref, *refs):
    out_refs, (kv, ow, ctx, kv_sem, ow_sem) = refs[:NC], refs[NC:]
    def kv_copy(s, b):
        part = pl.ds(b * KB, KB)
        return pltpu.make_async_copy(
            cache_ref.at[s, :, part, :], kv.at[s, :, part, :], kv_sem.at[s, b]
        )

    for s in range(SEQS):
        for b in range(NB):

            @pl.when(b * KB < len_ref[s])
            def _(s=s, b=b):
                kv_copy(s, b).start()

    ow_copy = pltpu.make_async_copy(ow_ref, ow, ow_sem)
    ow_copy.start()
    factor = HD ** -0.5 * 1.4426950408889634
    nt = (((1,), (1,)), ((), ()))
    nn = (((1,), (0,)), ((), ()))

    def sequence(s, _):
        length = len_ref[s]
        rows = q_ref[s]
        q = jnp.concatenate([rows[:, h * HD : (h + 1) * HD] for h in range(HEADS)], axis=0)
        scores = lax.dot_general(q, fresh_ref[s, 0], nt, preferred_element_type=F32) * factor
        i = lax.broadcasted_iota(jnp.int32, scores.shape, 0) % ROWS
        j = lax.broadcasted_iota(jnp.int32, scores.shape, 1)
        scores = jnp.where(j <= i, scores, NEG)
        high = jnp.max(scores, axis=1, keepdims=True)
        p = jnp.exp2(scores - high)
        total = jnp.sum(p, axis=1, keepdims=True)
        acc = lax.dot_general(p.astype(BF), fresh_ref[s, 1], nn, preferred_element_type=F32)

        def block(b, carry):
            high, total, acc = carry
            kv_copy(s, b).wait()
            start = pl.multiple_of(b * KB, KB)
            k = kv[s, 0, pl.ds(start, KB), :]
            v = kv[s, 1, pl.ds(start, KB), :]
            scores = lax.dot_general(q, k, nt, preferred_element_type=F32) * factor
            pos = lax.broadcasted_iota(jnp.int32, scores.shape, 1)
            scores = jnp.where(pos < length - start, scores, NEG)
            new = jnp.maximum(high, jnp.max(scores, axis=1, keepdims=True))
            old = jnp.exp2(high - new)
            p = jnp.exp2(scores - new)
            total = total * old + jnp.sum(p, axis=1, keepdims=True)
            acc = acc * old + lax.dot_general(p.astype(BF), v, nn, preferred_element_type=F32)
            return new, total, acc

        high, total, acc = lax.fori_loop(0, (length + KB - 1) // KB, block, (high, total, acc))
        done = (acc / total).astype(BF)
        at = pl.ds(pl.multiple_of(s * ROWS, ROWS), ROWS)
        for h in range(HEADS):
            ctx[at, h * HD : (h + 1) * HD] = done[h * ROWS : (h + 1) * ROWS, :]
        return 0

    lax.fori_loop(0, SEQS, sequence, 0)
    hot = one_hot(256, spread)
    mixed = jnp.dot(hot, ctx[...], preferred_element_type=F32).astype(BF)
    residual = jnp.dot(hot, res_ref[...], preferred_element_type=F32)
    ow_copy.wait()
    for t in range(8):
        terms = jnp.dot(mixed, ow[:, t * DT : (t + 1) * DT], preferred_element_type=F32)
        terms = (terms + jnp.where(len_ref[SEQS] == t, residual, 0.0)).astype(BF)
        for q in range(NC):
            out_refs[q][t] = terms[q * CR : (q + 1) * CR]


def front(lengths, queries, fresh, residual, cache, out_weight):
    return pl.pallas_call(
        front_kernel,
        out_shape=[jax.ShapeDtypeStruct((8, CR, DT), BF)] * NC,
        in_specs=[SM, VM, VM, VM, ANY, ANY],
        out_specs=[VM] * NC,
        scratch_shapes=[
            pltpu.VMEM((SEQS, 2, LMAX, HD), BF),
            pltpu.VMEM((1024, D), BF),
            pltpu.VMEM((256, 1024), BF),
            pltpu.SemaphoreType.DMA((SEQS, NB)),
            pltpu.SemaphoreType.DMA,
        ],
        compiler_params=pltpu.CompilerParams(vmem_limit_bytes=48 * 2**20),
        name="attend_project",
    )(lengths, queries, fresh, residual, cache, out_weight)


def feed_kernel(pos_ref, block_ref, src_ref, gain_ref, *refs):
    arrived, (near_ref, far_ref, out_ref, act, normed, w, act_sem, w_sem) = refs[:10], refs[10:]
    zh, tp, z, y = (pos_ref[i] for i in range(4))
    half = CR // 2
    steps = (0, 3, 1, 2)
    pieces = []
    for h in range(2):
        own, one, two, low, high = arrived[h * 5 : h * 5 + 5]
        blocks = [(own, j, 0, j) for j in range(4)]
        blocks += [(one, j, 3, j) for j in range(4)] + [(two, j, 1, j) for j in range(4)]
        blocks += [(low, j, 2, j) for j in range(2)] + [(high, j, 2, j + 2) for j in range(2)]
        for n, (ref, at, outer, j) in enumerate(blocks):
            dz, dy = (outer, steps[j]) if h == 0 else (steps[j], outer)
            zz = (z + dz) % 4
            row = pl.multiple_of(zz // 2 * CR + h * half, half)
            col = pl.multiple_of((zz % 2 * 4 + (y + dy) % 4) * DT, 128)
            pieces.append(
                pltpu.make_async_copy(
                    ref.at[at], act.at[pl.ds(row, half), pl.ds(col, DT)], act_sem.at[h * 16 + n]
                )
            )
    for copy in pieces:
        copy.start()

    tiles = ((0, 256), (256, 256), (512, 256), (768, 128))

    def weights(n):
        at, size = tiles[n]
        copies = []
        for dz, source in enumerate((near_ref, far_ref)):
            for i in range(8):
                g = i // 2 * 4 + (zh + dz) % 2 * 2 + i % 2
                row = pl.multiple_of(block_ref[g] * BLK, BLK)
                copies.append(
                    pltpu.make_async_copy(
                        source.at[i, :, :, pl.ds(at, size)],
                        w.at[:, pl.ds(row, BLK), pl.ds(at, size)],
                        w_sem.at[n, dz * 8 + i],
                    )
                )
        return copies

    for copy in weights(0):
        copy.start()
    for copy in pieces:
        copy.wait()
    for copy in weights(1):
        copy.start()
    gain = gain_ref[...].astype(F32)
    for r in range(0, 2 * CR, 64):
        rows = act[r : r + 64, :].astype(F32)
        inverse = lax.rsqrt(jnp.sum(rows * rows, axis=1, keepdims=True) / D + EPS)
        normed[r : r + 64, :] = (rows * inverse * gain).astype(BF)
    lhs = normed[...]
    for n, (at, size) in enumerate(tiles):
        for copy in weights(n):
            copy.wait()
        if n + 2 < len(tiles):
            for copy in weights(n + 2):
                copy.start()
        g = jnp.dot(lhs, w[0, :, at : at + size], preferred_element_type=F32)
        u = jnp.dot(lhs, w[1, :, at : at + size], preferred_element_type=F32)
        out_ref[:, at : at + size] = (g / (1 + jnp.exp(-g)) * u).astype(BF)
    own = pl.multiple_of(tp * DT, 128)
    flag = zh == 0
    mid = act[:, pl.ds(pl.multiple_of(own + 256, 128), 128)]
    low = act[:, pl.ds(own, 256)]
    high = act[:, pl.ds(pl.multiple_of(own + 384, 128), 256)]
    out_ref[:, 896:1152] = jnp.where(flag, low.astype(F32), high.astype(F32)).astype(BF)

    @pl.when(jnp.logical_not(flag))
    def _():
        out_ref[:, 0:128] = mid

    hot = (src_ref[...] == lax.broadcasted_iota(jnp.int32, (2 * CR, 2 * CR), 1)).astype(BF)
    out_ref[...] = jnp.dot(hot, out_ref[...], preferred_element_type=F32).astype(BF)


def feed(pos, block_of, src, gain, arrived, near, far):
    return pl.pallas_call(
        feed_kernel,
        out_shape=jax.ShapeDtypeStruct((2 * CR, 1152), BF),
        in_specs=[SM, SM, VM, VM] + [ANY] * 12,
        out_specs=VM,
        scratch_shapes=[
            pltpu.VMEM((2 * CR, D), BF),
            pltpu.VMEM((2 * CR, D), BF),
            pltpu.VMEM((2, D, NH), BF),
            pltpu.SemaphoreType.DMA((32,)),
            pltpu.SemaphoreType.DMA((4, 16)),
        ],
        compiler_params=pltpu.CompilerParams(vmem_limit_bytes=56 * 2**20),
        name="feed_forward",
    )(pos, block_of, src, gain, *arrived, near, far)


def finish_kernel(*refs):
    in_refs, (even_ref, gated_ref) = refs[:NC], refs[NC:]
    hot = one_hot(256, gather)
    halves = []
    for zh in range(2):
        rows = jnp.concatenate(
            [r[x * 4 + zh * 2 + c] for r in in_refs for x in range(4) for c in range(2)], axis=0
        )
        halves.append(jnp.dot(hot, rows, preferred_element_type=F32).astype(BF))
    a, b = halves
    gated_ref[:, 0:896] = a[:, 0:896]
    gated_ref[:, 896:1664] = b[:, 128:896]
    even_ref[:, 0:256] = a[:, 896:1152]
    even_ref[:, 256:384] = b[:, 0:128]
    even_ref[:, 384:640] = b[:, 896:1152]


def finish(parts):
    return pl.pallas_call(
        finish_kernel,
        out_shape=(jax.ShapeDtypeStruct((256, DT), BF), jax.ShapeDtypeStruct((256, FT), BF)),
        in_specs=[VM] * NC,
        out_specs=(VM, VM),
        compiler_params=pltpu.CompilerParams(vmem_limit_bytes=32 * 2**20),
        name="finish",
    )(*parts)


def per_device(
    residual, queries, cache_kv, fresh_kv, lengths, destination_place, out_weight, norm_gain, gate_up, block_of
):
    x, zh, c, zl, y = (lax.axis_index(a) for a in AX)
    pos = jnp.stack([zh, zl * 4 + y, zh * 2 + zl, y]).astype(jnp.int32)
    group = x * 4 + zh * 2 + c

    both = lax.optimization_barrier(gate_up.transpose(1, 0, 2))
    left, right = both[:, :, :NH], both[:, :, FT - NH :]
    own = jnp.where(zh == 0, left, right)
    other = jnp.where(zh == 0, right, left)
    near = lax.all_gather(own, ("x", "c"), axis=0)
    lower, upper = swap(other[:, : BLK // 2], "zh"), swap(other[:, BLK // 2 :], "zh")

    own_lengths = lax.dynamic_slice_in_dim(lengths, group * SEQS, SEQS, 0)
    scalars = jnp.concatenate([own_lengths, pos[1:2]])
    terms = front(scalars, queries, fresh_kv, residual, cache_kv, out_weight)
    lower, *terms = lax.optimization_barrier((lower, *terms))

    slots = lax.iota(jnp.int32, 128)
    seq = jnp.sum(
        jnp.where(destination_place[None, :] == slots[:, None], slots[None, :], 0), axis=1
    )
    g = seq // 8
    base = (g // 2 % 2) * CR + (g // 4 * 2 + g % 2) * (8 * RR) + seq % 8 * RR
    src = (base[:, None] + lax.iota(jnp.int32, RR)[None, :]).reshape(2 * CR, 1)
    gain = norm_gain.reshape(1, D)

    parts = []
    for q in range(NC):
        got = lax.all_to_all(terms[q], ("zl", "y"), 0, 0, tiled=True)
        even = jnp.sum(got.astype(F32), axis=0).astype(BF)
        even = lax.all_to_all(even, ("x", "c"), 0, 0, tiled=True)
        if q == 0:
            upper, even = lax.optimization_barrier((upper, even))
            other = jnp.concatenate([lower, upper], axis=1)
            far = lax.all_gather(other, ("x", "c"), axis=0)
        h1, h2 = even[: CR // 2], even[CR // 2 :]
        g1 = jnp.stack([h1, along_y(h1, 1), along_y(h1, -1), along_y(h1, 2)])
        g2 = jnp.stack([h2, along_z(h2, 1), along_z(h2, -1), along_z(h2, 2)])
        g1, g2 = lax.optimization_barrier((g1, g2))
        a1, a2, b1, b2 = along_z(g1, 1), along_z(g1, -1), along_y(g2, 1), along_y(g2, -1)
        a1, a2, b1, b2 = lax.optimization_barrier((a1, a2, b1, b2))
        arrived = [g1, a1, a2, along_z(a1[:2], 1), along_z(a2[2:], -1)]
        arrived += [g2, b1, b2, along_y(b1[:2], 1), along_y(b2[2:], -1)]
        mixed = feed(pos, block_of, src, gain, arrived, near, far)
        parts.append(lax.all_to_all(mixed.reshape(16, 8 * RR, 1152), ("x", "zh", "c"), 0, 0, tiled=True))
    return finish(parts)


def solution(mesh):
    inner = Mesh(mesh.devices.reshape(tuple(SIZES[a] for a in AX)), AX)
    grp, tp = ("x", "zh", "c"), ("zl", "y")
    return jax.shard_map(
        per_device,
        mesh=inner,
        in_specs=(
            P(grp, tp),
            P(grp, None, tp),
            P(grp, None, None, tp),
            P(grp, None, None, tp),
            P(),
            P(),
            P(tp, None),
            P(),
            P(grp, None, tp),
            P(),
        ),
        out_specs=(P(grp, tp), P(grp, tp)),
        check_vma=False,
    )
```

time: 245 us -> 199 us (0.81)
  local copies, waits for them, and re-layouts: 53.1 us -> 7.77 us
  starting transfers between devices: 45.9 us -> 31.2 us
  between operations: 0.92 us -> 14.3 us
  other arithmetic: 1.58 us -> 5.76 us
  waiting for transfers between devices: 74.6 us -> 71.2 us
  blocking collectives: 27.9 us -> 25 us
    ppermute x23 -> x16, waiting for transfers between devices: 60 us -> 30.5 us  [permute(): return lax.ppermute(value, axes, pairs)]
    unnamed x44 -> x31, local copies, waits for them, and re-layouts: 19.9 us -> 1.89 us
    all_to_all x1, waiting for transfers between devices: 14.6 us -> 32 us  [per_device(): got = lax.all_to_all(terms[q], ('zl', 'y'), 0, 0, tiled=True)]
    ppermute x23 -> x16, starting transfers between devices: 34.5 us -> 22.3 us  [permute(): return lax.ppermute(value, axes, pairs)]
    concatenate x4 -> x0, local copies, waits for them, and re-layouts: 8.11 us -> none  [the longest x2 5.34 us: portion(): return jnp.concatenate(wide + thin, axis=1)]
    dynamic_slice x2 -> x0, local copies, waits for them, and re-layouts: 7.99 us -> none  [the longest x1 6.22 us: portion(): lax.dynamic_slice_in_dim(gate_up[:, j, :], h * 896, 768, 1)]
    slice x6 -> x5, local copies, waits for them, and re-layouts: 11.6 us -> 4.31 us  [the longest x2 1.79 us: per_device(): arrived += [g2, b1, b2, along_y(b1[:2], 1), along_y(b2[2:], -1)]]
    all_to_all x1, waiting for transfers between devices: 0.01 us -> 4.56 us  [per_device(): even = lax.all_to_all(even, ('x', 'c'), 0, 0, tiled=True)]
  transfers between devices with their start and end apart: 25 -> 20, of which waited for: 13 -> 12; matrix products, arithmetic and copies ran while one was open for 14% -> 5% of each run, Pallas kernels for 7% -> 10%
where the time goes in v2:
time: 199 us; the launch traced here: 197 us
  waiting for transfers between devices  71.2 us (36%)
  Pallas kernels  42 us (21%)
  starting transfers between devices  31.2 us (16%)
  blocking collectives  25 us (13%)
  between operations  14.3 us (7%)
  local copies, waits for them, and re-layouts  7.77 us (4%)
  other arithmetic  5.76 us (3%)
    all_to_all x1, waiting for transfers between devices, per_device(): got = lax.all_to_all(terms[q], ('zl', 'y'), 0, 0, tiled=True)  32 us
    ppermute x16, waiting for transfers between devices, permute(): return lax.ppermute(value, axes, pairs)  30.5 us
    all_to_all x1, blocking collectives, per_device(): lax.all_to_all(mixed.reshape(16, 8 * RR, 1152), ('x', 'zh', 'c'), 0, 0, t...  25 us
    ppermute x16, starting transfers between devices, permute(): return lax.ppermute(value, axes, pairs)  22.3 us
    pallas_call x1, Pallas kernels, feed(): pl.pallas_call(feed_kernel, out_shape=jax.ShapeDtypeStruct((2 * CR, 1152)...  21 us
    pallas_call x1, Pallas kernels, front(): pl.pallas_call(front_kernel, out_shape=[jax.ShapeDtypeStruct((8, CR, DT),...  19.5 us
    all_to_all x1, starting transfers between devices, per_device(): got = lax.all_to_all(terms[q], ('zl', 'y'), 0, 0, tiled=True)  4.65 us
    all_to_all x1, waiting for transfers between devices, per_device(): even = lax.all_to_all(even, ('x', 'c'), 0, 0, tiled=True)  4.56 us
  transfers between devices with their start and end apart: 20, of which 12 were waited for; matrix products, arithmetic and copies ran while one was open for 5% of the time, Pallas kernels for 10%

profile of v2, /device:TPU:1, one launch (start us, length us, event | category | flops | bytes accessed | tf_op | source)
XLA Modules:
  0.0 197.3 jit_solution(11827763043655683964)
XLA Ops:
  7.2 0.0 all-gather.5.cloned.1.call-start
  7.2 1.8 copy.22
  9.0 1.3 broadcast_select_fusion
  10.3 0.0 all-gather.5.cloned.1.call-update
  10.3 0.0 copy-start.13
  10.3 0.0 copy-start
  10.4 0.0 copy-start.1
  10.4 0.0 copy-start.2
  10.4 0.9 fusion.6
  11.3 4.4 %collective-permute-start.1 = (bf16[2,160,896]{2,1,0:T(8,128)(2,1)S(1)}, bf16[2,160,896]{2,1,0:T(8,128)(2,1)S(1)}, u32[]{:S(2)}, u32[]{:S(2)}) collective-permute-start(bf16[2,160,896]{2,1,0:T(8,128)(2,1)S(1)} %get-tuple-element.24), channel_id=1, source_target_pairs={{0,16},{16,0},{1,17},{17,1},{2,18},{18,2},{3,19},{19,3},{4,20},{20... | collective-permute-start | bytes 1720328 | tf_op jit(solution)/shard_map/ppermute | solution.py:52
  15.7 0.1 dynamic_slice.3
  15.8 0.1 pad_add_fusion.1.len_ref
  15.9 19.5 %attend_project.1 = bf16[8,256,640]{2,1,0:T(8,128)(2,1)} custom-call(s32[9]{0:T(128)S(1)} %pad_add_fusion.1.len_ref, bf16[8,32,1024]{2,1,0:T(8,128)(2,1)S(1)} %copy-done, bf16[8,2,32,128]{3,2,1,0:T(8,128)(2,1)S(1)} %copy-done.2, bf16[256,640]{1,0:T(8,128)(2,1)S(1)} %copy-done.1, bf16[8,2,2048,128]{3,2,1,0:T(8,128)(2,1)} %cache_ref.1, bf16[1024,5120]{1,0:T(8,128)(2,1)} %ow_ref.1), custom_call_target="tpu_custom_call" | custom-call | tf_op jit(solution)/shard_map/attend_project/pallas_call | solution.py:159
  35.4 0.0 collective-permute-done.1
  35.4 4.7 %all-to-all-start = ((bf16[8,256,640]{2,1,0:T(8,128)(2,1)}), bf16[8,256,640]{2,1,0:T(8,128)(2,1)S(1)}, u32[]{:S(2)}, u32[]{:S(2)}) async-start(bf16[8,256,640]{2,1,0:T(8,128)(2,1)} %attend_project.1), calls=%async_computation | async-start | bytes 5242880 | tf_op jit(solution)/shard_map/all_to_all | solution.py:330
  40.1 0.0 collective-permute-start
  40.1 32.0 %all-to-all-done = bf16[8,256,640]{2,1,0:T(8,128)(2,1)S(1)} async-done(((bf16[8,256,640]{2,1,0:T(8,128)(2,1)}), bf16[8,256,640]{2,1,0:T(8,128)(2,1)S(1)}, u32[]{:S(2)}, u32[]{:S(2)}) %all-to-all-start) | async-done | bytes 2621472 | tf_op jit(solution)/shard_map/all_to_all | solution.py:330
  72.1 1.2 reduce_sum.22
  73.2 4.3 %all-to-all-start.1 = ((bf16[8,32,640]{2,1,0:T(8,128)(2,1)}), bf16[8,32,640]{2,1,0:T(8,128)(2,1)S(1)}, u32[]{:S(2)}, u32[]{:S(2)}) async-start(bf16[8,32,640]{2,1,0:T(8,128)(2,1)} %bitcast.5), calls=%async_computation.1 | async-start | bytes 655360 | tf_op jit(solution)/shard_map/all_to_all | solution.py:332
  77.5 2.6 %collective-permute-done = bf16[2,160,896]{2,1,0:T(8,128)(2,1)} collective-permute-done((bf16[2,160,896]{2,1,0:T(8,128)(2,1)}, bf16[2,160,896]{2,1,0:T(8,128)(2,1)}, u32[]{:S(2)}, u32[]{:S(2)}) %collective-permute-start) | collective-permute-done | bytes 573472 | tf_op jit(solution)/shard_map/ppermute | solution.py:52
  80.0 4.6 %all-to-all-done.1 = bf16[8,32,640]{2,1,0:T(8,128)(2,1)S(1)} async-done(((bf16[8,32,640]{2,1,0:T(8,128)(2,1)}), bf16[8,32,640]{2,1,0:T(8,128)(2,1)S(1)}, u32[]{:S(2)}, u32[]{:S(2)}) %all-to-all-start.1) | async-done | bytes 327712 | tf_op jit(solution)/shard_map/all_to_all | solution.py:332
  84.6 2.2 %pad_maximum_fusion = bf16[2,320,896]{2,1,0:T(8,128)(2,1)} fusion(bf16[2,160,896]{2,1,0:T(8,128)(2,1)} %collective-permute-done, bf16[2,160,896]{2,1,0:T(8,128)(2,1)S(1)} %collective-permute-done.1), kind=kLoop, calls=%fused_computation.1 | loop fusion | flops 2293760 | bytes 2293760 | tf_op jit(solution)/shard_map/concatenate | solution.py:335
  86.8 0.0 all-gather.7.cloned.1.call-update
  86.8 0.1 slice_bitcast_fusion
  86.9 0.1 collective-permute-start.6
  86.9 1.5 collective-permute-start.5
  88.4 0.3 collective-permute-start.7
  88.7 8.2 %collective-permute-start.3 = (bf16[128,640]{1,0:T(8,128)(2,1)S(1)}, bf16[128,640]{1,0:T(8,128)(2,1)S(1)}, u32[]{:S(2)}, u32[]{:S(2)}) collective-permute-start(bf16[128,640]{1,0:T(8,128)(2,1)S(1)} %get-tuple-element.29), channel_id=1, source_target_pairs={{0,3},{1,0},{2,1},{3,2},{4,7},{5,4},{6,5},{7,6},{8,11},{9,8},{10,9... | collective-permute-start | bytes 491528 | tf_op jit(solution)/shard_map/ppermute | solution.py:52
  96.9 0.0 collective-permute-start.2
  96.9 0.0 collective-permute-done.6
  96.9 1.2 collective-permute-start.4
  98.1 0.0 copy-start.14
  98.1 0.1 pad_maximum_fusion.2.refs_5_
  98.2 0.9 collective-permute-done.3
  99.2 7.5 %collective-permute-done.2 = bf16[128,640]{1,0:T(8,128)(2,1)S(1)} collective-permute-done((bf16[128,640]{1,0:T(8,128)(2,1)S(1)}, bf16[128,640]{1,0:T(8,128)(2,1)S(1)}, u32[]{:S(2)}, u32[]{:S(2)}) %collective-permute-start.2) | collective-permute-done | bytes 163872 | tf_op jit(solution)/shard_map/ppermute | solution.py:52
  106.7 0.1 pad_maximum_fusion.1.refs_0_
  106.8 0.0 copy-start.4
  106.8 2.2 %collective-permute-start.9 = (bf16[4,128,640]{2,1,0:T(8,128)(2,1)S(1)}, bf16[4,128,640]{2,1,0:T(8,128)(2,1)S(1)}, u32[]{:S(2)}, u32[]{:S(2)}) collective-permute-start(bf16[4,128,640]{2,1,0:T(8,128)(2,1)S(1)} %pad_maximum_fusion.1.refs_0_), channel_id=1, source_target_pairs={{0,20},{4,0},{16,4},{20,16},{1,21},{5,1},{17,5},{21,17},{2,22},{6,... | collective-permute-start | bytes 1966088 | tf_op jit(solution)/shard_map/ppermute | solution.py:52
  108.9 0.0 collective-permute-start.8
  108.9 0.0 collective-permute-start.11
  108.9 1.5 collective-permute-start.10
  110.4 0.6 reshape.118.gain_ref
  111.0 0.1 select_reduce_fusion
  111.2 10.4 %collective-permute-done.9.refs_2_ = bf16[4,128,640]{2,1,0:T(8,128)(2,1)S(1)} collective-permute-done((bf16[4,128,640]{2,1,0:T(8,128)(2,1)S(1)}, bf16[4,128,640]{2,1,0:T(8,128)(2,1)S(1)}, u32[]{:S(2)}, u32[]{:S(2)}) %collective-permute-start.9) | collective-permute-done | bytes 655392 | tf_op jit(solution)/shard_map/ppermute | solution.py:52
  121.6 3.0 %collective-permute-done.8.refs_1_ = bf16[4,128,640]{2,1,0:T(8,128)(2,1)S(1)} collective-permute-done((bf16[4,128,640]{2,1,0:T(8,128)(2,1)S(1)}, bf16[4,128,640]{2,1,0:T(8,128)(2,1)S(1)}, u32[]{:S(2)}, u32[]{:S(2)}) %collective-permute-start.8) | collective-permute-done | bytes 655392 | tf_op jit(solution)/shard_map/ppermute | solution.py:52
  124.6 0.0 collective-permute-done.11.refs_7_
  124.6 0.8 slice.36
  125.5 0.8 slice.37
  126.3 1.8 slice.38
  128.1 0.1 collective-permute-start.15
  128.2 1.5 collective-permute-start.14
  129.6 1.3 collective-permute-start.13
  131.0 0.1 collective-permute-start.12
  131.1 0.1 iota_add_fusion
  131.2 0.8 add.115.src_ref
  132.0 0.7 pad_add_fusion.pos_ref
  132.7 2.0 %collective-permute-done.15.refs_9_ = bf16[2,128,640]{2,1,0:T(8,128)(2,1)S(1)} collective-permute-done((bf16[2,128,640]{2,1,0:T(8,128)(2,1)S(1)}, bf16[2,128,640]{2,1,0:T(8,128)(2,1)S(1)}, u32[]{:S(2)}, u32[]{:S(2)}) %collective-permute-start.15) | collective-permute-done | bytes 327712 | tf_op jit(solution)/shard_map/ppermute | solution.py:52
  134.7 1.5 collective-permute-done.14.refs_8_
  136.1 0.1 collective-permute-done.13.refs_4_
  136.2 2.5 %collective-permute-done.12.refs_3_ = bf16[2,128,640]{2,1,0:T(8,128)(2,1)S(1)} collective-permute-done((bf16[2,128,640]{2,1,0:T(8,128)(2,1)}, bf16[2,128,640]{2,1,0:T(8,128)(2,1)S(1)}, u32[]{:S(2)}, u32[]{:S(2)}) %collective-permute-start.12) | collective-permute-done | bytes 327712 | tf_op jit(solution)/shard_map/ppermute | solution.py:52
  138.7 4.1 %all-gather.7.cloned.1.call-done = bf16[16,320,896]{2,1,0:T(8,128)(2,1)} async-done(((bf16[2,320,896]{2,1,0:T(8,128)(2,1)}), bf16[16,320,896]{2,1,0:T(8,128)(2,1)}) %all-gather.7.cloned.1.call-update) | async-done | bytes 9175056 | tf_op jit(solution)/shard_map/all_gather | solution.py:336
  142.9 21.0 %feed_forward.1 = bf16[512,1152]{1,0:T(8,128)(2,1)} custom-call(s32[4]{0:T(128)} %pad_add_fusion.pos_ref, s32[16]{0:T(128)} %block_ref.1, s32[512,1]{1,0:T(8,128)} %add.115.src_ref, bf16[1,5120]{1,0:T(2,128)(2,1)} %reshape.118.gain_ref, bf16[4,128,640]{2,1,0:T(8,128)(2,1)} %copy-done.4, bf16[4,128,640]{2,1,0:T(8,128)(2,1)} %copy-done.6, ...), custom_call_target="tpu_custom_call" | custom-call | tf_op jit(solution)/shard_map/feed_forward/pallas_call | solution.py:255
  163.9 25.0 %all_to_all.22.refs_0_ = bf16[16,32,1152]{2,1,0:T(8,128)(2,1)S(1)} all-to-all(bf16[16,32,1152]{2,1,0:T(8,128)(2,1)} %bitcast.25), channel_id=1, replica_groups=mesh['x'=4,'zh'=2,'c'=2,'zl'=2,'y'=4] {'x','zh','c'}, dimensions={0} | all-to-all | bytes 2359296 | tf_op jit(solution)/shard_map/all_to_all | solution.py:346
  188.9 1.5 finish.1
  (32 shorter events, 0.1 us)
Async XLA Ops:
  7.2 131.6 %all-gather.5.cloned.1.call-start = ((), (), s32[]{:S(2)}) async-start(), calls=%async_computation.3 | async-start | bytes 10321920 | tf_op jit(solution)/shard_map/all_gather | solution.py:311
  10.3 5.4 %copy-start.13 = (s32[128]{0:T(128)S(1)}, s32[128]{0:T(128)}, u32[]{:S(2)}) copy-start(s32[128]{0:T(128)} %param.14) | copy-start | bytes 1540
  10.3 5.5 %copy-start = (bf16[8,32,1024]{2,1,0:T(8,128)(2,1)S(1)}, bf16[8,32,1024]{2,1,0:T(8,128)(2,1)}, u32[]{:S(2)}) copy-start(bf16[8,32,1024]{2,1,0:T(8,128)(2,1)} %q_ref.1) | copy-start | bytes 1572868
  10.4 5.5 %copy-start.1 = (bf16[256,640]{1,0:T(8,128)(2,1)S(1)}, bf16[256,640]{1,0:T(8,128)(2,1)}, u32[]{:S(2)}) copy-start(bf16[256,640]{1,0:T(8,128)(2,1)} %res_ref.1) | copy-start | bytes 983044
  10.4 5.5 %copy-start.2 = (bf16[8,2,32,128]{3,2,1,0:T(8,128)(2,1)S(1)}, bf16[8,2,32,128]{3,2,1,0:T(8,128)(2,1)}, u32[]{:S(2)}) copy-start(bf16[8,2,32,128]{3,2,1,0:T(8,128)(2,1)} %fresh_ref.1) | copy-start | bytes 393220
  11.3 24.1 %collective-permute-start.1 = (bf16[2,160,896]{2,1,0:T(8,128)(2,1)S(1)}, bf16[2,160,896]{2,1,0:T(8,128)(2,1)S(1)}, u32[]{:S(2)}, u32[]{:S(2)}) collective-permute-start(bf16[2,160,896]{2,1,0:T(8,128)(2,1)S(1)} %get-tuple-element.24), channel_id=1, source_target_pairs={{0,16},{16,0},{1,17},{17,1},{2,18},{18,2},{3,19},{19,3},{4,20},{20... | collective-permute-start | bytes 1720328 | tf_op jit(solution)/shard_map/ppermute | solution.py:52
  35.4 36.6 %all-to-all-start = ((bf16[8,256,640]{2,1,0:T(8,128)(2,1)}), bf16[8,256,640]{2,1,0:T(8,128)(2,1)S(1)}, u32[]{:S(2)}, u32[]{:S(2)}) async-start(bf16[8,256,640]{2,1,0:T(8,128)(2,1)} %attend_project.1), calls=%async_computation | async-start | bytes 5242880 | tf_op jit(solution)/shard_map/all_to_all | solution.py:330
  40.1 40.0 %collective-permute-start = (bf16[2,160,896]{2,1,0:T(8,128)(2,1)}, bf16[2,160,896]{2,1,0:T(8,128)(2,1)}, u32[]{:S(2)}, u32[]{:S(2)}) collective-permute-start(bf16[2,160,896]{2,1,0:T(8,128)(2,1)} %get-tuple-element.25), channel_id=1, source_target_pairs={{0,16},{16,0},{1,17},{17,1},{2,18},{18,2},{3,19},{19,3},{4,20},{20... | collective-permute-start | bytes 1720328 | tf_op jit(solution)/shard_map/ppermute | solution.py:52
  73.2 11.4 %all-to-all-start.1 = ((bf16[8,32,640]{2,1,0:T(8,128)(2,1)}), bf16[8,32,640]{2,1,0:T(8,128)(2,1)S(1)}, u32[]{:S(2)}, u32[]{:S(2)}) async-start(bf16[8,32,640]{2,1,0:T(8,128)(2,1)} %bitcast.5), calls=%async_computation.1 | async-start | bytes 655360 | tf_op jit(solution)/shard_map/all_to_all | solution.py:332
  77.5 65.4 %all-gather.7.cloned.1.call-start = ((), (), s32[]{:S(2)}) async-start(), calls=%async_computation.4 | async-start | bytes 10321920 | tf_op jit(solution)/shard_map/all_gather | solution.py:336
  86.9 10.1 %collective-permute-start.6 = (bf16[128,640]{1,0:T(8,128)(2,1)S(1)}, bf16[128,640]{1,0:T(8,128)(2,1)S(1)}, u32[]{:S(2)}, u32[]{:S(2)}) collective-permute-start(bf16[128,640]{1,0:T(8,128)(2,1)S(1)} %get-tuple-element.28), channel_id=1, source_target_pairs={{0,20},{4,0},{16,4},{20,16},{1,21},{5,1},{17,5},{21,17},{2,22},{6,... | collective-permute-start | bytes 491528 | tf_op jit(solution)/shard_map/ppermute | solution.py:52
  86.9 11.2 %collective-permute-start.5 = (bf16[128,640]{1,0:T(8,128)(2,1)S(1)}, bf16[128,640]{1,0:T(8,128)(2,1)S(1)}, u32[]{:S(2)}, u32[]{:S(2)}) collective-permute-start(bf16[128,640]{1,0:T(8,128)(2,1)S(1)} %get-tuple-element.28), channel_id=1, source_target_pairs={{0,4},{4,16},{16,20},{20,0},{1,5},{5,17},{17,21},{21,1},{2,6},{6,1... | collective-permute-start | bytes 491528 | tf_op jit(solution)/shard_map/ppermute | solution.py:52
  88.4 9.7 %collective-permute-start.7 = (bf16[128,640]{1,0:T(8,128)(2,1)S(1)}, bf16[128,640]{1,0:T(8,128)(2,1)S(1)}, u32[]{:S(2)}, u32[]{:S(2)}) collective-permute-start(bf16[128,640]{1,0:T(8,128)(2,1)S(1)} %get-tuple-element.28), channel_id=1, source_target_pairs={{0,16},{4,20},{16,0},{20,4},{1,17},{5,21},{17,1},{21,5},{2,18},{6,... | collective-permute-start | bytes 491528 | tf_op jit(solution)/shard_map/ppermute | solution.py:52
  88.7 10.5 %collective-permute-start.3 = (bf16[128,640]{1,0:T(8,128)(2,1)S(1)}, bf16[128,640]{1,0:T(8,128)(2,1)S(1)}, u32[]{:S(2)}, u32[]{:S(2)}) collective-permute-start(bf16[128,640]{1,0:T(8,128)(2,1)S(1)} %get-tuple-element.29), channel_id=1, source_target_pairs={{0,3},{1,0},{2,1},{3,2},{4,7},{5,4},{6,5},{7,6},{8,11},{9,8},{10,9... | collective-permute-start | bytes 491528 | tf_op jit(solution)/shard_map/ppermute | solution.py:52
  96.9 9.7 %collective-permute-start.2 = (bf16[128,640]{1,0:T(8,128)(2,1)S(1)}, bf16[128,640]{1,0:T(8,128)(2,1)S(1)}, u32[]{:S(2)}, u32[]{:S(2)}) collective-permute-start(bf16[128,640]{1,0:T(8,128)(2,1)S(1)} %get-tuple-element.29), channel_id=1, source_target_pairs={{0,1},{1,2},{2,3},{3,0},{4,5},{5,6},{6,7},{7,4},{8,9},{9,10},{10,1... | collective-permute-start | bytes 491528 | tf_op jit(solution)/shard_map/ppermute | solution.py:52
  96.9 9.7 %collective-permute-start.4 = (bf16[128,640]{1,0:T(8,128)(2,1)S(1)}, bf16[128,640]{1,0:T(8,128)(2,1)S(1)}, u32[]{:S(2)}, u32[]{:S(2)}) collective-permute-start(bf16[128,640]{1,0:T(8,128)(2,1)S(1)} %get-tuple-element.29), channel_id=1, source_target_pairs={{0,2},{1,3},{2,0},{3,1},{4,6},{5,7},{6,4},{7,5},{8,10},{9,11},{10,... | collective-permute-start | bytes 491528 | tf_op jit(solution)/shard_map/ppermute | solution.py:52
  98.1 12.3 %copy-start.12 = (bf16[5120]{0:T(1024)(128)(2,1)S(1)}, bf16[5120]{0:T(1024)(128)(2,1)}, u32[]{:S(2)}) copy-start(bf16[5120]{0:T(1024)(128)(2,1)} %param.17) | copy-start | bytes 30724
  98.1 12.9 %copy-start.14 = (s32[128]{0:T(128)S(1)}, s32[128]{0:T(128)}, u32[]{:S(2)}) copy-start(s32[128]{0:T(128)} %param.15) | copy-start | bytes 1540
  98.2 28.0 %copy-start.3 = (bf16[4,128,640]{2,1,0:T(8,128)(2,1)}, bf16[4,128,640]{2,1,0:T(8,128)(2,1)S(1)}, u32[]{:S(2)}) copy-start(bf16[4,128,640]{2,1,0:T(8,128)(2,1)S(1)} %pad_maximum_fusion.2.refs_5_) | copy-start | bytes 1966084
  106.8 21.3 %copy-start.4 = (bf16[4,128,640]{2,1,0:T(8,128)(2,1)}, bf16[4,128,640]{2,1,0:T(8,128)(2,1)S(1)}, u32[]{:S(2)}) copy-start(bf16[4,128,640]{2,1,0:T(8,128)(2,1)S(1)} %pad_maximum_fusion.1.refs_0_) | copy-start | bytes 1966084
  106.8 14.8 %collective-permute-start.9 = (bf16[4,128,640]{2,1,0:T(8,128)(2,1)S(1)}, bf16[4,128,640]{2,1,0:T(8,128)(2,1)S(1)}, u32[]{:S(2)}, u32[]{:S(2)}) collective-permute-start(bf16[4,128,640]{2,1,0:T(8,128)(2,1)S(1)} %pad_maximum_fusion.1.refs_0_), channel_id=1, source_target_pairs={{0,20},{4,0},{16,4},{20,16},{1,21},{5,1},{17,5},{21,17},{2,22},{6,... | collective-permute-start | bytes 1966088 | tf_op jit(solution)/shard_map/ppermute | solution.py:52
  108.9 15.7 %collective-permute-start.8 = (bf16[4,128,640]{2,1,0:T(8,128)(2,1)S(1)}, bf16[4,128,640]{2,1,0:T(8,128)(2,1)S(1)}, u32[]{:S(2)}, u32[]{:S(2)}) collective-permute-start(bf16[4,128,640]{2,1,0:T(8,128)(2,1)S(1)} %pad_maximum_fusion.1.refs_0_), channel_id=1, source_target_pairs={{0,4},{4,16},{16,20},{20,0},{1,5},{5,17},{17,21},{21,1},{2,6},{6,1... | collective-permute-start | bytes 1966088 | tf_op jit(solution)/shard_map/ppermute | solution.py:52
  108.9 15.7 %collective-permute-start.11 = (bf16[4,128,640]{2,1,0:T(8,128)(2,1)S(1)}, bf16[4,128,640]{2,1,0:T(8,128)(2,1)S(1)}, u32[]{:S(2)}, u32[]{:S(2)}) collective-permute-start(bf16[4,128,640]{2,1,0:T(8,128)(2,1)S(1)} %pad_maximum_fusion.2.refs_5_), channel_id=1, source_target_pairs={{0,3},{1,0},{2,1},{3,2},{4,7},{5,4},{6,5},{7,6},{8,11},{9,8},{10,9... | collective-permute-start | bytes 1966088 | tf_op jit(solution)/shard_map/ppermute | solution.py:52
  108.9 15.7 %collective-permute-start.10 = (bf16[4,128,640]{2,1,0:T(8,128)(2,1)S(1)}, bf16[4,128,640]{2,1,0:T(8,128)(2,1)}, u32[]{:S(2)}, u32[]{:S(2)}) collective-permute-start(bf16[4,128,640]{2,1,0:T(8,128)(2,1)S(1)} %pad_maximum_fusion.2.refs_5_), channel_id=1, source_target_pairs={{0,1},{1,2},{2,3},{3,0},{4,5},{5,6},{6,7},{7,4},{8,9},{9,10},{10,1... | collective-permute-start | bytes 1966088 | tf_op jit(solution)/shard_map/ppermute | solution.py:52
  121.6 6.5 %copy-start.5 = (bf16[4,128,640]{2,1,0:T(8,128)(2,1)}, bf16[4,128,640]{2,1,0:T(8,128)(2,1)S(1)}, u32[]{:S(2)}) copy-start(bf16[4,128,640]{2,1,0:T(8,128)(2,1)S(1)} %collective-permute-done.9.refs_2_) | copy-start | bytes 1966084
  124.6 3.5 %copy-start.6 = (bf16[4,128,640]{2,1,0:T(8,128)(2,1)}, bf16[4,128,640]{2,1,0:T(8,128)(2,1)S(1)}, u32[]{:S(2)}) copy-start(bf16[4,128,640]{2,1,0:T(8,128)(2,1)S(1)} %collective-permute-done.8.refs_1_) | copy-start | bytes 1966084
  124.6 3.5 %copy-start.7 = (bf16[4,128,640]{2,1,0:T(8,128)(2,1)}, bf16[4,128,640]{2,1,0:T(8,128)(2,1)S(1)}, u32[]{:S(2)}) copy-start(bf16[4,128,640]{2,1,0:T(8,128)(2,1)S(1)} %collective-permute-done.11.refs_7_) | copy-start | bytes 1966084
  128.1 6.6 %collective-permute-start.15 = (bf16[2,128,640]{2,1,0:T(8,128)(2,1)S(1)}, bf16[2,128,640]{2,1,0:T(8,128)(2,1)S(1)}, u32[]{:S(2)}, u32[]{:S(2)}) collective-permute-start(bf16[2,128,640]{2,1,0:T(8,128)(2,1)S(1)} %slice.39), channel_id=1, source_target_pairs={{0,3},{1,0},{2,1},{3,2},{4,7},{5,4},{6,5},{7,6},{8,11},{9,8},{10,9... | collective-permute-start | bytes 983048 | tf_op jit(solution)/shard_map/ppermute | solution.py:52
  128.2 7.9 %collective-permute-start.14 = (bf16[2,128,640]{2,1,0:T(8,128)(2,1)}, bf16[2,128,640]{2,1,0:T(8,128)(2,1)S(1)}, u32[]{:S(2)}, u32[]{:S(2)}) collective-permute-start(bf16[2,128,640]{2,1,0:T(8,128)(2,1)} %slice.38), channel_id=1, source_target_pairs={{0,1},{1,2},{2,3},{3,0},{4,5},{5,6},{6,7},{7,4},{8,9},{9,10},{10,1... | collective-permute-start | bytes 983048 | tf_op jit(solution)/shard_map/ppermute | solution.py:52
  129.6 6.5 %collective-permute-start.13 = (bf16[2,128,640]{2,1,0:T(8,128)(2,1)}, bf16[2,128,640]{2,1,0:T(8,128)(2,1)S(1)}, u32[]{:S(2)}, u32[]{:S(2)}) collective-permute-start(bf16[2,128,640]{2,1,0:T(8,128)(2,1)} %slice.37), channel_id=1, source_target_pairs={{0,20},{4,0},{16,4},{20,16},{1,21},{5,1},{17,5},{21,17},{2,22},{6,... | collective-permute-start | bytes 983048 | tf_op jit(solution)/shard_map/ppermute | solution.py:52
  131.0 7.7 %collective-permute-start.12 = (bf16[2,128,640]{2,1,0:T(8,128)(2,1)}, bf16[2,128,640]{2,1,0:T(8,128)(2,1)S(1)}, u32[]{:S(2)}, u32[]{:S(2)}) collective-permute-start(bf16[2,128,640]{2,1,0:T(8,128)(2,1)} %slice.36), channel_id=1, source_target_pairs={{0,4},{4,16},{16,20},{20,0},{1,5},{5,17},{17,21},{21,1},{2,6},{6,1... | collective-permute-start | bytes 983048 | tf_op jit(solution)/shard_map/ppermute | solution.py:52
  134.7 8.2 %copy-start.8 = (bf16[2,128,640]{2,1,0:T(8,128)(2,1)}, bf16[2,128,640]{2,1,0:T(8,128)(2,1)S(1)}, u32[]{:S(2)}) copy-start(bf16[2,128,640]{2,1,0:T(8,128)(2,1)S(1)} %collective-permute-done.15.refs_9_) | copy-start | bytes 983044
  136.1 6.8 %copy-start.9 = (bf16[2,128,640]{2,1,0:T(8,128)(2,1)}, bf16[2,128,640]{2,1,0:T(8,128)(2,1)S(1)}, u32[]{:S(2)}) copy-start(bf16[2,128,640]{2,1,0:T(8,128)(2,1)S(1)} %collective-permute-done.14.refs_8_) | copy-start | bytes 983044
  136.2 6.7 %copy-start.10 = (bf16[2,128,640]{2,1,0:T(8,128)(2,1)}, bf16[2,128,640]{2,1,0:T(8,128)(2,1)S(1)}, u32[]{:S(2)}) copy-start(bf16[2,128,640]{2,1,0:T(8,128)(2,1)S(1)} %collective-permute-done.13.refs_4_) | copy-start | bytes 983044
  138.7 4.2 %copy-start.11 = (bf16[2,128,640]{2,1,0:T(8,128)(2,1)}, bf16[2,128,640]{2,1,0:T(8,128)(2,1)S(1)}, u32[]{:S(2)}) copy-start(bf16[2,128,640]{2,1,0:T(8,128)(2,1)S(1)} %collective-permute-done.12.refs_3_) | copy-start | bytes 983044
Sparse Core Ops, SparseCore 0:
  10.5 56.6 all-gather.4
  86.9 55.9 all-gather.6

commit v3 on v2

--- a/solution.py
+++ b/solution.py
@@ -173,17 +173,48 @@
     )(lengths, queries, fresh, residual, cache, out_weight)
 
 
-def feed_kernel(pos_ref, block_ref, src_ref, gain_ref, *refs):
-    arrived, (near_ref, far_ref, out_ref, act, normed, w, act_sem, w_sem) = refs[:10], refs[10:]
+def assemble_kernel(pos_ref, block_ref, near_ref, far_ref, w_ref, sem):
+    zh = pos_ref[0]
+    copies = []
+    for dz, source in enumerate((near_ref, far_ref)):
+        for i in range(8):
+            g = i // 2 * 4 + (zh + dz) % 2 * 2 + i % 2
+            row = pl.multiple_of(block_ref[g] * BLK, BLK)
+            copies.append(
+                pltpu.make_async_copy(
+                    source.at[i], w_ref.at[:, pl.ds(row, BLK), :], sem.at[dz * 8 + i]
+                )
+            )
+    for copy in copies:
+        copy.start()
+    for copy in copies:
+        copy.wait()
+
+
+def assemble(pos, block_of, near, far):
+    return pl.pallas_call(
+        assemble_kernel,
+        out_shape=pltpu.VMEM((2, D, NH), BF),
+        in_specs=[SM, SM, ANY, ANY],
+        out_specs=VM,
+        scratch_shapes=[pltpu.SemaphoreType.DMA((16,))],
+        compiler_params=pltpu.CompilerParams(vmem_limit_bytes=2**20),
+        name="assemble_weights",
+    )(pos, block_of, near, far)
+
+
+def feed_kernel(pos_ref, src_ref, gain_ref, w, *refs):
+    arrived, (out_ref, act, normed, act_sem) = refs[:16], refs[16:]
     zh, tp, z, y = (pos_ref[i] for i in range(4))
     half = CR // 2
     steps = (0, 3, 1, 2)
     pieces = []
     for h in range(2):
-        own, one, two, low, high = arrived[h * 5 : h * 5 + 5]
-        blocks = [(own, j, 0, j) for j in range(4)]
-        blocks += [(one, j, 3, j) for j in range(4)] + [(two, j, 1, j) for j in range(4)]
-        blocks += [(low, j, 2, j) for j in range(2)] + [(high, j, 2, j + 2) for j in range(2)]
+        group = arrived[h * 8 : h * 8 + 8]
+        offsets = (0, 0, 3, 3, 1, 1, 2, 2)
+        blocks = [
+            (ref, k, offsets[n], n % 2 * 2 + k) for n, ref in enumerate(group) for k in range(2)
+        ]
         for n, (ref, at, outer, j) in enumerate(blocks):
             dz, dy = (outer, steps[j]) if h == 0 else (steps[j], outer)
             zz = (z + dz) % 4
@@ -198,41 +229,15 @@
         copy.start()
 
     tiles = ((0, 256), (256, 256), (512, 256), (768, 128))
-
-    def weights(n):
-        at, size = tiles[n]
-        copies = []
-        for dz, source in enumerate((near_ref, far_ref)):
-            for i in range(8):
-                g = i // 2 * 4 + (zh + dz) % 2 * 2 + i % 2
-                row = pl.multiple_of(block_ref[g] * BLK, BLK)
-                copies.append(
-                    pltpu.make_async_copy(
-                        source.at[i, :, :, pl.ds(at, size)],
-                        w.at[:, pl.ds(row, BLK), pl.ds(at, size)],
-                        w_sem.at[n, dz * 8 + i],
-                    )
-                )
-        return copies
-
-    for copy in weights(0):
-        copy.start()
     for copy in pieces:
         copy.wait()
-    for copy in weights(1):
-        copy.start()
     gain = gain_ref[...].astype(F32)
     for r in range(0, 2 * CR, 64):
         rows = act[r : r + 64, :].astype(F32)
         inverse = lax.rsqrt(jnp.sum(rows * rows, axis=1, keepdims=True) / D + EPS)
         normed[r : r + 64, :] = (rows * inverse * gain).astype(BF)
     lhs = normed[...]
-    for n, (at, size) in enumerate(tiles):
-        for copy in weights(n):
-            copy.wait()
-        if n + 2 < len(tiles):
-            for copy in weights(n + 2):
-                copy.start()
+    for at, size in tiles:
         g = jnp.dot(lhs, w[0, :, at : at + size], preferred_element_type=F32)
         u = jnp.dot(lhs, w[1, :, at : at + size], preferred_element_type=F32)
         out_ref[:, at : at + size] = (g / (1 + jnp.exp(-g)) * u).astype(BF)
@@ -251,22 +256,20 @@
     out_ref[...] = jnp.dot(hot, out_ref[...], preferred_element_type=F32).astype(BF)
 
 
-def feed(pos, block_of, src, gain, arrived, near, far):
+def feed(pos, src, gain, w, arrived):
     return pl.pallas_call(
         feed_kernel,
         out_shape=jax.ShapeDtypeStruct((2 * CR, 1152), BF),
-        in_specs=[SM, SM, VM, VM] + [ANY] * 12,
+        in_specs=[SM, VM, VM, VM] + [ANY] * 16,
         out_specs=VM,
         scratch_shapes=[
             pltpu.VMEM((2 * CR, D), BF),
             pltpu.VMEM((2 * CR, D), BF),
-            pltpu.VMEM((2, D, NH), BF),
             pltpu.SemaphoreType.DMA((32,)),
-            pltpu.SemaphoreType.DMA((4, 16)),
         ],
-        compiler_params=pltpu.CompilerParams(vmem_limit_bytes=56 * 2**20),
+        compiler_params=pltpu.CompilerParams(vmem_limit_bytes=28 * 2**20),
         name="feed_forward",
-    )(pos, block_of, src, gain, *arrived, near, far)
+    )(pos, src, gain, pltpu.with_memory_space_constraint(w, pltpu.VMEM), *arrived)
 
 
 def finish_kernel(*refs):
@@ -309,7 +312,7 @@
     own = jnp.where(zh == 0, left, right)
     other = jnp.where(zh == 0, right, left)
     near = lax.all_gather(own, ("x", "c"), axis=0)
-    lower, upper = swap(other[:, : BLK // 2], "zh"), swap(other[:, BLK // 2 :], "zh")
+    lower, upper = swap(other[:, :224], "zh"), swap(other[:, 224:], "zh")
 
     own_lengths = lax.dynamic_slice_in_dim(lengths, group * SEQS, SEQS, 0)
     scalars = jnp.concatenate([own_lengths, pos[1:2]])
@@ -329,20 +332,24 @@
     for q in range(NC):
         got = lax.all_to_all(terms[q], ("zl", "y"), 0, 0, tiled=True)
         even = jnp.sum(got.astype(F32), axis=0).astype(BF)
-        even = lax.all_to_all(even, ("x", "c"), 0, 0, tiled=True)
         if q == 0:
             upper, even = lax.optimization_barrier((upper, even))
             other = jnp.concatenate([lower, upper], axis=1)
             far = lax.all_gather(other, ("x", "c"), axis=0)
+            w = assemble(pos, block_of, near, far)
+        even = lax.all_to_all(even, ("x", "c"), 0, 0, tiled=True)
         h1, h2 = even[: CR // 2], even[CR // 2 :]
-        g1 = jnp.stack([h1, along_y(h1, 1), along_y(h1, -1), along_y(h1, 2)])
-        g2 = jnp.stack([h2, along_z(h2, 1), along_z(h2, -1), along_z(h2, 2)])
-        g1, g2 = lax.optimization_barrier((g1, g2))
-        a1, a2, b1, b2 = along_z(g1, 1), along_z(g1, -1), along_y(g2, 1), along_y(g2, -1)
-        a1, a2, b1, b2 = lax.optimization_barrier((a1, a2, b1, b2))
-        arrived = [g1, a1, a2, along_z(a1[:2], 1), along_z(a2[2:], -1)]
-        arrived += [g2, b1, b2, along_y(b1[:2], 1), along_y(b2[2:], -1)]
-        mixed = feed(pos, block_of, src, gain, arrived, near, far)
+        p1 = [h1, along_y(h1, 1), along_y(h1, -1), along_y(h1, 2)]
+        p2 = [h2, along_z(h2, 1), along_z(h2, -1), along_z(h2, 2)]
+        stacks = [jnp.stack(p[k : k + 2]) for p in (p1, p2) for k in (0, 2)]
+        lo1, hi1, lo2, hi2 = lax.optimization_barrier(stacks)
+        early = [along_z(lo1, 1), along_z(hi1, -1), along_y(lo2, 1), along_y(hi2, -1)]
+        late = [along_z(hi1, 1), along_z(lo1, -1), along_y(hi2, 1), along_y(lo2, -1)]
+        early = lax.optimization_barrier(early)
+        on = [along_z(early[0], 1), along_z(early[1], -1), along_y(early[2], 1), along_y(early[3], -1)]
+        arrived = [lo1, hi1, early[0], late[0], late[1], early[1], on[0], on[1]]
+        arrived += [lo2, hi2, early[2], late[2], late[3], early[3], on[2], on[3]]
+        mixed = feed(pos, src, gain, w, arrived)
         parts.append(lax.all_to_all(mixed.reshape(16, 8 * RR, 1152), ("x", "zh", "c"), 0, 0, tiled=True))
     return finish(parts)
 

time: 199 us -> 199 us (level)
  waiting for transfers between devices: 71.2 us -> 49 us
  blocking collectives: 25 us -> 41.7 us
  local copies, waits for them, and re-layouts: 7.77 us -> 14.3 us
  starting transfers between devices: 31.2 us -> 35.4 us
  Pallas kernels: 42 us -> 38.4 us
    all_to_all x0 -> x1, blocking collectives: none -> 14.2 us  [per_device(): even = lax.all_to_all(even, ('x', 'c'), 0, 0, tiled=True)]
    ppermute x16 -> x20, waiting for transfers between devices: 30.5 us -> 21.3 us  [permute(): return lax.ppermute(value, axes, pairs)]
    ppermute x16 -> x20, starting transfers between devices: 22.3 us -> 30.6 us  [permute(): return lax.ppermute(value, axes, pairs)]
    unnamed x31 -> x25, local copies, waits for them, and re-layouts: 1.89 us -> 9.95 us
    pallas_call x1, Pallas kernels: 21 us -> 16.3 us  [feed(): pl.pallas_call(feed_kernel, out_shape=jax.ShapeDtypeStruct((2 * CR, 1152)...]
    all_to_all x1 -> x0, waiting for transfers between devices: 4.56 us -> none  [per_device(): even = lax.all_to_all(even, ('x', 'c'), 0, 0, tiled=True)]
    all_to_all x1, waiting for transfers between devices: 32 us -> 27.7 us  [per_device(): got = lax.all_to_all(terms[q], ('zl', 'y'), 0, 0, tiled=True)]
    all_to_all x1 -> x0, starting transfers between devices: 4.25 us -> none  [per_device(): even = lax.all_to_all(even, ('x', 'c'), 0, 0, tiled=True)]
  transfers between devices with their start and end apart: 20 -> 23, of which waited for: 12 -> 9; matrix products, arithmetic and copies ran while one was open for 5% -> 4% of each run, Pallas kernels for 10% -> 10%
where the time goes in v3:
time: 199 us; the launch traced here: 198 us
  waiting for transfers between devices  49 us (25%)
  blocking collectives  41.7 us (21%)
  Pallas kernels  38.4 us (19%)
  starting transfers between devices  35.4 us (18%)
  local copies, waits for them, and re-layouts  14.3 us (7%)
  between operations  14.3 us (7%)
  other arithmetic  5.21 us (3%)
    ppermute x20, starting transfers between devices, permute(): return lax.ppermute(value, axes, pairs)  30.6 us
    all_to_all x1, waiting for transfers between devices, per_device(): got = lax.all_to_all(terms[q], ('zl', 'y'), 0, 0, tiled=True)  27.7 us
    all_to_all x1, blocking collectives, per_device(): lax.all_to_all(mixed.reshape(16, 8 * RR, 1152), ('x', 'zh', 'c'), 0, 0, t...  27.5 us
    ppermute x20, waiting for transfers between devices, permute(): return lax.ppermute(value, axes, pairs)  21.3 us
    pallas_call x1, Pallas kernels, front(): pl.pallas_call(front_kernel, out_shape=[jax.ShapeDtypeStruct((8, CR, DT),...  17.5 us
    pallas_call x1, Pallas kernels, feed(): pl.pallas_call(feed_kernel, out_shape=jax.ShapeDtypeStruct((2 * CR, 1152)...  16.3 us
    all_to_all x1, blocking collectives, per_device(): even = lax.all_to_all(even, ('x', 'c'), 0, 0, tiled=True)  14.2 us
    unnamed x25, local copies, waits for them, and re-layouts  9.95 us
  transfers between devices with their start and end apart: 23, of which 9 were waited for; matrix products, arithmetic and copies ran while one was open for 4% of the time, Pallas kernels for 10%

profile of v3, /device:TPU:1, one launch (start us, length us, event | category | flops | bytes accessed | tf_op | source)
XLA Modules:
  0.0 198.3 jit_solution(15889076288332079195)
XLA Ops:
  7.2 0.0 all-gather.5.cloned.1.call-start
  7.2 1.8 copy.22
  9.0 1.3 broadcast_select_fusion
  10.3 0.0 copy-start.4
  10.3 0.0 all-gather.5.cloned.1.call-update
  10.4 0.9 slice.34
  11.3 4.4 %collective-permute-start = (bf16[2,224,896]{2,1,0:T(8,128)(2,1)}, bf16[2,224,896]{2,1,0:T(8,128)(2,1)S(1)}, u32[]{:S(2)}, u32[]{:S(2)}) collective-permute-start(bf16[2,224,896]{2,1,0:T(8,128)(2,1)} %slice.34), channel_id=1, source_target_pairs={{0,16},{16,0},{1,17},{17,1},{2,18},{18,2},{3,19},{19,3},{4,20},{20... | collective-permute-start | bytes 2408456 | tf_op jit(solution)/shard_map/ppermute | solution.py:52
  15.7 0.1 dynamic_slice.3
  15.8 0.1 pad_add_fusion.1.len_ref
  15.9 17.5 %attend_project.1 = bf16[8,256,640]{2,1,0:T(8,128)(2,1)} custom-call(s32[9]{0:T(128)S(1)} %pad_add_fusion.1.len_ref, bf16[8,32,1024]{2,1,0:T(8,128)(2,1)S(1)} %copy-done.2, bf16[8,2,32,128]{3,2,1,0:T(8,128)(2,1)S(1)} %copy-done.4, bf16[256,640]{1,0:T(8,128)(2,1)S(1)} %copy-done.3, bf16[8,2,2048,128]{3,2,1,0:T(8,128)(2,1)} %cache_ref.1, bf16[1024,5120]{1,0:T(8,128)(2,1)} %ow_ref.1), custom_call_target="tpu_custom_call" | custom-call | tf_op jit(solution)/shard_map/attend_project/pallas_call | solution.py:159
  33.5 0.1 collective-permute-done
  33.6 0.9 copy-done.8
  34.4 4.7 %all-to-all-start = ((bf16[8,256,640]{2,1,0:T(8,128)(2,1)}), bf16[8,256,640]{2,1,0:T(8,128)(2,1)S(1)}, u32[]{:S(2)}, u32[]{:S(2)}) async-start(bf16[8,256,640]{2,1,0:T(8,128)(2,1)} %attend_project.1), calls=%async_computation | async-start | bytes 5242880 | tf_op jit(solution)/shard_map/all_to_all | solution.py:333
  39.2 0.0 all-gather.7.cloned.1.call-start
  39.2 1.7 slice.35
  40.9 3.2 %collective-permute-start.1 = (bf16[2,96,896]{2,1,0:T(8,128)(2,1)}, bf16[2,96,896]{2,1,0:T(8,128)(2,1)S(1)}, u32[]{:S(2)}, u32[]{:S(2)}) collective-permute-start(bf16[2,96,896]{2,1,0:T(8,128)(2,1)} %slice.35), channel_id=1, source_target_pairs={{0,16},{16,0},{1,17},{17,1},{2,18},{18,2},{3,19},{19,3},{4,20},{20... | collective-permute-start | bytes 1032200 | tf_op jit(solution)/shard_map/ppermute | solution.py:52
  44.1 27.7 %all-to-all-done = bf16[8,256,640]{2,1,0:T(8,128)(2,1)S(1)} async-done(((bf16[8,256,640]{2,1,0:T(8,128)(2,1)}), bf16[8,256,640]{2,1,0:T(8,128)(2,1)S(1)}, u32[]{:S(2)}, u32[]{:S(2)}) %all-to-all-start) | async-done | bytes 2621472 | tf_op jit(solution)/shard_map/all_to_all | solution.py:333
  71.8 0.5 reduce_sum.22
  72.4 4.8 %collective-permute-done.1 = bf16[2,96,896]{2,1,0:T(8,128)(2,1)S(1)} collective-permute-done((bf16[2,96,896]{2,1,0:T(8,128)(2,1)}, bf16[2,96,896]{2,1,0:T(8,128)(2,1)S(1)}, u32[]{:S(2)}, u32[]{:S(2)}) %collective-permute-start.1) | collective-permute-done | bytes 344096 | tf_op jit(solution)/shard_map/ppermute | solution.py:52
  77.2 2.3 %pad_maximum_fusion = bf16[2,320,896]{2,1,0:T(8,128)(2,1)} fusion(bf16[2,96,896]{2,1,0:T(8,128)(2,1)S(1)} %collective-permute-done.1, bf16[2,224,896]{2,1,0:T(8,128)(2,1)} %copy-done.8), kind=kLoop, calls=%fused_computation.1 | loop fusion | flops 2293760 | bytes 2293760 | tf_op jit(solution)/shard_map/concatenate | solution.py:337
  79.5 0.0 all-gather.7.cloned.1.call-update
  79.5 0.0 copy-start.9
  79.5 0.0 copy-start.11
  79.5 0.0 copy-start.6
  79.5 14.2 %all_to_all.19 = bf16[8,32,640]{2,1,0:T(8,128)(2,1)S(1)} all-to-all(bf16[8,32,640]{2,1,0:T(8,128)(2,1)S(1)} %bitcast.25), channel_id=1, replica_groups=mesh['x'=4,'zh'=2,'c'=2,'zl'=2,'y'=4] {'x','c'}, dimensions={0} | all-to-all | bytes 655360 | tf_op jit(solution)/shard_map/all_to_all | solution.py:340
  93.8 2.8 %collective-permute-start.4 = (bf16[128,640]{1,0:T(8,128)(2,1)S(1)}, bf16[128,640]{1,0:T(8,128)(2,1)S(1)}, u32[]{:S(2)}, u32[]{:S(2)}) collective-permute-start(bf16[128,640]{1,0:T(8,128)(2,1)S(1)} %bitcast.30), channel_id=1, source_target_pairs={{0,2},{1,3},{2,0},{3,1},{4,6},{5,7},{6,4},{7,5},{8,10},{9,11},{10,... | collective-permute-start | bytes 491528 | tf_op jit(solution)/shard_map/ppermute | solution.py:52
  96.5 1.2 collective-permute-start.3
  97.7 0.3 collective-permute-start.2
  98.0 0.9 collective-permute-start.7
  98.9 2.5 %collective-permute-start.6 = (bf16[128,640]{1,0:T(8,128)(2,1)S(1)}, bf16[128,640]{1,0:T(8,128)(2,1)S(1)}, u32[]{:S(2)}, u32[]{:S(2)}) collective-permute-start(bf16[128,640]{1,0:T(8,128)(2,1)S(1)} %bitcast.27), channel_id=1, source_target_pairs={{0,20},{4,0},{16,4},{20,16},{1,21},{5,1},{17,5},{21,17},{2,22},{6,... | collective-permute-start | bytes 491528 | tf_op jit(solution)/shard_map/ppermute | solution.py:52
  101.4 0.0 collective-permute-done.4
  101.4 0.0 collective-permute-start.5
  101.4 3.6 %collective-permute-done.3 = bf16[128,640]{1,0:T(8,128)(2,1)S(1)} collective-permute-done((bf16[128,640]{1,0:T(8,128)(2,1)S(1)}, bf16[128,640]{1,0:T(8,128)(2,1)S(1)}, u32[]{:S(2)}, u32[]{:S(2)}) %collective-permute-start.3) | collective-permute-done | bytes 163872 | tf_op jit(solution)/shard_map/ppermute | solution.py:52
  105.0 0.0 collective-permute-done.2
  105.1 1.5 collective-permute-done.6
  106.6 2.0 collective-permute-done.5
  108.6 1.2 collective-permute-start.8
  109.8 1.6 collective-permute-start.9
  111.4 0.6 reshape.122.gain_ref
  112.0 0.2 collective-permute-start.13
  112.2 1.2 collective-permute-start.12
  113.4 2.1 %collective-permute-start.17 = (bf16[2,128,640]{2,1,0:T(8,128)(2,1)S(1)}, bf16[2,128,640]{2,1,0:T(8,128)(2,1)S(1)}, u32[]{:S(2)}, u32[]{:S(2)}) collective-permute-start(bf16[2,128,640]{2,1,0:T(8,128)(2,1)S(1)} %pad_maximum_fusion.3.refs_8_), channel_id=1, source_target_pairs={{0,3},{1,0},{2,1},{3,2},{4,7},{5,4},{6,5},{7,6},{8,11},{9,8},{10,9... | collective-permute-start | bytes 983048 | tf_op jit(solution)/shard_map/ppermute | solution.py:52
  115.5 2.0 collective-permute-done.8.refs_2_
  117.5 0.8 collective-permute-start.10
  118.3 1.9 collective-permute-start.11
  120.1 0.1 select_reduce_fusion
  120.3 4.7 %collective-permute-done.10.refs_10_ = bf16[2,128,640]{2,1,0:T(8,128)(2,1)S(1)} collective-permute-done((bf16[2,128,640]{2,1,0:T(8,128)(2,1)S(1)}, bf16[2,128,640]{2,1,0:T(8,128)(2,1)S(1)}, u32[]{:S(2)}, u32[]{:S(2)}) %collective-permute-start.10) | collective-permute-done | bytes 327712 | tf_op jit(solution)/shard_map/ppermute | solution.py:52
  125.0 2.6 %collective-permute-done.11.refs_13_ = bf16[2,128,640]{2,1,0:T(8,128)(2,1)} collective-permute-done((bf16[2,128,640]{2,1,0:T(8,128)(2,1)S(1)}, bf16[2,128,640]{2,1,0:T(8,128)(2,1)}, u32[]{:S(2)}, u32[]{:S(2)}) %collective-permute-start.11) | collective-permute-done | bytes 327712 | tf_op jit(solution)/shard_map/ppermute | solution.py:52
  127.6 0.8 collective-permute-start.14
  128.4 0.0 collective-permute-done.13.refs_4_
  128.4 1.8 collective-permute-start.15
  130.3 0.4 collective-permute-start.18
  130.7 3.4 %collective-permute-start.19 = (bf16[2,128,640]{2,1,0:T(8,128)(2,1)}, bf16[2,128,640]{2,1,0:T(8,128)(2,1)}, u32[]{:S(2)}, u32[]{:S(2)}) collective-permute-start(bf16[2,128,640]{2,1,0:T(8,128)(2,1)} %collective-permute-done.11.refs_13_), channel_id=1, source_target_pairs={{0,3},{1,0},{2,1},{3,2},{4,7},{5,4},{6,5},{7,6},{8,11},{9,8},{10,9... | collective-permute-start | bytes 983048 | tf_op jit(solution)/shard_map/ppermute | solution.py:52
  134.1 0.7 iota_add_fusion
  134.8 0.9 add.115.src_ref
  135.7 0.1 pad_add_fusion.pos_ref
  135.8 3.6 %copy-done = bf16[16,320,896]{2,1,0:T(8,128)(2,1)S(1)} copy-done((bf16[16,320,896]{2,1,0:T(8,128)(2,1)S(1)}, bf16[16,320,896]{2,1,0:T(8,128)(2,1)}, u32[]{:S(2)}) %copy-start) | copy-done | bytes 9175064
  139.4 3.6 %copy-done.1 = bf16[16,320,896]{2,1,0:T(8,128)(2,1)S(1)} copy-done((bf16[16,320,896]{2,1,0:T(8,128)(2,1)S(1)}, bf16[16,320,896]{2,1,0:T(8,128)(2,1)}, u32[]{:S(2)}) %copy-start.1) | copy-done | bytes 9175064
  143.0 3.0 %assemble_weights.1.w = bf16[2,5120,896]{2,1,0:T(8,128)(2,1)S(1)} custom-call(s32[4]{0:T(128)S(1)} %pad_add_fusion.pos_ref, s32[16]{0:T(128)S(1)} %copy-done.6, bf16[8,2,320,896]{3,2,1,0:T(8,128)(2,1)S(1)} %bitcast.21, bf16[8,2,320,896]{3,2,1,0:T(8,128)(2,1)S(1)} %bitcast.22), custom_call_target="tpu_custom_call" | custom-call | tf_op jit(solution)/shard_map/assemble_weights/pallas_call | solution.py:195
  146.1 0.0 collective-permute-done.16.refs_11_
  146.1 0.0 collective-permute-done.18.refs_14_
  146.1 16.3 %feed_forward.1 = bf16[512,1152]{1,0:T(8,128)(2,1)S(1)} custom-call(s32[4]{0:T(128)S(1)} %pad_add_fusion.pos_ref, s32[512,1]{1,0:T(8,128)S(1)} %add.115.src_ref, bf16[1,5120]{1,0:T(2,128)(2,1)S(1)} %copy-done.5, bf16[2,5120,896]{2,1,0:T(8,128)(2,1)S(1)} %assemble_weights.1.w, bf16[2,128,640]{2,1,0:T(8,128)(2,1)S(1)} %pad_maximum_fusion.1.refs_0_, ...), custom_call_target="tpu_custom_call" | custom-call | tf_op jit(solution)/shard_map/feed_forward/pallas_call | solution.py:260
  162.4 27.5 %all_to_all.20.refs_0_ = bf16[16,32,1152]{2,1,0:T(8,128)(2,1)S(1)} all-to-all(bf16[16,32,1152]{2,1,0:T(8,128)(2,1)S(1)} %bitcast.23), channel_id=1, replica_groups=mesh['x'=4,'zh'=2,'c'=2,'zl'=2,'y'=4] {'x','zh','c'}, dimensions={0} | all-to-all | bytes 2359296 | tf_op jit(solution)/shard_map/all_to_all | solution.py:353
  189.9 1.5 finish.1
  (33 shorter events, 0.3 us)
Async XLA Ops:
  7.2 128.6 %all-gather.5.cloned.1.call-start = ((), (), s32[]{:S(2)}) async-start(), calls=%async_computation.3 | async-start | bytes 10321920 | tf_op jit(solution)/shard_map/all_gather | solution.py:314
  10.3 23.1 %copy-start.7 = (bf16[2,320,896]{2,1,0:T(8,128)(2,1)}, bf16[2,320,896]{2,1,0:T(8,128)(2,1)S(1)}, u32[]{:S(2)}) copy-start(bf16[2,320,896]{2,1,0:T(8,128)(2,1)S(1)} %get-tuple-element.26) | copy-start | bytes 3440644
  10.3 5.4 %copy-start.10 = (s32[128]{0:T(128)S(1)}, s32[128]{0:T(128)}, u32[]{:S(2)}) copy-start(s32[128]{0:T(128)} %param.14) | copy-start | bytes 1540
  10.3 5.6 %copy-start.2 = (bf16[8,32,1024]{2,1,0:T(8,128)(2,1)S(1)}, bf16[8,32,1024]{2,1,0:T(8,128)(2,1)}, u32[]{:S(2)}) copy-start(bf16[8,32,1024]{2,1,0:T(8,128)(2,1)} %q_ref.1) | copy-start | bytes 1572868
  10.3 5.6 %copy-start.3 = (bf16[256,640]{1,0:T(8,128)(2,1)S(1)}, bf16[256,640]{1,0:T(8,128)(2,1)}, u32[]{:S(2)}) copy-start(bf16[256,640]{1,0:T(8,128)(2,1)} %res_ref.1) | copy-start | bytes 983044
  10.3 5.6 %copy-start.4 = (bf16[8,2,32,128]{3,2,1,0:T(8,128)(2,1)S(1)}, bf16[8,2,32,128]{3,2,1,0:T(8,128)(2,1)}, u32[]{:S(2)}) copy-start(bf16[8,2,32,128]{3,2,1,0:T(8,128)(2,1)} %fresh_ref.1) | copy-start | bytes 393220
  11.3 22.3 %collective-permute-start = (bf16[2,224,896]{2,1,0:T(8,128)(2,1)}, bf16[2,224,896]{2,1,0:T(8,128)(2,1)S(1)}, u32[]{:S(2)}, u32[]{:S(2)}) collective-permute-start(bf16[2,224,896]{2,1,0:T(8,128)(2,1)} %slice.34), channel_id=1, source_target_pairs={{0,16},{16,0},{1,17},{17,1},{2,18},{18,2},{3,19},{19,3},{4,20},{20... | collective-permute-start | bytes 2408456 | tf_op jit(solution)/shard_map/ppermute | solution.py:52
  33.6 0.9 copy-start.8
  34.4 37.4 %all-to-all-start = ((bf16[8,256,640]{2,1,0:T(8,128)(2,1)}), bf16[8,256,640]{2,1,0:T(8,128)(2,1)S(1)}, u32[]{:S(2)}, u32[]{:S(2)}) async-start(bf16[8,256,640]{2,1,0:T(8,128)(2,1)} %attend_project.1), calls=%async_computation | async-start | bytes 5242880 | tf_op jit(solution)/shard_map/all_to_all | solution.py:333
  39.2 96.7 %all-gather.7.cloned.1.call-start = ((), (), s32[]{:S(2)}) async-start(), calls=%async_computation.4 | async-start | bytes 10321920 | tf_op jit(solution)/shard_map/all_gather | solution.py:338
  40.9 36.2 %collective-permute-start.1 = (bf16[2,96,896]{2,1,0:T(8,128)(2,1)}, bf16[2,96,896]{2,1,0:T(8,128)(2,1)S(1)}, u32[]{:S(2)}, u32[]{:S(2)}) collective-permute-start(bf16[2,96,896]{2,1,0:T(8,128)(2,1)} %slice.35), channel_id=1, source_target_pairs={{0,16},{16,0},{1,17},{17,1},{2,18},{18,2},{3,19},{19,3},{4,20},{20... | collective-permute-start | bytes 1032200 | tf_op jit(solution)/shard_map/ppermute | solution.py:52
  79.5 31.9 %copy-start.9 = (bf16[5120]{0:T(1024)(128)(2,1)S(1)}, bf16[5120]{0:T(1024)(128)(2,1)}, u32[]{:S(2)}) copy-start(bf16[5120]{0:T(1024)(128)(2,1)} %param.17) | copy-start | bytes 30724
  79.5 40.6 %copy-start.11 = (s32[128]{0:T(128)S(1)}, s32[128]{0:T(128)}, u32[]{:S(2)}) copy-start(s32[128]{0:T(128)} %param.15) | copy-start | bytes 1540
  79.5 56.3 %copy-start.6 = (s32[16]{0:T(128)S(1)}, s32[16]{0:T(128)}, u32[]{:S(2)}) copy-start(s32[16]{0:T(128)} %block_ref.1) | copy-start | bytes 196
  93.8 7.6 %collective-permute-start.4 = (bf16[128,640]{1,0:T(8,128)(2,1)S(1)}, bf16[128,640]{1,0:T(8,128)(2,1)S(1)}, u32[]{:S(2)}, u32[]{:S(2)}) collective-permute-start(bf16[128,640]{1,0:T(8,128)(2,1)S(1)} %bitcast.30), channel_id=1, source_target_pairs={{0,2},{1,3},{2,0},{3,1},{4,6},{5,7},{6,4},{7,5},{8,10},{9,11},{10,... | collective-permute-start | bytes 491528 | tf_op jit(solution)/shard_map/ppermute | solution.py:52
  96.5 8.4 %collective-permute-start.3 = (bf16[128,640]{1,0:T(8,128)(2,1)S(1)}, bf16[128,640]{1,0:T(8,128)(2,1)S(1)}, u32[]{:S(2)}, u32[]{:S(2)}) collective-permute-start(bf16[128,640]{1,0:T(8,128)(2,1)S(1)} %bitcast.31), channel_id=1, source_target_pairs={{0,3},{1,0},{2,1},{3,2},{4,7},{5,4},{6,5},{7,6},{8,11},{9,8},{10,9... | collective-permute-start | bytes 491528 | tf_op jit(solution)/shard_map/ppermute | solution.py:52
  97.7 7.3 %collective-permute-start.2 = (bf16[128,640]{1,0:T(8,128)(2,1)S(1)}, bf16[128,640]{1,0:T(8,128)(2,1)S(1)}, u32[]{:S(2)}, u32[]{:S(2)}) collective-permute-start(bf16[128,640]{1,0:T(8,128)(2,1)S(1)} %bitcast.32), channel_id=1, source_target_pairs={{0,1},{1,2},{2,3},{3,0},{4,5},{5,6},{6,7},{7,4},{8,9},{9,10},{10,1... | collective-permute-start | bytes 491528 | tf_op jit(solution)/shard_map/ppermute | solution.py:52
  98.0 7.1 %collective-permute-start.7 = (bf16[128,640]{1,0:T(8,128)(2,1)S(1)}, bf16[128,640]{1,0:T(8,128)(2,1)S(1)}, u32[]{:S(2)}, u32[]{:S(2)}) collective-permute-start(bf16[128,640]{1,0:T(8,128)(2,1)S(1)} %bitcast.26), channel_id=1, source_target_pairs={{0,16},{4,20},{16,0},{20,4},{1,17},{5,21},{17,1},{21,5},{2,18},{6,... | collective-permute-start | bytes 491528 | tf_op jit(solution)/shard_map/ppermute | solution.py:52
  98.9 7.7 %collective-permute-start.6 = (bf16[128,640]{1,0:T(8,128)(2,1)S(1)}, bf16[128,640]{1,0:T(8,128)(2,1)S(1)}, u32[]{:S(2)}, u32[]{:S(2)}) collective-permute-start(bf16[128,640]{1,0:T(8,128)(2,1)S(1)} %bitcast.27), channel_id=1, source_target_pairs={{0,20},{4,0},{16,4},{20,16},{1,21},{5,1},{17,5},{21,17},{2,22},{6,... | collective-permute-start | bytes 491528 | tf_op jit(solution)/shard_map/ppermute | solution.py:52
  101.4 7.2 %collective-permute-start.5 = (bf16[128,640]{1,0:T(8,128)(2,1)S(1)}, bf16[128,640]{1,0:T(8,128)(2,1)S(1)}, u32[]{:S(2)}, u32[]{:S(2)}) collective-permute-start(bf16[128,640]{1,0:T(8,128)(2,1)S(1)} %bitcast.28), channel_id=1, source_target_pairs={{0,4},{4,16},{16,20},{20,0},{1,5},{5,17},{17,21},{21,1},{2,6},{6,1... | collective-permute-start | bytes 491528 | tf_op jit(solution)/shard_map/ppermute | solution.py:52
  108.6 8.9 %collective-permute-start.8 = (bf16[2,128,640]{2,1,0:T(8,128)(2,1)S(1)}, bf16[2,128,640]{2,1,0:T(8,128)(2,1)S(1)}, u32[]{:S(2)}, u32[]{:S(2)}) collective-permute-start(bf16[2,128,640]{2,1,0:T(8,128)(2,1)S(1)} %pad_maximum_fusion.1.refs_0_), channel_id=1, source_target_pairs={{0,4},{4,16},{16,20},{20,0},{1,5},{5,17},{17,21},{21,1},{2,6},{6,1... | collective-permute-start | bytes 983048 | tf_op jit(solution)/shard_map/ppermute | solution.py:52
  109.8 8.5 %collective-permute-start.9 = (bf16[2,128,640]{2,1,0:T(8,128)(2,1)S(1)}, bf16[2,128,640]{2,1,0:T(8,128)(2,1)S(1)}, u32[]{:S(2)}, u32[]{:S(2)}) collective-permute-start(bf16[2,128,640]{2,1,0:T(8,128)(2,1)S(1)} %pad_maximum_fusion.2.refs_1_), channel_id=1, source_target_pairs={{0,20},{4,0},{16,4},{20,16},{1,21},{5,1},{17,5},{21,17},{2,22},{6,... | collective-permute-start | bytes 983048 | tf_op jit(solution)/shard_map/ppermute | solution.py:52
  112.0 16.5 %collective-permute-start.13 = (bf16[2,128,640]{2,1,0:T(8,128)(2,1)S(1)}, bf16[2,128,640]{2,1,0:T(8,128)(2,1)S(1)}, u32[]{:S(2)}, u32[]{:S(2)}) collective-permute-start(bf16[2,128,640]{2,1,0:T(8,128)(2,1)S(1)} %pad_maximum_fusion.1.refs_0_), channel_id=1, source_target_pairs={{0,20},{4,0},{16,4},{20,16},{1,21},{5,1},{17,5},{21,17},{2,22},{6,... | collective-permute-start | bytes 983048 | tf_op jit(solution)/shard_map/ppermute | solution.py:52
  112.2 18.1 %collective-permute-start.12 = (bf16[2,128,640]{2,1,0:T(8,128)(2,1)S(1)}, bf16[2,128,640]{2,1,0:T(8,128)(2,1)S(1)}, u32[]{:S(2)}, u32[]{:S(2)}) collective-permute-start(bf16[2,128,640]{2,1,0:T(8,128)(2,1)S(1)} %pad_maximum_fusion.2.refs_1_), channel_id=1, source_target_pairs={{0,4},{4,16},{16,20},{20,0},{1,5},{5,17},{17,21},{21,1},{2,6},{6,1... | collective-permute-start | bytes 983048 | tf_op jit(solution)/shard_map/ppermute | solution.py:52
  113.4 17.2 %collective-permute-start.17 = (bf16[2,128,640]{2,1,0:T(8,128)(2,1)S(1)}, bf16[2,128,640]{2,1,0:T(8,128)(2,1)S(1)}, u32[]{:S(2)}, u32[]{:S(2)}) collective-permute-start(bf16[2,128,640]{2,1,0:T(8,128)(2,1)S(1)} %pad_maximum_fusion.3.refs_8_), channel_id=1, source_target_pairs={{0,3},{1,0},{2,1},{3,2},{4,7},{5,4},{6,5},{7,6},{8,11},{9,8},{10,9... | collective-permute-start | bytes 983048 | tf_op jit(solution)/shard_map/ppermute | solution.py:52
  117.5 7.5 %collective-permute-start.10 = (bf16[2,128,640]{2,1,0:T(8,128)(2,1)S(1)}, bf16[2,128,640]{2,1,0:T(8,128)(2,1)S(1)}, u32[]{:S(2)}, u32[]{:S(2)}) collective-permute-start(bf16[2,128,640]{2,1,0:T(8,128)(2,1)S(1)} %pad_maximum_fusion.3.refs_8_), channel_id=1, source_target_pairs={{0,1},{1,2},{2,3},{3,0},{4,5},{5,6},{6,7},{7,4},{8,9},{9,10},{10,1... | collective-permute-start | bytes 983048 | tf_op jit(solution)/shard_map/ppermute | solution.py:52
  118.3 9.3 %collective-permute-start.11 = (bf16[2,128,640]{2,1,0:T(8,128)(2,1)S(1)}, bf16[2,128,640]{2,1,0:T(8,128)(2,1)}, u32[]{:S(2)}, u32[]{:S(2)}) collective-permute-start(bf16[2,128,640]{2,1,0:T(8,128)(2,1)S(1)} %pad_maximum_fusion.4.refs_9_), channel_id=1, source_target_pairs={{0,3},{1,0},{2,1},{3,2},{4,7},{5,4},{6,5},{7,6},{8,11},{9,8},{10,9... | collective-permute-start | bytes 983048 | tf_op jit(solution)/shard_map/ppermute | solution.py:52
  125.0 21.1 %collective-permute-start.16 = (bf16[2,128,640]{2,1,0:T(8,128)(2,1)S(1)}, bf16[2,128,640]{2,1,0:T(8,128)(2,1)}, u32[]{:S(2)}, u32[]{:S(2)}) collective-permute-start(bf16[2,128,640]{2,1,0:T(8,128)(2,1)S(1)} %pad_maximum_fusion.4.refs_9_), channel_id=1, source_target_pairs={{0,1},{1,2},{2,3},{3,0},{4,5},{5,6},{6,7},{7,4},{8,9},{9,10},{10,1... | collective-permute-start | bytes 983048 | tf_op jit(solution)/shard_map/ppermute | solution.py:52
  127.6 18.5 %collective-permute-start.14 = (bf16[2,128,640]{2,1,0:T(8,128)(2,1)S(1)}, bf16[2,128,640]{2,1,0:T(8,128)(2,1)}, u32[]{:S(2)}, u32[]{:S(2)}) collective-permute-start(bf16[2,128,640]{2,1,0:T(8,128)(2,1)S(1)} %collective-permute-done.8.refs_2_), channel_id=1, source_target_pairs={{0,4},{4,16},{16,20},{20,0},{1,5},{5,17},{17,21},{21,1},{2,6},{6,1... | collective-permute-start | bytes 983048 | tf_op jit(solution)/shard_map/ppermute | solution.py:52
  128.4 17.7 %collective-permute-start.15 = (bf16[2,128,640]{2,1,0:T(8,128)(2,1)S(1)}, bf16[2,128,640]{2,1,0:T(8,128)(2,1)}, u32[]{:S(2)}, u32[]{:S(2)}) collective-permute-start(bf16[2,128,640]{2,1,0:T(8,128)(2,1)S(1)} %collective-permute-done.9.refs_5_), channel_id=1, source_target_pairs={{0,20},{4,0},{16,4},{20,16},{1,21},{5,1},{17,5},{21,17},{2,22},{6,... | collective-permute-start | bytes 983048 | tf_op jit(solution)/shard_map/ppermute | solution.py:52
  130.3 15.8 %collective-permute-start.18 = (bf16[2,128,640]{2,1,0:T(8,128)(2,1)S(1)}, bf16[2,128,640]{2,1,0:T(8,128)(2,1)}, u32[]{:S(2)}, u32[]{:S(2)}) collective-permute-start(bf16[2,128,640]{2,1,0:T(8,128)(2,1)S(1)} %collective-permute-done.10.refs_10_), channel_id=1, source_target_pairs={{0,1},{1,2},{2,3},{3,0},{4,5},{5,6},{6,7},{7,4},{8,9},{9,10},{10,1... | collective-permute-start | bytes 983048 | tf_op jit(solution)/shard_map/ppermute | solution.py:52
  130.7 15.4 %collective-permute-start.19 = (bf16[2,128,640]{2,1,0:T(8,128)(2,1)}, bf16[2,128,640]{2,1,0:T(8,128)(2,1)}, u32[]{:S(2)}, u32[]{:S(2)}) collective-permute-start(bf16[2,128,640]{2,1,0:T(8,128)(2,1)} %collective-permute-done.11.refs_13_), channel_id=1, source_target_pairs={{0,3},{1,0},{2,1},{3,2},{4,7},{5,4},{6,5},{7,6},{8,11},{9,8},{10,9... | collective-permute-start | bytes 983048 | tf_op jit(solution)/shard_map/ppermute | solution.py:52
  135.8 3.6 %copy-start = (bf16[16,320,896]{2,1,0:T(8,128)(2,1)S(1)}, bf16[16,320,896]{2,1,0:T(8,128)(2,1)}, u32[]{:S(2)}) copy-start(bf16[16,320,896]{2,1,0:T(8,128)(2,1)} %all-gather.5.cloned.1.call-done) | copy-start | bytes 27525124
  139.4 3.6 %copy-start.1 = (bf16[16,320,896]{2,1,0:T(8,128)(2,1)S(1)}, bf16[16,320,896]{2,1,0:T(8,128)(2,1)}, u32[]{:S(2)}) copy-start(bf16[16,320,896]{2,1,0:T(8,128)(2,1)} %all-gather.7.cloned.1.call-done) | copy-start | bytes 27525124
  143.0 3.1 %copy-start.5 = (bf16[1,5120]{1,0:T(2,128)(2,1)S(1)}, bf16[1,5120]{1,0:T(2,128)(2,1)}, u32[]{:S(2)}) copy-start(bf16[1,5120]{1,0:T(2,128)(2,1)} %reshape.122.gain_ref) | copy-start | bytes 30724
Sparse Core Ops, SparseCore 0:
  10.5 56.6 all-gather.4
  79.6 55.4 all-gather.6

commit v4 on v3

--- a/solution.py
+++ b/solution.py
@@ -120,15 +120,16 @@
         total = jnp.sum(p, axis=1, keepdims=True)
         acc = lax.dot_general(p.astype(BF), fresh_ref[s, 1], nn, preferred_element_type=F32)
 
-        def block(b, carry):
+        def block(b, carry, last=False):
             high, total, acc = carry
             kv_copy(s, b).wait()
             start = pl.multiple_of(b * KB, KB)
             k = kv[s, 0, pl.ds(start, KB), :]
             v = kv[s, 1, pl.ds(start, KB), :]
             scores = lax.dot_general(q, k, nt, preferred_element_type=F32) * factor
-            pos = lax.broadcasted_iota(jnp.int32, scores.shape, 1)
-            scores = jnp.where(pos < length - start, scores, NEG)
+            if last:
+                pos = lax.broadcasted_iota(jnp.int32, scores.shape, 1)
+                scores = jnp.where(pos < length - start, scores, NEG)
             new = jnp.maximum(high, jnp.max(scores, axis=1, keepdims=True))
             old = jnp.exp2(high - new)
             p = jnp.exp2(scores - new)
@@ -136,7 +137,9 @@
             acc = acc * old + lax.dot_general(p.astype(BF), v, nn, preferred_element_type=F32)
             return new, total, acc
 
-        high, total, acc = lax.fori_loop(0, (length + KB - 1) // KB, block, (high, total, acc))
+        full = (length - 1) // KB
+        carry = lax.fori_loop(0, full, block, (high, total, acc))
+        high, total, acc = block(full, carry, last=True)
         done = (acc / total).astype(BF)
         at = pl.ds(pl.multiple_of(s * ROWS, ROWS), ROWS)
         for h in range(HEADS):
@@ -148,11 +151,12 @@
     mixed = jnp.dot(hot, ctx[...], preferred_element_type=F32).astype(BF)
     residual = jnp.dot(hot, res_ref[...], preferred_element_type=F32)
     ow_copy.wait()
-    for t in range(8):
-        terms = jnp.dot(mixed, ow[:, t * DT : (t + 1) * DT], preferred_element_type=F32)
-        terms = (terms + jnp.where(len_ref[SEQS] == t, residual, 0.0)).astype(BF)
-        for q in range(NC):
-            out_refs[q][t] = terms[q * CR : (q + 1) * CR]
+    for t in range(0, 8, 2):
+        terms = jnp.dot(mixed, ow[:, t * DT : (t + 2) * DT], preferred_element_type=F32)
+        for i in range(2):
+            part = terms[:, i * DT : (i + 1) * DT]
+            own = jnp.where(len_ref[SEQS] == t + i, residual, 0.0)
+            out_refs[0][t + i] = (part + own).astype(BF)
 
 
 def front(lengths, queries, fresh, residual, cache, out_weight):

time: 199 us -> 198 us (level)
  transfers between devices with their start and end apart: 23 -> 23, of which waited for: 9 -> 10; matrix products, arithmetic and copies ran while one was open for 4% -> 4% of each run, Pallas kernels for 10% -> 10%
where the time goes in v4:
time: 198 us; the launch traced here: 197 us
  waiting for transfers between devices  49.3 us (25%)
  blocking collectives  40.7 us (21%)
  Pallas kernels  38 us (19%)
  starting transfers between devices  35.3 us (18%)
  local copies, waits for them, and re-layouts  14.3 us (7%)
  between operations  14.3 us (7%)
  other arithmetic  5.21 us (3%)
    ppermute x20, starting transfers between devices, permute(): return lax.ppermute(value, axes, pairs)  30.5 us
    all_to_all x1, waiting for transfers between devices, per_device(): got = lax.all_to_all(terms[q], ('zl', 'y'), 0, 0, tiled=True)  27.7 us
    all_to_all x1, blocking collectives, per_device(): lax.all_to_all(mixed.reshape(16, 8 * RR, 1152), ('x', 'zh', 'c'), 0, 0, t...  26.5 us
    ppermute x20, waiting for transfers between devices, permute(): return lax.ppermute(value, axes, pairs)  21.6 us
    pallas_call x1, Pallas kernels, front(): pl.pallas_call(front_kernel, out_shape=[jax.ShapeDtypeStruct((8, CR, DT),...  17.2 us
    pallas_call x1, Pallas kernels, feed(): pl.pallas_call(feed_kernel, out_shape=jax.ShapeDtypeStruct((2 * CR, 1152)...  16.3 us
    all_to_all x1, blocking collectives, per_device(): even = lax.all_to_all(even, ('x', 'c'), 0, 0, tiled=True)  14.2 us
    unnamed x25, local copies, waits for them, and re-layouts  9.95 us
  transfers between devices with their start and end apart: 23, of which 10 were waited for; matrix products, arithmetic and copies ran while one was open for 4% of the time, Pallas kernels for 10%

profile of v4, /device:TPU:1, one launch (start us, length us, event | category | flops | bytes accessed | tf_op | source)
XLA Modules:
  0.0 197.0 jit_solution(12343648326898545213)
XLA Ops:
  7.2 0.0 all-gather.5.cloned.1.call-start
  7.2 1.8 copy.22
  9.0 1.3 broadcast_select_fusion
  10.3 0.0 copy-start.4
  10.3 0.0 all-gather.5.cloned.1.call-update
  10.4 0.9 slice.34
  11.3 4.4 %collective-permute-start = (bf16[2,224,896]{2,1,0:T(8,128)(2,1)}, bf16[2,224,896]{2,1,0:T(8,128)(2,1)S(1)}, u32[]{:S(2)}, u32[]{:S(2)}) collective-permute-start(bf16[2,224,896]{2,1,0:T(8,128)(2,1)} %slice.34), channel_id=1, source_target_pairs={{0,16},{16,0},{1,17},{17,1},{2,18},{18,2},{3,19},{19,3},{4,20},{20... | collective-permute-start | bytes 2408456 | tf_op jit(solution)/shard_map/ppermute | solution.py:52
  15.7 0.1 dynamic_slice.3
  15.8 0.1 pad_add_fusion.1.len_ref
  15.9 17.2 %attend_project.1 = bf16[8,256,640]{2,1,0:T(8,128)(2,1)} custom-call(s32[9]{0:T(128)S(1)} %pad_add_fusion.1.len_ref, bf16[8,32,1024]{2,1,0:T(8,128)(2,1)S(1)} %copy-done.2, bf16[8,2,32,128]{3,2,1,0:T(8,128)(2,1)S(1)} %copy-done.4, bf16[256,640]{1,0:T(8,128)(2,1)S(1)} %copy-done.3, bf16[8,2,2048,128]{3,2,1,0:T(8,128)(2,1)} %cache_ref.1, bf16[1024,5120]{1,0:T(8,128)(2,1)} %ow_ref.1), custom_call_target="tpu_custom_call" | custom-call | tf_op jit(solution)/shard_map/attend_project/pallas_call | solution.py:163
  33.1 0.5 collective-permute-done
  33.6 0.9 copy-done.8
  34.4 4.7 %all-to-all-start = ((bf16[8,256,640]{2,1,0:T(8,128)(2,1)}), bf16[8,256,640]{2,1,0:T(8,128)(2,1)S(1)}, u32[]{:S(2)}, u32[]{:S(2)}) async-start(bf16[8,256,640]{2,1,0:T(8,128)(2,1)} %attend_project.1), calls=%async_computation | async-start | bytes 5242880 | tf_op jit(solution)/shard_map/all_to_all | solution.py:337
  39.2 0.0 all-gather.7.cloned.1.call-start
  39.2 1.7 slice.35
  40.9 3.2 %collective-permute-start.1 = (bf16[2,96,896]{2,1,0:T(8,128)(2,1)}, bf16[2,96,896]{2,1,0:T(8,128)(2,1)S(1)}, u32[]{:S(2)}, u32[]{:S(2)}) collective-permute-start(bf16[2,96,896]{2,1,0:T(8,128)(2,1)} %slice.35), channel_id=1, source_target_pairs={{0,16},{16,0},{1,17},{17,1},{2,18},{18,2},{3,19},{19,3},{4,20},{20... | collective-permute-start | bytes 1032200 | tf_op jit(solution)/shard_map/ppermute | solution.py:52
  44.1 27.7 %all-to-all-done = bf16[8,256,640]{2,1,0:T(8,128)(2,1)S(1)} async-done(((bf16[8,256,640]{2,1,0:T(8,128)(2,1)}), bf16[8,256,640]{2,1,0:T(8,128)(2,1)S(1)}, u32[]{:S(2)}, u32[]{:S(2)}) %all-to-all-start) | async-done | bytes 2621472 | tf_op jit(solution)/shard_map/all_to_all | solution.py:337
  71.8 0.5 reduce_sum.22
  72.4 4.8 %collective-permute-done.1 = bf16[2,96,896]{2,1,0:T(8,128)(2,1)S(1)} collective-permute-done((bf16[2,96,896]{2,1,0:T(8,128)(2,1)}, bf16[2,96,896]{2,1,0:T(8,128)(2,1)S(1)}, u32[]{:S(2)}, u32[]{:S(2)}) %collective-permute-start.1) | collective-permute-done | bytes 344096 | tf_op jit(solution)/shard_map/ppermute | solution.py:52
  77.2 2.3 %pad_maximum_fusion = bf16[2,320,896]{2,1,0:T(8,128)(2,1)} fusion(bf16[2,96,896]{2,1,0:T(8,128)(2,1)S(1)} %collective-permute-done.1, bf16[2,224,896]{2,1,0:T(8,128)(2,1)} %copy-done.8), kind=kLoop, calls=%fused_computation.1 | loop fusion | flops 2293760 | bytes 2293760 | tf_op jit(solution)/shard_map/concatenate | solution.py:341
  79.5 0.0 all-gather.7.cloned.1.call-update
  79.5 0.0 copy-start.9
  79.5 0.0 copy-start.11
  79.5 0.0 copy-start.6
  79.5 14.2 %all_to_all.19 = bf16[8,32,640]{2,1,0:T(8,128)(2,1)S(1)} all-to-all(bf16[8,32,640]{2,1,0:T(8,128)(2,1)S(1)} %bitcast.25), channel_id=1, replica_groups=mesh['x'=4,'zh'=2,'c'=2,'zl'=2,'y'=4] {'x','c'}, dimensions={0} | all-to-all | bytes 655360 | tf_op jit(solution)/shard_map/all_to_all | solution.py:344
  93.8 2.8 %collective-permute-start.4 = (bf16[128,640]{1,0:T(8,128)(2,1)S(1)}, bf16[128,640]{1,0:T(8,128)(2,1)S(1)}, u32[]{:S(2)}, u32[]{:S(2)}) collective-permute-start(bf16[128,640]{1,0:T(8,128)(2,1)S(1)} %bitcast.30), channel_id=1, source_target_pairs={{0,2},{1,3},{2,0},{3,1},{4,6},{5,7},{6,4},{7,5},{8,10},{9,11},{10,... | collective-permute-start | bytes 491528 | tf_op jit(solution)/shard_map/ppermute | solution.py:52
  96.5 1.2 collective-permute-start.3
  97.7 0.3 collective-permute-start.2
  98.0 0.0 collective-permute-start.7
  98.0 3.2 %collective-permute-start.6 = (bf16[128,640]{1,0:T(8,128)(2,1)S(1)}, bf16[128,640]{1,0:T(8,128)(2,1)S(1)}, u32[]{:S(2)}, u32[]{:S(2)}) collective-permute-start(bf16[128,640]{1,0:T(8,128)(2,1)S(1)} %bitcast.27), channel_id=1, source_target_pairs={{0,20},{4,0},{16,4},{20,16},{1,21},{5,1},{17,5},{21,17},{2,22},{6,... | collective-permute-start | bytes 491528 | tf_op jit(solution)/shard_map/ppermute | solution.py:52
  101.2 0.0 collective-permute-done.4
  101.2 0.0 collective-permute-start.5
  101.2 2.7 %collective-permute-done.3 = bf16[128,640]{1,0:T(8,128)(2,1)S(1)} collective-permute-done((bf16[128,640]{1,0:T(8,128)(2,1)S(1)}, bf16[128,640]{1,0:T(8,128)(2,1)S(1)}, u32[]{:S(2)}, u32[]{:S(2)}) %collective-permute-start.3) | collective-permute-done | bytes 163872 | tf_op jit(solution)/shard_map/ppermute | solution.py:52
  104.0 0.6 collective-permute-done.2
  104.6 0.0 collective-permute-done.7
  104.6 0.9 collective-permute-done.6
  105.5 3.2 %collective-permute-done.5 = bf16[128,640]{1,0:T(8,128)(2,1)S(1)} collective-permute-done((bf16[128,640]{1,0:T(8,128)(2,1)S(1)}, bf16[128,640]{1,0:T(8,128)(2,1)S(1)}, u32[]{:S(2)}, u32[]{:S(2)}) %collective-permute-start.5) | collective-permute-done | bytes 163872 | tf_op jit(solution)/shard_map/ppermute | solution.py:52
  108.8 0.1 collective-permute-start.8
  108.9 2.7 %collective-permute-start.9 = (bf16[2,128,640]{2,1,0:T(8,128)(2,1)S(1)}, bf16[2,128,640]{2,1,0:T(8,128)(2,1)S(1)}, u32[]{:S(2)}, u32[]{:S(2)}) collective-permute-start(bf16[2,128,640]{2,1,0:T(8,128)(2,1)S(1)} %pad_maximum_fusion.2.refs_1_), channel_id=1, source_target_pairs={{0,20},{4,0},{16,4},{20,16},{1,21},{5,1},{17,5},{21,17},{2,22},{6,... | collective-permute-start | bytes 983048 | tf_op jit(solution)/shard_map/ppermute | solution.py:52
  111.6 0.6 reshape.122.gain_ref
  112.2 0.0 collective-permute-start.13
  112.2 1.5 collective-permute-start.12
  113.6 2.3 %collective-permute-start.17 = (bf16[2,128,640]{2,1,0:T(8,128)(2,1)S(1)}, bf16[2,128,640]{2,1,0:T(8,128)(2,1)S(1)}, u32[]{:S(2)}, u32[]{:S(2)}) collective-permute-start(bf16[2,128,640]{2,1,0:T(8,128)(2,1)S(1)} %pad_maximum_fusion.3.refs_8_), channel_id=1, source_target_pairs={{0,3},{1,0},{2,1},{3,2},{4,7},{5,4},{6,5},{7,6},{8,11},{9,8},{10,9... | collective-permute-start | bytes 983048 | tf_op jit(solution)/shard_map/ppermute | solution.py:52
  115.9 1.8 collective-permute-done.8.refs_2_
  117.8 0.0 collective-permute-start.10
  117.8 2.7 %collective-permute-start.11 = (bf16[2,128,640]{2,1,0:T(8,128)(2,1)S(1)}, bf16[2,128,640]{2,1,0:T(8,128)(2,1)}, u32[]{:S(2)}, u32[]{:S(2)}) collective-permute-start(bf16[2,128,640]{2,1,0:T(8,128)(2,1)S(1)} %pad_maximum_fusion.4.refs_9_), channel_id=1, source_target_pairs={{0,3},{1,0},{2,1},{3,2},{4,7},{5,4},{6,5},{7,6},{8,11},{9,8},{10,9... | collective-permute-start | bytes 983048 | tf_op jit(solution)/shard_map/ppermute | solution.py:52
  120.4 0.1 select_reduce_fusion
  120.6 4.7 %collective-permute-done.10.refs_10_ = bf16[2,128,640]{2,1,0:T(8,128)(2,1)S(1)} collective-permute-done((bf16[2,128,640]{2,1,0:T(8,128)(2,1)S(1)}, bf16[2,128,640]{2,1,0:T(8,128)(2,1)S(1)}, u32[]{:S(2)}, u32[]{:S(2)}) %collective-permute-start.10) | collective-permute-done | bytes 327712 | tf_op jit(solution)/shard_map/ppermute | solution.py:52
  125.3 2.3 %collective-permute-done.11.refs_13_ = bf16[2,128,640]{2,1,0:T(8,128)(2,1)} collective-permute-done((bf16[2,128,640]{2,1,0:T(8,128)(2,1)S(1)}, bf16[2,128,640]{2,1,0:T(8,128)(2,1)}, u32[]{:S(2)}, u32[]{:S(2)}) %collective-permute-start.11) | collective-permute-done | bytes 327712 | tf_op jit(solution)/shard_map/ppermute | solution.py:52
  127.6 2.7 %collective-permute-start.15 = (bf16[2,128,640]{2,1,0:T(8,128)(2,1)S(1)}, bf16[2,128,640]{2,1,0:T(8,128)(2,1)}, u32[]{:S(2)}, u32[]{:S(2)}) collective-permute-start(bf16[2,128,640]{2,1,0:T(8,128)(2,1)S(1)} %collective-permute-done.9.refs_5_), channel_id=1, source_target_pairs={{0,20},{4,0},{16,4},{20,16},{1,21},{5,1},{17,5},{21,17},{2,22},{6,... | collective-permute-start | bytes 983048 | tf_op jit(solution)/shard_map/ppermute | solution.py:52
  130.3 0.0 collective-permute-done.12.refs_3_
  130.3 0.1 collective-permute-start.18
  130.4 0.0 collective-permute-done.17.refs_12_
  130.4 3.5 %collective-permute-start.19 = (bf16[2,128,640]{2,1,0:T(8,128)(2,1)}, bf16[2,128,640]{2,1,0:T(8,128)(2,1)}, u32[]{:S(2)}, u32[]{:S(2)}) collective-permute-start(bf16[2,128,640]{2,1,0:T(8,128)(2,1)} %collective-permute-done.11.refs_13_), channel_id=1, source_target_pairs={{0,3},{1,0},{2,1},{3,2},{4,7},{5,4},{6,5},{7,6},{8,11},{9,8},{10,9... | collective-permute-start | bytes 983048 | tf_op jit(solution)/shard_map/ppermute | solution.py:52
  133.9 0.7 iota_add_fusion
  134.6 0.9 add.115.src_ref
  135.5 0.1 pad_add_fusion.pos_ref
  135.6 3.6 %copy-done = bf16[16,320,896]{2,1,0:T(8,128)(2,1)S(1)} copy-done((bf16[16,320,896]{2,1,0:T(8,128)(2,1)S(1)}, bf16[16,320,896]{2,1,0:T(8,128)(2,1)}, u32[]{:S(2)}) %copy-start) | copy-done | bytes 9175064
  139.2 3.6 %copy-done.1 = bf16[16,320,896]{2,1,0:T(8,128)(2,1)S(1)} copy-done((bf16[16,320,896]{2,1,0:T(8,128)(2,1)S(1)}, bf16[16,320,896]{2,1,0:T(8,128)(2,1)}, u32[]{:S(2)}) %copy-start.1) | copy-done | bytes 9175064
  142.8 3.0 %assemble_weights.1.w = bf16[2,5120,896]{2,1,0:T(8,128)(2,1)S(1)} custom-call(s32[4]{0:T(128)S(1)} %pad_add_fusion.pos_ref, s32[16]{0:T(128)S(1)} %copy-done.6, bf16[8,2,320,896]{3,2,1,0:T(8,128)(2,1)S(1)} %bitcast.21, bf16[8,2,320,896]{3,2,1,0:T(8,128)(2,1)S(1)} %bitcast.22), custom_call_target="tpu_custom_call" | custom-call | tf_op jit(solution)/shard_map/assemble_weights/pallas_call | solution.py:199
  145.9 0.0 collective-permute-done.14.refs_6_
  145.9 16.3 %feed_forward.1 = bf16[512,1152]{1,0:T(8,128)(2,1)S(1)} custom-call(s32[4]{0:T(128)S(1)} %pad_add_fusion.pos_ref, s32[512,1]{1,0:T(8,128)S(1)} %add.115.src_ref, bf16[1,5120]{1,0:T(2,128)(2,1)S(1)} %copy-done.5, bf16[2,5120,896]{2,1,0:T(8,128)(2,1)S(1)} %assemble_weights.1.w, bf16[2,128,640]{2,1,0:T(8,128)(2,1)S(1)} %pad_maximum_fusion.1.refs_0_, ...), custom_call_target="tpu_custom_call" | custom-call | tf_op jit(solution)/shard_map/feed_forward/pallas_call | solution.py:264
  162.2 26.5 %all_to_all.20.refs_0_ = bf16[16,32,1152]{2,1,0:T(8,128)(2,1)S(1)} all-to-all(bf16[16,32,1152]{2,1,0:T(8,128)(2,1)S(1)} %bitcast.23), channel_id=1, replica_groups=mesh['x'=4,'zh'=2,'c'=2,'zl'=2,'y'=4] {'x','zh','c'}, dimensions={0} | all-to-all | bytes 2359296 | tf_op jit(solution)/shard_map/all_to_all | solution.py:357
  188.7 1.5 finish.1
  (33 shorter events, 0.3 us)
Async XLA Ops:
  7.2 128.4 %all-gather.5.cloned.1.call-start = ((), (), s32[]{:S(2)}) async-start(), calls=%async_computation.3 | async-start | bytes 10321920 | tf_op jit(solution)/shard_map/all_gather | solution.py:318
  10.3 22.8 %copy-start.7 = (bf16[2,320,896]{2,1,0:T(8,128)(2,1)}, bf16[2,320,896]{2,1,0:T(8,128)(2,1)S(1)}, u32[]{:S(2)}) copy-start(bf16[2,320,896]{2,1,0:T(8,128)(2,1)S(1)} %get-tuple-element.26) | copy-start | bytes 3440644
  10.3 5.4 %copy-start.10 = (s32[128]{0:T(128)S(1)}, s32[128]{0:T(128)}, u32[]{:S(2)}) copy-start(s32[128]{0:T(128)} %param.14) | copy-start | bytes 1540
  10.3 5.6 %copy-start.2 = (bf16[8,32,1024]{2,1,0:T(8,128)(2,1)S(1)}, bf16[8,32,1024]{2,1,0:T(8,128)(2,1)}, u32[]{:S(2)}) copy-start(bf16[8,32,1024]{2,1,0:T(8,128)(2,1)} %q_ref.1) | copy-start | bytes 1572868
  10.3 5.6 %copy-start.3 = (bf16[256,640]{1,0:T(8,128)(2,1)S(1)}, bf16[256,640]{1,0:T(8,128)(2,1)}, u32[]{:S(2)}) copy-start(bf16[256,640]{1,0:T(8,128)(2,1)} %res_ref.1) | copy-start | bytes 983044
  10.3 5.6 %copy-start.4 = (bf16[8,2,32,128]{3,2,1,0:T(8,128)(2,1)S(1)}, bf16[8,2,32,128]{3,2,1,0:T(8,128)(2,1)}, u32[]{:S(2)}) copy-start(bf16[8,2,32,128]{3,2,1,0:T(8,128)(2,1)} %fresh_ref.1) | copy-start | bytes 393220
  11.3 22.3 %collective-permute-start = (bf16[2,224,896]{2,1,0:T(8,128)(2,1)}, bf16[2,224,896]{2,1,0:T(8,128)(2,1)S(1)}, u32[]{:S(2)}, u32[]{:S(2)}) collective-permute-start(bf16[2,224,896]{2,1,0:T(8,128)(2,1)} %slice.34), channel_id=1, source_target_pairs={{0,16},{16,0},{1,17},{17,1},{2,18},{18,2},{3,19},{19,3},{4,20},{20... | collective-permute-start | bytes 2408456 | tf_op jit(solution)/shard_map/ppermute | solution.py:52
  33.6 0.9 copy-start.8
  34.4 37.4 %all-to-all-start = ((bf16[8,256,640]{2,1,0:T(8,128)(2,1)}), bf16[8,256,640]{2,1,0:T(8,128)(2,1)S(1)}, u32[]{:S(2)}, u32[]{:S(2)}) async-start(bf16[8,256,640]{2,1,0:T(8,128)(2,1)} %attend_project.1), calls=%async_computation | async-start | bytes 5242880 | tf_op jit(solution)/shard_map/all_to_all | solution.py:337
  39.2 96.5 %all-gather.7.cloned.1.call-start = ((), (), s32[]{:S(2)}) async-start(), calls=%async_computation.4 | async-start | bytes 10321920 | tf_op jit(solution)/shard_map/all_gather | solution.py:342
  40.9 36.2 %collective-permute-start.1 = (bf16[2,96,896]{2,1,0:T(8,128)(2,1)}, bf16[2,96,896]{2,1,0:T(8,128)(2,1)S(1)}, u32[]{:S(2)}, u32[]{:S(2)}) collective-permute-start(bf16[2,96,896]{2,1,0:T(8,128)(2,1)} %slice.35), channel_id=1, source_target_pairs={{0,16},{16,0},{1,17},{17,1},{2,18},{18,2},{3,19},{19,3},{4,20},{20... | collective-permute-start | bytes 1032200 | tf_op jit(solution)/shard_map/ppermute | solution.py:52
  79.5 32.1 %copy-start.9 = (bf16[5120]{0:T(1024)(128)(2,1)S(1)}, bf16[5120]{0:T(1024)(128)(2,1)}, u32[]{:S(2)}) copy-start(bf16[5120]{0:T(1024)(128)(2,1)} %param.17) | copy-start | bytes 30724
  79.5 40.9 %copy-start.11 = (s32[128]{0:T(128)S(1)}, s32[128]{0:T(128)}, u32[]{:S(2)}) copy-start(s32[128]{0:T(128)} %param.15) | copy-start | bytes 1540
  79.5 56.1 %copy-start.6 = (s32[16]{0:T(128)S(1)}, s32[16]{0:T(128)}, u32[]{:S(2)}) copy-start(s32[16]{0:T(128)} %block_ref.1) | copy-start | bytes 196
  93.8 7.5 %collective-permute-start.4 = (bf16[128,640]{1,0:T(8,128)(2,1)S(1)}, bf16[128,640]{1,0:T(8,128)(2,1)S(1)}, u32[]{:S(2)}, u32[]{:S(2)}) collective-permute-start(bf16[128,640]{1,0:T(8,128)(2,1)S(1)} %bitcast.30), channel_id=1, source_target_pairs={{0,2},{1,3},{2,0},{3,1},{4,6},{5,7},{6,4},{7,5},{8,10},{9,11},{10,... | collective-permute-start | bytes 491528 | tf_op jit(solution)/shard_map/ppermute | solution.py:52
  96.5 7.4 %collective-permute-start.3 = (bf16[128,640]{1,0:T(8,128)(2,1)S(1)}, bf16[128,640]{1,0:T(8,128)(2,1)S(1)}, u32[]{:S(2)}, u32[]{:S(2)}) collective-permute-start(bf16[128,640]{1,0:T(8,128)(2,1)S(1)} %bitcast.31), channel_id=1, source_target_pairs={{0,3},{1,0},{2,1},{3,2},{4,7},{5,4},{6,5},{7,6},{8,11},{9,8},{10,9... | collective-permute-start | bytes 491528 | tf_op jit(solution)/shard_map/ppermute | solution.py:52
  97.7 6.9 %collective-permute-start.2 = (bf16[128,640]{1,0:T(8,128)(2,1)S(1)}, bf16[128,640]{1,0:T(8,128)(2,1)S(1)}, u32[]{:S(2)}, u32[]{:S(2)}) collective-permute-start(bf16[128,640]{1,0:T(8,128)(2,1)S(1)} %bitcast.32), channel_id=1, source_target_pairs={{0,1},{1,2},{2,3},{3,0},{4,5},{5,6},{6,7},{7,4},{8,9},{9,10},{10,1... | collective-permute-start | bytes 491528 | tf_op jit(solution)/shard_map/ppermute | solution.py:52
  98.0 6.6 %collective-permute-start.7 = (bf16[128,640]{1,0:T(8,128)(2,1)S(1)}, bf16[128,640]{1,0:T(8,128)(2,1)S(1)}, u32[]{:S(2)}, u32[]{:S(2)}) collective-permute-start(bf16[128,640]{1,0:T(8,128)(2,1)S(1)} %bitcast.26), channel_id=1, source_target_pairs={{0,16},{4,20},{16,0},{20,4},{1,17},{5,21},{17,1},{21,5},{2,18},{6,... | collective-permute-start | bytes 491528 | tf_op jit(solution)/shard_map/ppermute | solution.py:52
  98.0 7.5 %collective-permute-start.6 = (bf16[128,640]{1,0:T(8,128)(2,1)S(1)}, bf16[128,640]{1,0:T(8,128)(2,1)S(1)}, u32[]{:S(2)}, u32[]{:S(2)}) collective-permute-start(bf16[128,640]{1,0:T(8,128)(2,1)S(1)} %bitcast.27), channel_id=1, source_target_pairs={{0,20},{4,0},{16,4},{20,16},{1,21},{5,1},{17,5},{21,17},{2,22},{6,... | collective-permute-start | bytes 491528 | tf_op jit(solution)/shard_map/ppermute | solution.py:52
  101.2 7.5 %collective-permute-start.5 = (bf16[128,640]{1,0:T(8,128)(2,1)S(1)}, bf16[128,640]{1,0:T(8,128)(2,1)S(1)}, u32[]{:S(2)}, u32[]{:S(2)}) collective-permute-start(bf16[128,640]{1,0:T(8,128)(2,1)S(1)} %bitcast.28), channel_id=1, source_target_pairs={{0,4},{4,16},{16,20},{20,0},{1,5},{5,17},{17,21},{21,1},{2,6},{6,1... | collective-permute-start | bytes 491528 | tf_op jit(solution)/shard_map/ppermute | solution.py:52
  108.8 9.0 %collective-permute-start.8 = (bf16[2,128,640]{2,1,0:T(8,128)(2,1)S(1)}, bf16[2,128,640]{2,1,0:T(8,128)(2,1)S(1)}, u32[]{:S(2)}, u32[]{:S(2)}) collective-permute-start(bf16[2,128,640]{2,1,0:T(8,128)(2,1)S(1)} %pad_maximum_fusion.1.refs_0_), channel_id=1, source_target_pairs={{0,4},{4,16},{16,20},{20,0},{1,5},{5,17},{17,21},{21,1},{2,6},{6,1... | collective-permute-start | bytes 983048 | tf_op jit(solution)/shard_map/ppermute | solution.py:52
  108.9 8.9 %collective-permute-start.9 = (bf16[2,128,640]{2,1,0:T(8,128)(2,1)S(1)}, bf16[2,128,640]{2,1,0:T(8,128)(2,1)S(1)}, u32[]{:S(2)}, u32[]{:S(2)}) collective-permute-start(bf16[2,128,640]{2,1,0:T(8,128)(2,1)S(1)} %pad_maximum_fusion.2.refs_1_), channel_id=1, source_target_pairs={{0,20},{4,0},{16,4},{20,16},{1,21},{5,1},{17,5},{21,17},{2,22},{6,... | collective-permute-start | bytes 983048 | tf_op jit(solution)/shard_map/ppermute | solution.py:52
  112.2 15.4 %collective-permute-start.13 = (bf16[2,128,640]{2,1,0:T(8,128)(2,1)S(1)}, bf16[2,128,640]{2,1,0:T(8,128)(2,1)S(1)}, u32[]{:S(2)}, u32[]{:S(2)}) collective-permute-start(bf16[2,128,640]{2,1,0:T(8,128)(2,1)S(1)} %pad_maximum_fusion.1.refs_0_), channel_id=1, source_target_pairs={{0,20},{4,0},{16,4},{20,16},{1,21},{5,1},{17,5},{21,17},{2,22},{6,... | collective-permute-start | bytes 983048 | tf_op jit(solution)/shard_map/ppermute | solution.py:52
  112.2 18.1 %collective-permute-start.12 = (bf16[2,128,640]{2,1,0:T(8,128)(2,1)S(1)}, bf16[2,128,640]{2,1,0:T(8,128)(2,1)S(1)}, u32[]{:S(2)}, u32[]{:S(2)}) collective-permute-start(bf16[2,128,640]{2,1,0:T(8,128)(2,1)S(1)} %pad_maximum_fusion.2.refs_1_), channel_id=1, source_target_pairs={{0,4},{4,16},{16,20},{20,0},{1,5},{5,17},{17,21},{21,1},{2,6},{6,1... | collective-permute-start | bytes 983048 | tf_op jit(solution)/shard_map/ppermute | solution.py:52
  113.6 16.7 %collective-permute-start.17 = (bf16[2,128,640]{2,1,0:T(8,128)(2,1)S(1)}, bf16[2,128,640]{2,1,0:T(8,128)(2,1)S(1)}, u32[]{:S(2)}, u32[]{:S(2)}) collective-permute-start(bf16[2,128,640]{2,1,0:T(8,128)(2,1)S(1)} %pad_maximum_fusion.3.refs_8_), channel_id=1, source_target_pairs={{0,3},{1,0},{2,1},{3,2},{4,7},{5,4},{6,5},{7,6},{8,11},{9,8},{10,9... | collective-permute-start | bytes 983048 | tf_op jit(solution)/shard_map/ppermute | solution.py:52
  117.8 7.5 %collective-permute-start.10 = (bf16[2,128,640]{2,1,0:T(8,128)(2,1)S(1)}, bf16[2,128,640]{2,1,0:T(8,128)(2,1)S(1)}, u32[]{:S(2)}, u32[]{:S(2)}) collective-permute-start(bf16[2,128,640]{2,1,0:T(8,128)(2,1)S(1)} %pad_maximum_fusion.3.refs_8_), channel_id=1, source_target_pairs={{0,1},{1,2},{2,3},{3,0},{4,5},{5,6},{6,7},{7,4},{8,9},{9,10},{10,1... | collective-permute-start | bytes 983048 | tf_op jit(solution)/shard_map/ppermute | solution.py:52
  117.8 9.8 %collective-permute-start.11 = (bf16[2,128,640]{2,1,0:T(8,128)(2,1)S(1)}, bf16[2,128,640]{2,1,0:T(8,128)(2,1)}, u32[]{:S(2)}, u32[]{:S(2)}) collective-permute-start(bf16[2,128,640]{2,1,0:T(8,128)(2,1)S(1)} %pad_maximum_fusion.4.refs_9_), channel_id=1, source_target_pairs={{0,3},{1,0},{2,1},{3,2},{4,7},{5,4},{6,5},{7,6},{8,11},{9,8},{10,9... | collective-permute-start | bytes 983048 | tf_op jit(solution)/shard_map/ppermute | solution.py:52
  125.3 20.6 %collective-permute-start.16 = (bf16[2,128,640]{2,1,0:T(8,128)(2,1)S(1)}, bf16[2,128,640]{2,1,0:T(8,128)(2,1)}, u32[]{:S(2)}, u32[]{:S(2)}) collective-permute-start(bf16[2,128,640]{2,1,0:T(8,128)(2,1)S(1)} %pad_maximum_fusion.4.refs_9_), channel_id=1, source_target_pairs={{0,1},{1,2},{2,3},{3,0},{4,5},{5,6},{6,7},{7,4},{8,9},{9,10},{10,1... | collective-permute-start | bytes 983048 | tf_op jit(solution)/shard_map/ppermute | solution.py:52
  127.6 18.3 %collective-permute-start.14 = (bf16[2,128,640]{2,1,0:T(8,128)(2,1)S(1)}, bf16[2,128,640]{2,1,0:T(8,128)(2,1)}, u32[]{:S(2)}, u32[]{:S(2)}) collective-permute-start(bf16[2,128,640]{2,1,0:T(8,128)(2,1)S(1)} %collective-permute-done.8.refs_2_), channel_id=1, source_target_pairs={{0,4},{4,16},{16,20},{20,0},{1,5},{5,17},{17,21},{21,1},{2,6},{6,1... | collective-permute-start | bytes 983048 | tf_op jit(solution)/shard_map/ppermute | solution.py:52
  127.6 18.3 %collective-permute-start.15 = (bf16[2,128,640]{2,1,0:T(8,128)(2,1)S(1)}, bf16[2,128,640]{2,1,0:T(8,128)(2,1)}, u32[]{:S(2)}, u32[]{:S(2)}) collective-permute-start(bf16[2,128,640]{2,1,0:T(8,128)(2,1)S(1)} %collective-permute-done.9.refs_5_), channel_id=1, source_target_pairs={{0,20},{4,0},{16,4},{20,16},{1,21},{5,1},{17,5},{21,17},{2,22},{6,... | collective-permute-start | bytes 983048 | tf_op jit(solution)/shard_map/ppermute | solution.py:52
  130.3 15.6 %collective-permute-start.18 = (bf16[2,128,640]{2,1,0:T(8,128)(2,1)S(1)}, bf16[2,128,640]{2,1,0:T(8,128)(2,1)}, u32[]{:S(2)}, u32[]{:S(2)}) collective-permute-start(bf16[2,128,640]{2,1,0:T(8,128)(2,1)S(1)} %collective-permute-done.10.refs_10_), channel_id=1, source_target_pairs={{0,1},{1,2},{2,3},{3,0},{4,5},{5,6},{6,7},{7,4},{8,9},{9,10},{10,1... | collective-permute-start | bytes 983048 | tf_op jit(solution)/shard_map/ppermute | solution.py:52
  130.4 15.6 %collective-permute-start.19 = (bf16[2,128,640]{2,1,0:T(8,128)(2,1)}, bf16[2,128,640]{2,1,0:T(8,128)(2,1)}, u32[]{:S(2)}, u32[]{:S(2)}) collective-permute-start(bf16[2,128,640]{2,1,0:T(8,128)(2,1)} %collective-permute-done.11.refs_13_), channel_id=1, source_target_pairs={{0,3},{1,0},{2,1},{3,2},{4,7},{5,4},{6,5},{7,6},{8,11},{9,8},{10,9... | collective-permute-start | bytes 983048 | tf_op jit(solution)/shard_map/ppermute | solution.py:52
  135.6 3.6 %copy-start = (bf16[16,320,896]{2,1,0:T(8,128)(2,1)S(1)}, bf16[16,320,896]{2,1,0:T(8,128)(2,1)}, u32[]{:S(2)}) copy-start(bf16[16,320,896]{2,1,0:T(8,128)(2,1)} %all-gather.5.cloned.1.call-done) | copy-start | bytes 27525124
  139.2 3.6 %copy-start.1 = (bf16[16,320,896]{2,1,0:T(8,128)(2,1)S(1)}, bf16[16,320,896]{2,1,0:T(8,128)(2,1)}, u32[]{:S(2)}) copy-start(bf16[16,320,896]{2,1,0:T(8,128)(2,1)} %all-gather.7.cloned.1.call-done) | copy-start | bytes 27525124
  142.8 3.1 %copy-start.5 = (bf16[1,5120]{1,0:T(2,128)(2,1)S(1)}, bf16[1,5120]{1,0:T(2,128)(2,1)}, u32[]{:S(2)}) copy-start(bf16[1,5120]{1,0:T(2,128)(2,1)} %reshape.122.gain_ref) | copy-start | bytes 30724
Sparse Core Ops, SparseCore 0:
  10.5 56.6 all-gather.4
  79.6 54.4 all-gather.6

commit v5 on v4

--- a/solution.py
+++ b/solution.py
@@ -316,7 +316,7 @@
     own = jnp.where(zh == 0, left, right)
     other = jnp.where(zh == 0, right, left)
     near = lax.all_gather(own, ("x", "c"), axis=0)
-    lower, upper = swap(other[:, :224], "zh"), swap(other[:, 224:], "zh")
+    lower, upper = swap(other[:, :192], "zh"), swap(other[:, 192:], "zh")
 
     own_lengths = lax.dynamic_slice_in_dim(lengths, group * SEQS, SEQS, 0)
     scalars = jnp.concatenate([own_lengths, pos[1:2]])

time: 198 us -> 197 us (level)
  waiting for transfers between devices: 49.3 us -> 52.2 us
  transfers between devices with their start and end apart: 23 -> 23, of which waited for: 10 -> 9; matrix products, arithmetic and copies ran while one was open for 4% -> 3% of each run, Pallas kernels for 10% -> 9%
where the time goes in v5:
time: 197 us
  waiting for transfers between devices  52.2 us (26%)
  blocking collectives  41.1 us (21%)
  Pallas kernels  36.4 us (18%)
  starting transfers between devices  35.1 us (18%)
  between operations  14.3 us (7%)
  local copies, waits for them, and re-layouts  12.7 us (6%)
  other arithmetic  5.31 us (3%)
    ppermute x20, starting transfers between devices, permute(): return lax.ppermute(value, axes, pairs)  30.4 us
    all_to_all x1, waiting for transfers between devices, per_device(): got = lax.all_to_all(terms[q], ('zl', 'y'), 0, 0, tiled=True)  28.7 us
    all_to_all x1, blocking collectives, per_device(): lax.all_to_all(mixed.reshape(16, 8 * RR, 1152), ('x', 'zh', 'c'), 0, 0, t...  26.3 us
    ppermute x20, waiting for transfers between devices, permute(): return lax.ppermute(value, axes, pairs)  23.4 us
    pallas_call x1, Pallas kernels, feed(): pl.pallas_call(feed_kernel, out_shape=jax.ShapeDtypeStruct((2 * CR, 1152)...  16.3 us
    pallas_call x1, Pallas kernels, front(): pl.pallas_call(front_kernel, out_shape=[jax.ShapeDtypeStruct((8, CR, DT),...  15.6 us
    all_to_all x1, blocking collectives, per_device(): even = lax.all_to_all(even, ('x', 'c'), 0, 0, tiled=True)  14.7 us
    unnamed x25, local copies, waits for them, and re-layouts  9.91 us
  transfers between devices with their start and end apart: 23, of which 9 were waited for; matrix products, arithmetic and copies ran while one was open for 3% of the time, Pallas kernels for 9%

profile of v5, /device:TPU:1, one launch (start us, length us, event | category | flops | bytes accessed | tf_op | source)
XLA Modules:
  0.0 197.1 jit_solution(17538575309409401425)
XLA Ops:
  7.2 0.0 all-gather.5.cloned.1.call-start
  7.2 1.8 copy.22
  9.0 1.3 broadcast_select_fusion
  10.3 0.0 copy-start.4
  10.3 0.0 all-gather.5.cloned.1.call-update
  10.4 0.1 slice.34
  10.4 4.5 %collective-permute-start = (bf16[2,192,896]{2,1,0:T(8,128)(2,1)S(1)}, bf16[2,192,896]{2,1,0:T(8,128)(2,1)S(1)}, u32[]{:S(2)}, u32[]{:S(2)}) collective-permute-start(bf16[2,192,896]{2,1,0:T(8,128)(2,1)S(1)} %slice.34), channel_id=1, source_target_pairs={{0,16},{16,0},{1,17},{17,1},{2,18},{18,2},{3,19},{19,3},{4,20},{20... | collective-permute-start | bytes 2064392 | tf_op jit(solution)/shard_map/ppermute | solution.py:52
  14.9 0.1 dynamic_slice.3
  15.0 0.1 pad_add_fusion.1.len_ref
  15.1 15.6 %attend_project.1 = bf16[8,256,640]{2,1,0:T(8,128)(2,1)} custom-call(s32[9]{0:T(128)S(1)} %pad_add_fusion.1.len_ref, bf16[8,32,1024]{2,1,0:T(8,128)(2,1)S(1)} %copy-done.2, bf16[8,2,32,128]{3,2,1,0:T(8,128)(2,1)S(1)} %copy-done.4, bf16[256,640]{1,0:T(8,128)(2,1)S(1)} %copy-done.3, bf16[8,2,2048,128]{3,2,1,0:T(8,128)(2,1)} %cache_ref.1, bf16[1024,5120]{1,0:T(8,128)(2,1)} %ow_ref.1), custom_call_target="tpu_custom_call" | custom-call | tf_op jit(solution)/shard_map/attend_project/pallas_call | solution.py:163
  30.7 0.0 copy-start.8
  30.7 0.8 copy-done.8
  31.5 4.6 %all-to-all-start = ((bf16[8,256,640]{2,1,0:T(8,128)(2,1)}), bf16[8,256,640]{2,1,0:T(8,128)(2,1)S(1)}, u32[]{:S(2)}, u32[]{:S(2)}) async-start(bf16[8,256,640]{2,1,0:T(8,128)(2,1)} %attend_project.1), calls=%async_computation | async-start | bytes 5242880 | tf_op jit(solution)/shard_map/all_to_all | solution.py:337
  36.2 0.0 all-gather.7.cloned.1.call-start
  36.2 1.1 slice.35
  37.3 3.0 %collective-permute-start.1 = (bf16[2,128,896]{2,1,0:T(8,128)(2,1)S(1)}, bf16[2,128,896]{2,1,0:T(8,128)(2,1)}, u32[]{:S(2)}, u32[]{:S(2)}) collective-permute-start(bf16[2,128,896]{2,1,0:T(8,128)(2,1)S(1)} %slice.35), channel_id=1, source_target_pairs={{0,16},{16,0},{1,17},{17,1},{2,18},{18,2},{3,19},{19,3},{4,20},{20... | collective-permute-start | bytes 1376264 | tf_op jit(solution)/shard_map/ppermute | solution.py:52
  40.2 28.7 %all-to-all-done = bf16[8,256,640]{2,1,0:T(8,128)(2,1)S(1)} async-done(((bf16[8,256,640]{2,1,0:T(8,128)(2,1)}), bf16[8,256,640]{2,1,0:T(8,128)(2,1)S(1)}, u32[]{:S(2)}, u32[]{:S(2)}) %all-to-all-start) | async-done | bytes 2621472 | tf_op jit(solution)/shard_map/all_to_all | solution.py:337
  69.0 0.5 reduce_sum.22
  69.5 7.2 %collective-permute-done.1 = bf16[2,128,896]{2,1,0:T(8,128)(2,1)} collective-permute-done((bf16[2,128,896]{2,1,0:T(8,128)(2,1)S(1)}, bf16[2,128,896]{2,1,0:T(8,128)(2,1)}, u32[]{:S(2)}, u32[]{:S(2)}) %collective-permute-start.1) | collective-permute-done | bytes 458784 | tf_op jit(solution)/shard_map/ppermute | solution.py:52
  76.7 2.4 %pad_maximum_fusion = bf16[2,320,896]{2,1,0:T(8,128)(2,1)} fusion(bf16[2,128,896]{2,1,0:T(8,128)(2,1)} %collective-permute-done.1, bf16[2,192,896]{2,1,0:T(8,128)(2,1)} %copy-done.8), kind=kLoop, calls=%fused_computation.1 | loop fusion | flops 2293760 | bytes 2293760 | tf_op jit(solution)/shard_map/concatenate | solution.py:341
  79.1 0.0 all-gather.7.cloned.1.call-update
  79.1 0.0 copy-start.9
  79.1 0.0 copy-start.11
  79.1 0.0 copy-start.6
  79.1 14.7 %all_to_all.19 = bf16[8,32,640]{2,1,0:T(8,128)(2,1)S(1)} all-to-all(bf16[8,32,640]{2,1,0:T(8,128)(2,1)S(1)} %bitcast.25), channel_id=1, replica_groups=mesh['x'=4,'zh'=2,'c'=2,'zl'=2,'y'=4] {'x','c'}, dimensions={0} | all-to-all | bytes 655360 | tf_op jit(solution)/shard_map/all_to_all | solution.py:344
  93.9 2.8 %collective-permute-start.4 = (bf16[128,640]{1,0:T(8,128)(2,1)S(1)}, bf16[128,640]{1,0:T(8,128)(2,1)S(1)}, u32[]{:S(2)}, u32[]{:S(2)}) collective-permute-start(bf16[128,640]{1,0:T(8,128)(2,1)S(1)} %bitcast.30), channel_id=1, source_target_pairs={{0,2},{1,3},{2,0},{3,1},{4,6},{5,7},{6,4},{7,5},{8,10},{9,11},{10,... | collective-permute-start | bytes 491528 | tf_op jit(solution)/shard_map/ppermute | solution.py:52
  96.7 1.2 collective-permute-start.3
  97.8 0.3 collective-permute-start.2
  98.1 0.1 collective-permute-start.7
  98.2 3.1 %collective-permute-start.6 = (bf16[128,640]{1,0:T(8,128)(2,1)S(1)}, bf16[128,640]{1,0:T(8,128)(2,1)S(1)}, u32[]{:S(2)}, u32[]{:S(2)}) collective-permute-start(bf16[128,640]{1,0:T(8,128)(2,1)S(1)} %bitcast.27), channel_id=1, source_target_pairs={{0,20},{4,0},{16,4},{20,16},{1,21},{5,1},{17,5},{21,17},{2,22},{6,... | collective-permute-start | bytes 491528 | tf_op jit(solution)/shard_map/ppermute | solution.py:52
  101.4 0.0 collective-permute-done.4
  101.4 0.0 collective-permute-start.5
  101.4 2.7 %collective-permute-done.3 = bf16[128,640]{1,0:T(8,128)(2,1)S(1)} collective-permute-done((bf16[128,640]{1,0:T(8,128)(2,1)S(1)}, bf16[128,640]{1,0:T(8,128)(2,1)S(1)}, u32[]{:S(2)}, u32[]{:S(2)}) %collective-permute-start.3) | collective-permute-done | bytes 163872 | tf_op jit(solution)/shard_map/ppermute | solution.py:52
  104.1 0.6 collective-permute-done.2
  104.8 0.0 collective-permute-done.7
  104.8 1.2 collective-permute-done.6
  106.0 2.9 %collective-permute-done.5 = bf16[128,640]{1,0:T(8,128)(2,1)S(1)} collective-permute-done((bf16[128,640]{1,0:T(8,128)(2,1)S(1)}, bf16[128,640]{1,0:T(8,128)(2,1)S(1)}, u32[]{:S(2)}, u32[]{:S(2)}) %collective-permute-start.5) | collective-permute-done | bytes 163872 | tf_op jit(solution)/shard_map/ppermute | solution.py:52
  108.9 0.1 collective-permute-start.8
  109.0 2.7 %collective-permute-start.9 = (bf16[2,128,640]{2,1,0:T(8,128)(2,1)S(1)}, bf16[2,128,640]{2,1,0:T(8,128)(2,1)S(1)}, u32[]{:S(2)}, u32[]{:S(2)}) collective-permute-start(bf16[2,128,640]{2,1,0:T(8,128)(2,1)S(1)} %pad_maximum_fusion.2.refs_1_), channel_id=1, source_target_pairs={{0,20},{4,0},{16,4},{20,16},{1,21},{5,1},{17,5},{21,17},{2,22},{6,... | collective-permute-start | bytes 983048 | tf_op jit(solution)/shard_map/ppermute | solution.py:52
  111.7 0.6 reshape.122.gain_ref
  112.3 0.0 collective-permute-start.13
  112.3 1.5 collective-permute-start.12
  113.8 2.3 %collective-permute-start.17 = (bf16[2,128,640]{2,1,0:T(8,128)(2,1)S(1)}, bf16[2,128,640]{2,1,0:T(8,128)(2,1)S(1)}, u32[]{:S(2)}, u32[]{:S(2)}) collective-permute-start(bf16[2,128,640]{2,1,0:T(8,128)(2,1)S(1)} %pad_maximum_fusion.3.refs_8_), channel_id=1, source_target_pairs={{0,3},{1,0},{2,1},{3,2},{4,7},{5,4},{6,5},{7,6},{8,11},{9,8},{10,9... | collective-permute-start | bytes 983048 | tf_op jit(solution)/shard_map/ppermute | solution.py:52
  116.1 1.8 collective-permute-done.8.refs_2_
  117.9 0.0 collective-permute-start.10
  117.9 0.0 collective-permute-done.9.refs_5_
  117.9 2.7 %collective-permute-start.11 = (bf16[2,128,640]{2,1,0:T(8,128)(2,1)S(1)}, bf16[2,128,640]{2,1,0:T(8,128)(2,1)}, u32[]{:S(2)}, u32[]{:S(2)}) collective-permute-start(bf16[2,128,640]{2,1,0:T(8,128)(2,1)S(1)} %pad_maximum_fusion.4.refs_9_), channel_id=1, source_target_pairs={{0,3},{1,0},{2,1},{3,2},{4,7},{5,4},{6,5},{7,6},{8,11},{9,8},{10,9... | collective-permute-start | bytes 983048 | tf_op jit(solution)/shard_map/ppermute | solution.py:52
  120.6 0.1 select_reduce_fusion
  120.7 4.7 %collective-permute-done.10.refs_10_ = bf16[2,128,640]{2,1,0:T(8,128)(2,1)S(1)} collective-permute-done((bf16[2,128,640]{2,1,0:T(8,128)(2,1)S(1)}, bf16[2,128,640]{2,1,0:T(8,128)(2,1)S(1)}, u32[]{:S(2)}, u32[]{:S(2)}) %collective-permute-start.10) | collective-permute-done | bytes 327712 | tf_op jit(solution)/shard_map/ppermute | solution.py:52
  125.4 2.3 %collective-permute-done.11.refs_13_ = bf16[2,128,640]{2,1,0:T(8,128)(2,1)} collective-permute-done((bf16[2,128,640]{2,1,0:T(8,128)(2,1)S(1)}, bf16[2,128,640]{2,1,0:T(8,128)(2,1)}, u32[]{:S(2)}, u32[]{:S(2)}) %collective-permute-start.11) | collective-permute-done | bytes 327712 | tf_op jit(solution)/shard_map/ppermute | solution.py:52
  127.7 0.0 collective-permute-start.14
  127.7 2.7 %collective-permute-start.15 = (bf16[2,128,640]{2,1,0:T(8,128)(2,1)S(1)}, bf16[2,128,640]{2,1,0:T(8,128)(2,1)}, u32[]{:S(2)}, u32[]{:S(2)}) collective-permute-start(bf16[2,128,640]{2,1,0:T(8,128)(2,1)S(1)} %collective-permute-done.9.refs_5_), channel_id=1, source_target_pairs={{0,20},{4,0},{16,4},{20,16},{1,21},{5,1},{17,5},{21,17},{2,22},{6,... | collective-permute-start | bytes 983048 | tf_op jit(solution)/shard_map/ppermute | solution.py:52
  130.4 0.1 collective-permute-start.18
  130.5 0.0 collective-permute-done.17.refs_12_
  130.5 3.5 %collective-permute-start.19 = (bf16[2,128,640]{2,1,0:T(8,128)(2,1)}, bf16[2,128,640]{2,1,0:T(8,128)(2,1)}, u32[]{:S(2)}, u32[]{:S(2)}) collective-permute-start(bf16[2,128,640]{2,1,0:T(8,128)(2,1)} %collective-permute-done.11.refs_13_), channel_id=1, source_target_pairs={{0,3},{1,0},{2,1},{3,2},{4,7},{5,4},{6,5},{7,6},{8,11},{9,8},{10,9... | collective-permute-start | bytes 983048 | tf_op jit(solution)/shard_map/ppermute | solution.py:52
  134.0 0.7 iota_add_fusion
  134.7 0.9 add.115.src_ref
  135.7 0.1 pad_add_fusion.pos_ref
  135.8 3.6 %copy-done = bf16[16,320,896]{2,1,0:T(8,128)(2,1)S(1)} copy-done((bf16[16,320,896]{2,1,0:T(8,128)(2,1)S(1)}, bf16[16,320,896]{2,1,0:T(8,128)(2,1)}, u32[]{:S(2)}) %copy-start) | copy-done | bytes 9175064
  139.4 3.6 %copy-done.1 = bf16[16,320,896]{2,1,0:T(8,128)(2,1)S(1)} copy-done((bf16[16,320,896]{2,1,0:T(8,128)(2,1)S(1)}, bf16[16,320,896]{2,1,0:T(8,128)(2,1)}, u32[]{:S(2)}) %copy-start.1) | copy-done | bytes 9175064
  143.0 3.0 %assemble_weights.1.w = bf16[2,5120,896]{2,1,0:T(8,128)(2,1)S(1)} custom-call(s32[4]{0:T(128)S(1)} %pad_add_fusion.pos_ref, s32[16]{0:T(128)S(1)} %copy-done.6, bf16[8,2,320,896]{3,2,1,0:T(8,128)(2,1)S(1)} %bitcast.21, bf16[8,2,320,896]{3,2,1,0:T(8,128)(2,1)S(1)} %bitcast.22), custom_call_target="tpu_custom_call" | custom-call | tf_op jit(solution)/shard_map/assemble_weights/pallas_call | solution.py:199
  146.1 16.3 %feed_forward.1 = bf16[512,1152]{1,0:T(8,128)(2,1)S(1)} custom-call(s32[4]{0:T(128)S(1)} %pad_add_fusion.pos_ref, s32[512,1]{1,0:T(8,128)S(1)} %add.115.src_ref, bf16[1,5120]{1,0:T(2,128)(2,1)S(1)} %copy-done.5, bf16[2,5120,896]{2,1,0:T(8,128)(2,1)S(1)} %assemble_weights.1.w, bf16[2,128,640]{2,1,0:T(8,128)(2,1)S(1)} %pad_maximum_fusion.1.refs_0_, ...), custom_call_target="tpu_custom_call" | custom-call | tf_op jit(solution)/shard_map/feed_forward/pallas_call | solution.py:264
  162.4 26.3 %all_to_all.20.refs_0_ = bf16[16,32,1152]{2,1,0:T(8,128)(2,1)S(1)} all-to-all(bf16[16,32,1152]{2,1,0:T(8,128)(2,1)S(1)} %bitcast.23), channel_id=1, replica_groups=mesh['x'=4,'zh'=2,'c'=2,'zl'=2,'y'=4] {'x','zh','c'}, dimensions={0} | all-to-all | bytes 2359296 | tf_op jit(solution)/shard_map/all_to_all | solution.py:357
  188.7 1.5 finish.1
  (33 shorter events, 0.3 us)
Async XLA Ops:
  7.2 128.6 %all-gather.5.cloned.1.call-start = ((), (), s32[]{:S(2)}) async-start(), calls=%async_computation.3 | async-start | bytes 10321920 | tf_op jit(solution)/shard_map/all_gather | solution.py:318
  10.3 20.4 %copy-start.7 = (bf16[2,320,896]{2,1,0:T(8,128)(2,1)}, bf16[2,320,896]{2,1,0:T(8,128)(2,1)S(1)}, u32[]{:S(2)}) copy-start(bf16[2,320,896]{2,1,0:T(8,128)(2,1)S(1)} %get-tuple-element.26) | copy-start | bytes 3440644
  10.3 4.6 %copy-start.10 = (s32[128]{0:T(128)S(1)}, s32[128]{0:T(128)}, u32[]{:S(2)}) copy-start(s32[128]{0:T(128)} %param.14) | copy-start | bytes 1540
  10.3 4.8 %copy-start.2 = (bf16[8,32,1024]{2,1,0:T(8,128)(2,1)S(1)}, bf16[8,32,1024]{2,1,0:T(8,128)(2,1)}, u32[]{:S(2)}) copy-start(bf16[8,32,1024]{2,1,0:T(8,128)(2,1)} %q_ref.1) | copy-start | bytes 1572868
  10.3 4.8 %copy-start.3 = (bf16[256,640]{1,0:T(8,128)(2,1)S(1)}, bf16[256,640]{1,0:T(8,128)(2,1)}, u32[]{:S(2)}) copy-start(bf16[256,640]{1,0:T(8,128)(2,1)} %res_ref.1) | copy-start | bytes 983044
  10.3 4.8 %copy-start.4 = (bf16[8,2,32,128]{3,2,1,0:T(8,128)(2,1)S(1)}, bf16[8,2,32,128]{3,2,1,0:T(8,128)(2,1)}, u32[]{:S(2)}) copy-start(bf16[8,2,32,128]{3,2,1,0:T(8,128)(2,1)} %fresh_ref.1) | copy-start | bytes 393220
  10.4 20.3 %collective-permute-start = (bf16[2,192,896]{2,1,0:T(8,128)(2,1)S(1)}, bf16[2,192,896]{2,1,0:T(8,128)(2,1)S(1)}, u32[]{:S(2)}, u32[]{:S(2)}) collective-permute-start(bf16[2,192,896]{2,1,0:T(8,128)(2,1)S(1)} %slice.34), channel_id=1, source_target_pairs={{0,16},{16,0},{1,17},{17,1},{2,18},{18,2},{3,19},{19,3},{4,20},{20... | collective-permute-start | bytes 2064392 | tf_op jit(solution)/shard_map/ppermute | solution.py:52
  30.7 0.8 copy-start.8
  31.5 37.4 %all-to-all-start = ((bf16[8,256,640]{2,1,0:T(8,128)(2,1)}), bf16[8,256,640]{2,1,0:T(8,128)(2,1)S(1)}, u32[]{:S(2)}, u32[]{:S(2)}) async-start(bf16[8,256,640]{2,1,0:T(8,128)(2,1)} %attend_project.1), calls=%async_computation | async-start | bytes 5242880 | tf_op jit(solution)/shard_map/all_to_all | solution.py:337
  36.2 99.6 %all-gather.7.cloned.1.call-start = ((), (), s32[]{:S(2)}) async-start(), calls=%async_computation.4 | async-start | bytes 10321920 | tf_op jit(solution)/shard_map/all_gather | solution.py:342
  37.3 39.4 %collective-permute-start.1 = (bf16[2,128,896]{2,1,0:T(8,128)(2,1)S(1)}, bf16[2,128,896]{2,1,0:T(8,128)(2,1)}, u32[]{:S(2)}, u32[]{:S(2)}) collective-permute-start(bf16[2,128,896]{2,1,0:T(8,128)(2,1)S(1)} %slice.35), channel_id=1, source_target_pairs={{0,16},{16,0},{1,17},{17,1},{2,18},{18,2},{3,19},{19,3},{4,20},{20... | collective-permute-start | bytes 1376264 | tf_op jit(solution)/shard_map/ppermute | solution.py:52
  79.1 32.6 %copy-start.9 = (bf16[5120]{0:T(1024)(128)(2,1)S(1)}, bf16[5120]{0:T(1024)(128)(2,1)}, u32[]{:S(2)}) copy-start(bf16[5120]{0:T(1024)(128)(2,1)} %param.17) | copy-start | bytes 30724
  79.1 41.5 %copy-start.11 = (s32[128]{0:T(128)S(1)}, s32[128]{0:T(128)}, u32[]{:S(2)}) copy-start(s32[128]{0:T(128)} %param.15) | copy-start | bytes 1540
  79.1 56.7 %copy-start.6 = (s32[16]{0:T(128)S(1)}, s32[16]{0:T(128)}, u32[]{:S(2)}) copy-start(s32[16]{0:T(128)} %block_ref.1) | copy-start | bytes 196
  93.9 7.5 %collective-permute-start.4 = (bf16[128,640]{1,0:T(8,128)(2,1)S(1)}, bf16[128,640]{1,0:T(8,128)(2,1)S(1)}, u32[]{:S(2)}, u32[]{:S(2)}) collective-permute-start(bf16[128,640]{1,0:T(8,128)(2,1)S(1)} %bitcast.30), channel_id=1, source_target_pairs={{0,2},{1,3},{2,0},{3,1},{4,6},{5,7},{6,4},{7,5},{8,10},{9,11},{10,... | collective-permute-start | bytes 491528 | tf_op jit(solution)/shard_map/ppermute | solution.py:52
  96.7 7.4 %collective-permute-start.3 = (bf16[128,640]{1,0:T(8,128)(2,1)S(1)}, bf16[128,640]{1,0:T(8,128)(2,1)S(1)}, u32[]{:S(2)}, u32[]{:S(2)}) collective-permute-start(bf16[128,640]{1,0:T(8,128)(2,1)S(1)} %bitcast.31), channel_id=1, source_target_pairs={{0,3},{1,0},{2,1},{3,2},{4,7},{5,4},{6,5},{7,6},{8,11},{9,8},{10,9... | collective-permute-start | bytes 491528 | tf_op jit(solution)/shard_map/ppermute | solution.py:52
  97.8 6.9 %collective-permute-start.2 = (bf16[128,640]{1,0:T(8,128)(2,1)S(1)}, bf16[128,640]{1,0:T(8,128)(2,1)S(1)}, u32[]{:S(2)}, u32[]{:S(2)}) collective-permute-start(bf16[128,640]{1,0:T(8,128)(2,1)S(1)} %bitcast.32), channel_id=1, source_target_pairs={{0,1},{1,2},{2,3},{3,0},{4,5},{5,6},{6,7},{7,4},{8,9},{9,10},{10,1... | collective-permute-start | bytes 491528 | tf_op jit(solution)/shard_map/ppermute | solution.py:52
  98.1 6.6 %collective-permute-start.7 = (bf16[128,640]{1,0:T(8,128)(2,1)S(1)}, bf16[128,640]{1,0:T(8,128)(2,1)S(1)}, u32[]{:S(2)}, u32[]{:S(2)}) collective-permute-start(bf16[128,640]{1,0:T(8,128)(2,1)S(1)} %bitcast.26), channel_id=1, source_target_pairs={{0,16},{4,20},{16,0},{20,4},{1,17},{5,21},{17,1},{21,5},{2,18},{6,... | collective-permute-start | bytes 491528 | tf_op jit(solution)/shard_map/ppermute | solution.py:52
  98.2 7.7 %collective-permute-start.6 = (bf16[128,640]{1,0:T(8,128)(2,1)S(1)}, bf16[128,640]{1,0:T(8,128)(2,1)S(1)}, u32[]{:S(2)}, u32[]{:S(2)}) collective-permute-start(bf16[128,640]{1,0:T(8,128)(2,1)S(1)} %bitcast.27), channel_id=1, source_target_pairs={{0,20},{4,0},{16,4},{20,16},{1,21},{5,1},{17,5},{21,17},{2,22},{6,... | collective-permute-start | bytes 491528 | tf_op jit(solution)/shard_map/ppermute | solution.py:52
  101.4 7.5 %collective-permute-start.5 = (bf16[128,640]{1,0:T(8,128)(2,1)S(1)}, bf16[128,640]{1,0:T(8,128)(2,1)S(1)}, u32[]{:S(2)}, u32[]{:S(2)}) collective-permute-start(bf16[128,640]{1,0:T(8,128)(2,1)S(1)} %bitcast.28), channel_id=1, source_target_pairs={{0,4},{4,16},{16,20},{20,0},{1,5},{5,17},{17,21},{21,1},{2,6},{6,1... | collective-permute-start | bytes 491528 | tf_op jit(solution)/shard_map/ppermute | solution.py:52
  108.9 9.0 %collective-permute-start.8 = (bf16[2,128,640]{2,1,0:T(8,128)(2,1)S(1)}, bf16[2,128,640]{2,1,0:T(8,128)(2,1)S(1)}, u32[]{:S(2)}, u32[]{:S(2)}) collective-permute-start(bf16[2,128,640]{2,1,0:T(8,128)(2,1)S(1)} %pad_maximum_fusion.1.refs_0_), channel_id=1, source_target_pairs={{0,4},{4,16},{16,20},{20,0},{1,5},{5,17},{17,21},{21,1},{2,6},{6,1... | collective-permute-start | bytes 983048 | tf_op jit(solution)/shard_map/ppermute | solution.py:52
  109.0 8.9 %collective-permute-start.9 = (bf16[2,128,640]{2,1,0:T(8,128)(2,1)S(1)}, bf16[2,128,640]{2,1,0:T(8,128)(2,1)S(1)}, u32[]{:S(2)}, u32[]{:S(2)}) collective-permute-start(bf16[2,128,640]{2,1,0:T(8,128)(2,1)S(1)} %pad_maximum_fusion.2.refs_1_), channel_id=1, source_target_pairs={{0,20},{4,0},{16,4},{20,16},{1,21},{5,1},{17,5},{21,17},{2,22},{6,... | collective-permute-start | bytes 983048 | tf_op jit(solution)/shard_map/ppermute | solution.py:52
  112.3 15.4 %collective-permute-start.13 = (bf16[2,128,640]{2,1,0:T(8,128)(2,1)S(1)}, bf16[2,128,640]{2,1,0:T(8,128)(2,1)S(1)}, u32[]{:S(2)}, u32[]{:S(2)}) collective-permute-start(bf16[2,128,640]{2,1,0:T(8,128)(2,1)S(1)} %pad_maximum_fusion.1.refs_0_), channel_id=1, source_target_pairs={{0,20},{4,0},{16,4},{20,16},{1,21},{5,1},{17,5},{21,17},{2,22},{6,... | collective-permute-start | bytes 983048 | tf_op jit(solution)/shard_map/ppermute | solution.py:52
  112.3 18.1 %collective-permute-start.12 = (bf16[2,128,640]{2,1,0:T(8,128)(2,1)S(1)}, bf16[2,128,640]{2,1,0:T(8,128)(2,1)S(1)}, u32[]{:S(2)}, u32[]{:S(2)}) collective-permute-start(bf16[2,128,640]{2,1,0:T(8,128)(2,1)S(1)} %pad_maximum_fusion.2.refs_1_), channel_id=1, source_target_pairs={{0,4},{4,16},{16,20},{20,0},{1,5},{5,17},{17,21},{21,1},{2,6},{6,1... | collective-permute-start | bytes 983048 | tf_op jit(solution)/shard_map/ppermute | solution.py:52
  113.8 16.7 %collective-permute-start.17 = (bf16[2,128,640]{2,1,0:T(8,128)(2,1)S(1)}, bf16[2,128,640]{2,1,0:T(8,128)(2,1)S(1)}, u32[]{:S(2)}, u32[]{:S(2)}) collective-permute-start(bf16[2,128,640]{2,1,0:T(8,128)(2,1)S(1)} %pad_maximum_fusion.3.refs_8_), channel_id=1, source_target_pairs={{0,3},{1,0},{2,1},{3,2},{4,7},{5,4},{6,5},{7,6},{8,11},{9,8},{10,9... | collective-permute-start | bytes 983048 | tf_op jit(solution)/shard_map/ppermute | solution.py:52
  117.9 7.5 %collective-permute-start.10 = (bf16[2,128,640]{2,1,0:T(8,128)(2,1)S(1)}, bf16[2,128,640]{2,1,0:T(8,128)(2,1)S(1)}, u32[]{:S(2)}, u32[]{:S(2)}) collective-permute-start(bf16[2,128,640]{2,1,0:T(8,128)(2,1)S(1)} %pad_maximum_fusion.3.refs_8_), channel_id=1, source_target_pairs={{0,1},{1,2},{2,3},{3,0},{4,5},{5,6},{6,7},{7,4},{8,9},{9,10},{10,1... | collective-permute-start | bytes 983048 | tf_op jit(solution)/shard_map/ppermute | solution.py:52
  117.9 9.8 %collective-permute-start.11 = (bf16[2,128,640]{2,1,0:T(8,128)(2,1)S(1)}, bf16[2,128,640]{2,1,0:T(8,128)(2,1)}, u32[]{:S(2)}, u32[]{:S(2)}) collective-permute-start(bf16[2,128,640]{2,1,0:T(8,128)(2,1)S(1)} %pad_maximum_fusion.4.refs_9_), channel_id=1, source_target_pairs={{0,3},{1,0},{2,1},{3,2},{4,7},{5,4},{6,5},{7,6},{8,11},{9,8},{10,9... | collective-permute-start | bytes 983048 | tf_op jit(solution)/shard_map/ppermute | solution.py:52
  125.4 20.6 %collective-permute-start.16 = (bf16[2,128,640]{2,1,0:T(8,128)(2,1)S(1)}, bf16[2,128,640]{2,1,0:T(8,128)(2,1)}, u32[]{:S(2)}, u32[]{:S(2)}) collective-permute-start(bf16[2,128,640]{2,1,0:T(8,128)(2,1)S(1)} %pad_maximum_fusion.4.refs_9_), channel_id=1, source_target_pairs={{0,1},{1,2},{2,3},{3,0},{4,5},{5,6},{6,7},{7,4},{8,9},{9,10},{10,1... | collective-permute-start | bytes 983048 | tf_op jit(solution)/shard_map/ppermute | solution.py:52
  127.7 18.3 %collective-permute-start.14 = (bf16[2,128,640]{2,1,0:T(8,128)(2,1)S(1)}, bf16[2,128,640]{2,1,0:T(8,128)(2,1)}, u32[]{:S(2)}, u32[]{:S(2)}) collective-permute-start(bf16[2,128,640]{2,1,0:T(8,128)(2,1)S(1)} %collective-permute-done.8.refs_2_), channel_id=1, source_target_pairs={{0,4},{4,16},{16,20},{20,0},{1,5},{5,17},{17,21},{21,1},{2,6},{6,1... | collective-permute-start | bytes 983048 | tf_op jit(solution)/shard_map/ppermute | solution.py:52
  127.7 18.3 %collective-permute-start.15 = (bf16[2,128,640]{2,1,0:T(8,128)(2,1)S(1)}, bf16[2,128,640]{2,1,0:T(8,128)(2,1)}, u32[]{:S(2)}, u32[]{:S(2)}) collective-permute-start(bf16[2,128,640]{2,1,0:T(8,128)(2,1)S(1)} %collective-permute-done.9.refs_5_), channel_id=1, source_target_pairs={{0,20},{4,0},{16,4},{20,16},{1,21},{5,1},{17,5},{21,17},{2,22},{6,... | collective-permute-start | bytes 983048 | tf_op jit(solution)/shard_map/ppermute | solution.py:52
  130.4 15.6 %collective-permute-start.18 = (bf16[2,128,640]{2,1,0:T(8,128)(2,1)S(1)}, bf16[2,128,640]{2,1,0:T(8,128)(2,1)}, u32[]{:S(2)}, u32[]{:S(2)}) collective-permute-start(bf16[2,128,640]{2,1,0:T(8,128)(2,1)S(1)} %collective-permute-done.10.refs_10_), channel_id=1, source_target_pairs={{0,1},{1,2},{2,3},{3,0},{4,5},{5,6},{6,7},{7,4},{8,9},{9,10},{10,1... | collective-permute-start | bytes 983048 | tf_op jit(solution)/shard_map/ppermute | solution.py:52
  130.5 15.6 %collective-permute-start.19 = (bf16[2,128,640]{2,1,0:T(8,128)(2,1)}, bf16[2,128,640]{2,1,0:T(8,128)(2,1)}, u32[]{:S(2)}, u32[]{:S(2)}) collective-permute-start(bf16[2,128,640]{2,1,0:T(8,128)(2,1)} %collective-permute-done.11.refs_13_), channel_id=1, source_target_pairs={{0,3},{1,0},{2,1},{3,2},{4,7},{5,4},{6,5},{7,6},{8,11},{9,8},{10,9... | collective-permute-start | bytes 983048 | tf_op jit(solution)/shard_map/ppermute | solution.py:52
  135.8 3.6 %copy-start = (bf16[16,320,896]{2,1,0:T(8,128)(2,1)S(1)}, bf16[16,320,896]{2,1,0:T(8,128)(2,1)}, u32[]{:S(2)}) copy-start(bf16[16,320,896]{2,1,0:T(8,128)(2,1)} %all-gather.5.cloned.1.call-done) | copy-start | bytes 27525124
  139.4 3.6 %copy-start.1 = (bf16[16,320,896]{2,1,0:T(8,128)(2,1)S(1)}, bf16[16,320,896]{2,1,0:T(8,128)(2,1)}, u32[]{:S(2)}) copy-start(bf16[16,320,896]{2,1,0:T(8,128)(2,1)} %all-gather.7.cloned.1.call-done) | copy-start | bytes 27525124
  143.0 3.1 %copy-start.5 = (bf16[1,5120]{1,0:T(2,128)(2,1)S(1)}, bf16[1,5120]{1,0:T(2,128)(2,1)}, u32[]{:S(2)}) copy-start(bf16[1,5120]{1,0:T(2,128)(2,1)} %reshape.122.gain_ref) | copy-start | bytes 30724
Sparse Core Ops, SparseCore 0:
  10.5 56.6 all-gather.4
  79.2 55.1 all-gather.6
